TPU v7x, 32 devices: a whole 2x2x4 slice. The times are simulated.
32 devices in a mesh: tile: 8 (over z, core), chan: 4 (over y, x).
Axes of the slice: x: 2, y: 2, z: 4, core: 2. Of those that a mesh axis runs over, the one named last changes fastest.
Arguments:
- voltages: int32 [512, 131072], P('tile', 'chan'), may hold values from -128 to 127
- history: int32 [512, 30720], P('tile'), may hold values from -128 to 127
- filter_taps: int32 [16, 2048], replicated, may hold values from -64 to 64
Outputs:
- visibilities: float32 [2, 1024, 512, 512], P(None, 'chan', 'tile')
Inputs may be any that keep to these rules, and one draw needn't show every extreme that they name: `voltages`: 8-bit signed samples. `history`: 8-bit signed samples.
All inputs are finite; a program needn't handle non-finite values.
Results may differ from a plain program's by a relative error of at most 0.006.
Values may be sent and summed in bfloat16 or wider, within the bound.
No kernel may reach another device: no remote copies, remote signals or barrier semaphores. Data moves between devices by JAX's collectives and lax.ppermute only.
A program may use at most 320 MiB of HBM per device.

v0:
```python
import math

import jax
import jax.numpy as jnp
from jax import lax
from jax.sharding import PartitionSpec as P

CH = 1024
TAPS = 16
FFT = 2048


filter_norm = 1.0 / 16384.0


def from_behind(value, axis, steps):
    count = lax.axis_size(axis)
    leading, last = (max(0, -steps), min(count, count - steps))
    return lax.ppermute(value, axis, [(source, source + steps) for source in range(leading, last)])


def dft_table(samples, channels):
    rows_index = jnp.arange(samples, dtype=jnp.int32)[:, None]
    cols_index = jnp.arange(channels, dtype=jnp.int32)[None, :]
    angles = (rows_index * cols_index % samples).astype(jnp.float32) * (2.0 * math.pi / samples)
    factor = 1.0 / math.sqrt(channels)
    return jnp.concatenate([jnp.cos(angles) * factor, -jnp.sin(angles) * factor], axis=1).astype(
        jnp.bfloat16
    )


def polyphase(extended, weights, spectra_count):
    summed = jnp.zeros((extended.shape[0], spectra_count, extended.shape[2]), jnp.float32)
    for tap_index in range(weights.shape[0]):
        summed = (
            summed
            + weights[tap_index][None, None, :]
            * extended[:, tap_index : tap_index + spectra_count, :]
        )
    return summed


def counter_rows(spectra):
    real_part = spectra[:, :, 0]
    imag_part = spectra[:, :, 1]
    rotated = jnp.stack([imag_part, -real_part], axis=2)
    return jnp.stack([spectra, rotated], axis=0)


def body(voltages, history, filter_taps):
    local_inputs = voltages.shape[0]
    spectra_count = voltages.shape[1] // FFT
    tail_blocks = voltages[:, (spectra_count - TAPS + 1) * FFT :].astype(jnp.bfloat16)
    carried = from_behind(tail_blocks, "chan", 1)
    is_first = lax.axis_index("chan") == 0
    earlier = jnp.where(is_first, history.astype(jnp.float32), carried.astype(jnp.float32))
    extended = jnp.concatenate([earlier, voltages.astype(jnp.float32)], axis=1)
    extended = extended.reshape(local_inputs, spectra_count + TAPS - 1, FFT)
    filtered = (
        polyphase(extended, filter_taps.astype(jnp.float32), spectra_count) * filter_norm
    ).astype(jnp.bfloat16)
    spectra = jnp.dot(
        filtered.reshape(-1, FFT), dft_table(FFT, CH), preferred_element_type=jnp.float32
    )
    spectra = spectra.reshape(local_inputs, spectra_count, 2, CH).astype(jnp.bfloat16)
    turned = lax.all_to_all(spectra, "chan", split_axis=3, concat_axis=1, tiled=True)
    total_spectra = turned.shape[1]
    average = 1.0 / total_spectra
    row_sets = counter_rows(turned)
    return (
        jnp.einsum(
            "qaspc,bspc->qcab",
            row_sets,
            lax.all_gather(turned, "tile", axis=0, tiled=True),
            preferred_element_type=jnp.float32,
        )
        * average
    )


def solution(mesh):
    in_specs = (P("tile", "chan"), P("tile", None), P())
    out_specs = P(None, "chan", "tile", None)
    return jax.shard_map(body, mesh=mesh, in_specs=in_specs, out_specs=out_specs, check_vma=False)
```

profile of v0, /device:TPU:0, one launch (start us, length us, event | category | flops | bytes accessed | tf_op | source)
XLA Modules:
  0.0 998.3 jit_solution(9194824762870197267)
XLA Ops:
  6.5 0.0 all-gather.2.cloned.1.call-start
  6.5 0.0 copy-start
  6.5 5.8 slice_convert_fusion
  12.3 6.8 collective-permute-start
  19.2 0.0 copy-done
  19.2 0.0 copy-start.1
  19.2 4.1 convert_element_type.28
  23.2 0.0 copy-done.1
  23.3 0.1 fusion.40
  23.4 35.0 %multiply_convert_fusion = (bf16[2048,1024]{0,1:T(8,128)(2,1)}, bf16[2048,1024]{0,1:T(8,128)(2,1)}) fusion(), kind=kLoop, calls=%fused_computation.49 | loop fusion | flops 39845888 | bytes 8388608 | tf_op jit(solution)/shard_map/convert.1
  58.3 8.3 pad_maximum_fusion.1
  66.6 35.1 %collective-permute-done = bf16[64,30720]{1,0:T(8,128)(2,1)} collective-permute-done((bf16[64,30720]{1,0:T(8,128)(2,1)}, bf16[64,30720]{1,0:T(8,128)(2,1)}, u32[]{:S(2)}, u32[]{:S(2)}) %collective-permute-start) | collective-permute-done | bytes 3932192 | tf_op jit(solution)/shard_map/ppermute | solution.py:19
  101.8 5.2 convert_select_fusion
  107.0 9.5 pad_maximum_fusion
  116.5 14.9 %reshape.25 = f32[64,31,2048]{2,1,0:T(8,128)} reshape(f32[64,63488]{1,0:T(8,128)} %pad_maximum_fusion) | data formatting | bytes 32505856 | tf_op jit(solution)/shard_map/reshape | solution.py:58
  131.4 69.0 %fusion.48 = bf16[64,16,2048,1]{2,1,3,0:T(8,128)(2,1)S(1)} fusion(f32[64,31,2048]{2,1,0:T(8,128)} %reshape.25, f32[2048]{0:T(1024)S(1)} %bitcast.66, f32[2048]{0:T(1024)S(1)} %bitcast.67, f32[2048]{0:T(1024)S(1)} %bitcast.68, f32[2048]{0:T(1024)S(1)} %bitcast.69, f32[2048]{0:T(1024)S(1)} %bitcast.70, f32[2048]{0:T(1024)S(1)} %bitcast.71, ...), kind=kLoop, calls=%fused_computation.58.clone.clone.clone.1 | loop fusion | flops 69206016 | bytes 138543104 | tf_op jit(solution)/shard_map/dot_general | solution.py:62
  200.4 12.7 %fusion.34 = bf16[64,16,2,1024]{3,1,2,0:T(8,128)(2,1)} fusion(bf16[2,1024,2048,1]{2,1,0,3:T(8,128)(2,1)} %bitcast.64, bf16[64,16,2048,1]{2,1,3,0:T(8,128)(2,1)S(1)} %fusion.48), kind=kOutput, calls=%fused_computation.59 | convolution fusion | flops 8592031744 | bytes 16777216 | tf_op jit(solution)/shard_map/dot_general | solution.py:62
  213.1 15.5 %copy.28 = bf16[64,16,2,1024]{0,1,2,3:T(8,128)(2,1)} copy(bf16[64,16,2,1024]{3,1,2,0:T(8,128)(2,1)} %fusion.34) | data formatting | bytes 8388608 | tf_op jit(solution)/shard_map/convert_element_type | solution.py:65
  228.6 9.5 reshape.30
  238.1 54.1 %all_to_all.18 = bf16[4,2,262144]{2,1,0:T(2,128)(2,1)} all-to-all(bf16[4,2,262144]{2,1,0:T(2,128)(2,1)} %reshape.30), channel_id=1, replica_groups=mesh['tile'=8,'chan'=4] {'chan'}, dimensions={0} | all-to-all | bytes 8388608 | tf_op jit(solution)/shard_map/all_to_all | solution.py:66
  292.2 9.3 reshape.31
  301.5 12.2 %copy.40 = bf16[64,16,2,4,256]{4,3,1,2,0:T(4,128)(2,1)} copy(bf16[64,16,2,4,256]{0,1,2,4,3:T(8,128)(2,1)} %bitcast.62) | data formatting | bytes 8388608 | tf_op jit(solution)/shard_map/all_to_all | solution.py:66
  313.7 5.2 copy.30
  319.0 13.0 %copy.31 = bf16[64,64,2,256]{1,0,2,3:T(8,128)(2,1)} copy(bf16[64,64,2,256]{3,1,2,0:T(8,128)(2,1)} %bitcast.59) | data formatting | bytes 8388608 | tf_op jit(solution)/shard_map/all_to_all | solution.py:66
  331.9 0.0 all-gather.2.cloned.1.call-update
  331.9 13.2 %copy.35 = bf16[1,64,64,2,256]{2,1,3,0,4:T(8,128)(2,1)} copy(bf16[1,64,64,2,256]{4,2,3,1,0:T(8,128)(2,1)} %bitcast.60) | data formatting | bytes 8388608 | tf_op jit(solution)/shard_map/stack | solution.py:47
  345.2 7.7 fusion.39
  352.9 8.7 maximum_bitcast_fusion
  361.6 534.7 %all-gather.2.cloned.1.call-done = bf16[512,64,2,256]{1,0,2,3:T(8,128)(2,1)} async-done(((bf16[64,64,2,256]{1,0,2,3:T(8,128)(2,1)}), bf16[512,64,2,256]{1,0,2,3:T(8,128)(2,1)}) %all-gather.2.cloned.1.call-update) | async-done | bytes 33554448 | tf_op jit(solution)/shard_map/all_gather | solution.py:74
  896.3 50.7 %fusion.2 = f32[2,256,64,512]{3,2,0,1:T(8,128)} fusion(bf16[512,64,2,256]{1,0,2,3:T(8,128)(2,1)} %all-gather.2.cloned.1.call-done, bf16[1,64,64,2,256]{2,1,3,0,4:T(8,128)(2,1)} %maximum_bitcast_fusion, bf16[1,64,64,2,256]{2,1,3,0,4:T(8,128)(2,1)} %copy.35), kind=kOutput, calls=%fused_computation.3 | convolution fusion | flops 4328521728 | bytes 109051904 | tf_op jit(solution)/shard_map/qaspc,bspc->qcab/dot_general | solution.py:71
  947.0 44.5 %copy.36 = f32[2,256,64,512]{3,2,1,0:T(8,128)} copy(f32[2,256,64,512]{3,2,0,1:T(8,128)} %fusion.2) | data formatting | bytes 134217728 | tf_op jit(solution)/shard_map/mul | solution.py:71
  (1 shorter events, 0.0 us)
Async XLA Ops:
  6.5 889.8 %all-gather.2.cloned.1.call-start = ((), (), s32[]{:S(2)}) async-start(), calls=%async_computation.1 | async-start | bytes 75497472 | tf_op jit(solution)/shard_map/all_gather | solution.py:74
  6.5 12.6 %copy-start = (s32[64,32768]{1,0:T(8,128)S(1)}, s32[64,32768]{1,0:T(8,128)}, u32[]{:S(2)}) copy-start(s32[64,32768]{1,0:T(8,128)} %param.3) | copy-start | bytes 25165828
  12.3 89.5 %collective-permute-start = (bf16[64,30720]{1,0:T(8,128)(2,1)}, bf16[64,30720]{1,0:T(8,128)(2,1)}, u32[]{:S(2)}, u32[]{:S(2)}) collective-permute-start(bf16[64,30720]{1,0:T(8,128)(2,1)} %slice_convert_fusion), channel_id=1, source_target_pairs={{0,1},{1,2},{2,3},{4,5},{5,6},{6,7},{8,9},{9,10},{10,11},{12,13},{... | collective-permute-start | bytes 11796488 | tf_op jit(solution)/shard_map/ppermute | solution.py:19
  19.2 4.1 copy-start.1
Sparse Core Ops, SparseCore 0:
  332.1 564.2 all-gather.1
where the time goes:
time: 1000 us; the launch traced here: 998 us
  waiting for transfers between devices  570 us (57%)
  other arithmetic  153 us (15%)
  local copies, waits for them, and re-layouts  137 us (14%)
  matrix products  63.4 us (6%)
  blocking collectives  54.1 us (5%)
  between operations  13.4 us (1%)
    all_gather x1, waiting for transfers between devices, body(): lax.all_gather(turned, 'tile', axis=0, tiled=True)  535 us
    dot_general x1, other arithmetic, body(): jnp.dot(filtered.reshape(-1, FFT), dft_table(FFT, CH), preferred_element_...  69 us
    all_to_all x1, blocking collectives, body(): lax.all_to_all(spectra, 'chan', split_axis=3, concat_axis=1, tiled=True)  54.1 us
    dot_general x1, matrix products, body(): jnp.einsum('qaspc,bspc->qcab', row_sets, lax.all_gather(turned, 'tile', a...  50.7 us
    mul x1, local copies, waits for them, and re-layouts, body(): jnp.einsum('qaspc,bspc->qcab', row_sets, lax.all_gather(turned, 'tile', a...  44.5 us
    another operation x2, other arithmetic  40.7 us
    ppermute x1, waiting for transfers between devices, from_behind(): lax.ppermute(value, axis, [(source, source + steps) for source in range(l...  35.1 us
    all_to_all x3, local copies, waits for them, and re-layouts, body(): lax.all_to_all(spectra, 'chan', split_axis=3, concat_axis=1, tiled=True)  30.4 us
  transfers between devices with their start and end apart: 2, of which 2 were waited for; matrix products, arithmetic and copies ran while one was open for 8% of the time, Pallas kernels for 0%

commit v1 on v0

v1 whole, which is shorter than its diff:
```python
import functools
import math

import jax
import jax.numpy as jnp
import ml_dtypes
import numpy as np
from jax import lax
from jax.experimental import pallas as pl
from jax.experimental.pallas import tpu as pltpu
from jax.sharding import PartitionSpec as P

LANES = 128
ROWS = 16
VMEM = 48 * 1024 * 1024
FLOPS_A_MICROSECOND = 1.15e9
filter_norm = 1.0 / 16384.0


def dft_rows(samples):
    channels = samples // 2
    index = np.arange(channels, dtype=np.int64)[:, None] * np.arange(samples, dtype=np.int64)[None, :]
    angles = (index % samples).astype(np.float32) * np.float32(2.0 * math.pi / samples)
    factor = np.float32(1.0 / math.sqrt(channels))
    rows = np.concatenate([np.cos(angles) * factor, -np.sin(angles) * factor], axis=0)
    return rows.astype(ml_dtypes.bfloat16)


def params():
    return pltpu.CompilerParams(vmem_limit_bytes=VMEM)


class Order:
    def __init__(self):
        self.token = None

    def call(self, kernel, name, place, operands, in_specs, out_shape, out_specs, grid, scratch=(), after=(), aliased=(), micros=1.0):
        later = list(after) + ([] if self.token is None else [self.token])
        extra = [*aliased, *later]
        inputs, outputs = len(operands), len(out_shape)

        def wrapped(place_ref, *refs):
            outs = refs[inputs + len(extra) :]
            outs[outputs][...] = jnp.zeros_like(outs[outputs])
            kernel(place_ref, refs[:inputs], outs[:outputs], outs[outputs + 1 :])

        results = pl.pallas_call(
            wrapped,
            out_shape=[*out_shape, jax.ShapeDtypeStruct((8, LANES), jnp.float32)],
            grid_spec=pltpu.PrefetchScalarGridSpec(
                num_scalar_prefetch=1,
                grid=grid,
                in_specs=[*in_specs, *[pl.BlockSpec(memory_space=pl.ANY)] * len(extra)],
                out_specs=[*out_specs, pl.BlockSpec((8, LANES), lambda g, place: (0, 0))],
                scratch_shapes=list(scratch),
            ),
            input_output_aliases={1 + inputs + i: i for i in range(len(aliased))},
            compiler_params=params(),
            cost_estimate=pl.CostEstimate(
                flops=int(micros * FLOPS_A_MICROSECOND), bytes_accessed=0, transcendentals=0
            ),
            name=name,
        )(place, *operands, *extra)
        self.token = results[-1]
        return results[:-1]


def convert(order, place, voltages, chunk, count, parts, spectra, fft):
    each = ROWS // parts

    def kernel(place, ins, outs, scratch):
        (v_ref,), (work,), me = ins, scratch, place[0]

        def block(nb, carry):
            lane = pl.multiple_of(nb * LANES, LANES)
            for s in range(spectra):
                for top in range(0, ROWS, 8):
                    x = v_ref[top : top + 8, pl.ds(pl.multiple_of(s * fft + lane, LANES), LANES)]
                    work[pl.ds(top * spectra + s, 8, stride=spectra), :] = x.astype(jnp.float32)
            for slot in range(parts):
                for i in range(each):
                    row = pl.multiple_of(((me ^ slot) * each + i) * spectra, spectra)
                    outs[slot][0, i, :, pl.ds(lane, LANES)] = work[pl.ds(row, spectra), :].astype(jnp.bfloat16)
            return carry

        lax.fori_loop(0, fft // LANES, block, 0)

    return order.call(
        kernel,
        "convert",
        place,
        [voltages],
        [pl.BlockSpec((ROWS, spectra * fft), lambda g, place: (chunk + g, 0))],
        [jax.ShapeDtypeStruct((count, each, spectra, fft), jnp.bfloat16)] * parts,
        [pl.BlockSpec((1, each, spectra, fft), lambda g, place: (g, 0, 0, 0))] * parts,
        (count,),
        [pltpu.VMEM((ROWS * spectra, LANES), jnp.float32)],
        micros=2.5 * count,
    )


def own_history(order, place, history, parts, taps, fft):
    each = ROWS // parts
    chunks = history.shape[0] // ROWS

    def kernel(place, ins, outs, scratch):
        (h_ref,), (out,), (work,), me = ins, outs, scratch, place[0]
        work[...] = jnp.zeros_like(work)

        def block(nb, carry):
            lane = pl.multiple_of(nb * LANES, LANES)
            for s in range(taps - 1):
                x = h_ref[:, pl.ds(pl.multiple_of(s * fft + lane, LANES), LANES)]
                work[pl.ds(s + 1, 8, stride=taps), :] = x.astype(jnp.float32)
            for i in range(each):
                row = pl.multiple_of((lax.rem(me * each, 8) + i) * taps, taps)
                out[0, i, :, pl.ds(lane, LANES)] = work[pl.ds(row, taps), :].astype(jnp.bfloat16)
            return carry

        lax.fori_loop(0, fft // LANES, block, 0)

    return order.call(
        kernel,
        "history",
        place,
        [history],
        [pl.BlockSpec((8, history.shape[1]), lambda g, place: (g * (ROWS // 8) + place[0] * each // 8, 0))],
        [jax.ShapeDtypeStruct((chunks, each, taps, fft), jnp.bfloat16)],
        [pl.BlockSpec((1, each, taps, fft), lambda g, place: (g, 0, 0, 0))],
        (chunks,),
        [pltpu.VMEM((8 * taps, LANES), jnp.float32)],
        micros=4.5,
    )[0]


def channelize(order, place, filter_taps, hist, pieces, inner, table, chunk, split, after=()):
    parts = len(pieces)
    _, each, spectra, fft = pieces[0].shape
    taps = filter_taps.shape[0]
    total = parts * spectra
    channels = fft // 2 // parts

    def kernel(place, ins, outs, scratch):
        taps_ref, hist_ref, *refs = ins
        blocks, (cos_ref, sin_ref) = refs[:parts], refs[parts:]
        extended, filtered = scratch
        me, step = place[0], pl.program_id(0)

        @pl.when(step == 0)
        def _():
            def block(nb, carry):
                lane = pl.multiple_of(nb * LANES, LANES)
                columns = pl.ds(lane, LANES)
                weights = taps_ref[:, columns].astype(jnp.float32)
                for i in range(each):
                    extended[i, 0:taps, :] = hist_ref[0, i, :, columns].astype(jnp.float32)
                    for slot in range(parts):
                        row = pl.multiple_of(taps + (me ^ slot) * spectra, ROWS)
                        extended[i, pl.ds(row, spectra), :] = blocks[slot][0, i, :, columns].astype(jnp.float32)
                for i in range(each):
                    summed = weights[0:1, :] * extended[i, 1 : 1 + total, :]
                    for t in range(1, taps):
                        summed = summed + weights[t : t + 1, :] * extended[i, t + 1 : t + 1 + total, :]
                    filtered[i * total : (i + 1) * total, columns] = (summed * filter_norm).astype(jnp.bfloat16)
                return carry

            lax.fori_loop(0, fft // LANES, block, 0)

        dims = (((1,), (1,)), ((), ()))
        block = filtered[...]
        real = lax.dot_general(cos_ref[...], block, dims, preferred_element_type=jnp.float32)
        imag = lax.dot_general(sin_ref[...], block, dims, preferred_element_type=jnp.float32)
        results = []
        if 2 * total == LANES and each % 2 == 0:
            low = lax.broadcasted_iota(jnp.int32, (real.shape[0], LANES), 1) < total
            for pair in range(each // 2):
                r = real[:, pair * LANES : (pair + 1) * LANES]
                m = imag[:, pair * LANES : (pair + 1) * LANES]
                results.append(jnp.where(low, r, pltpu.roll(m, total, 1)))
                results.append(jnp.where(low, pltpu.roll(r, total, 1), m))
        else:
            for i in range(each):
                cut = slice(i * total, (i + 1) * total)
                results.append(jnp.concatenate([real[:, cut], imag[:, cut]], axis=1))
        results = [value.astype(jnp.bfloat16) for value in results]
        if not split:
            for i in range(each):
                outs[0][0, i] = results[i]
            return
        for slot in range(parts):

            @pl.when(step == slot)
            def _(slot=slot):
                for i in range(each):
                    outs[slot][i] = results[i]

    shape = (each, channels, 2 * total)
    if split:
        out_shape = [jax.ShapeDtypeStruct(shape, jnp.bfloat16)] * parts
        out_specs = [pl.BlockSpec(shape, lambda g, place: (0, 0, 0))] * parts
    else:
        out_shape = [jax.ShapeDtypeStruct((parts, *shape), jnp.bfloat16)]
        out_specs = [pl.BlockSpec((1, *shape), lambda g, place: (g, 0, 0, 0))]
    return order.call(
        kernel,
        "channelize",
        place,
        [filter_taps, hist, *pieces, table, table],
        [
            pl.BlockSpec((taps, fft), lambda g, place: (0, 0)),
            pl.BlockSpec((1, each, taps, fft), lambda g, place: (chunk, 0, 0, 0)),
            *[pl.BlockSpec((1, each, spectra, fft), lambda g, place: (inner, 0, 0, 0))] * parts,
            pl.BlockSpec((channels, fft), lambda g, place: (place[0] ^ g, 0)),
            pl.BlockSpec((channels, fft), lambda g, place: (parts + (place[0] ^ g), 0)),
        ],
        out_shape,
        out_specs,
        (parts,),
        [pltpu.VMEM((each, taps + total, LANES), jnp.float32), pltpu.VMEM((each * total, fft), jnp.bfloat16)],
        after=after,
        micros=9.0,
    )


def choose(order, place, candidates, after=()):
    parts, each, channels, width = candidates[0].shape

    def kernel(place, ins, outs, scratch):
        for which, ref in enumerate(ins):

            @pl.when(place[3] == which)
            def _(ref=ref):
                for slot in range(parts):

                    @pl.when(pl.program_id(0) == slot)
                    def _(slot=slot):
                        outs[slot][...] = ref[0]

    def spec(which):
        return pl.BlockSpec(
            (1, each, channels, width), lambda g, place: (jnp.where(place[3] == which, g, 0), 0, 0, 0)
        )

    return order.call(
        kernel,
        "choose",
        place,
        candidates,
        [spec(which) for which in range(len(candidates))],
        [jax.ShapeDtypeStruct((each, channels, width), jnp.bfloat16)] * parts,
        [pl.BlockSpec((each, channels, width), lambda g, place: (0, 0, 0))] * parts,
        (parts,),
        after=after,
    )


def merge(order, place, pieces, cuts=1, position=0, rows=ROWS, into=(), after=()):
    parts = len(pieces)
    each, channels, width = pieces[0].shape
    cut = channels // cuts

    def kernel(place, ins, outs, scratch):
        (work,), me = scratch, place[0]
        for slot in range(parts):
            for i in range(each):
                row = pl.multiple_of(((me ^ slot) * each + i) * channels, channels)
                for lane in range(0, width, LANES):
                    value = ins[slot][i, :, lane : lane + LANES]
                    work[lane // LANES, pl.ds(row, channels), :] = value.astype(jnp.float32)

        for which in range(cuts):

            def block(group, carry, which=which):
                for inner in range(8):
                    k = group * 8 + inner
                    for lane in range(0, width, LANES):
                        value = work[lane // LANES, pl.ds(which * cut + k, ROWS, stride=channels), :]
                        outs[which][k, :, lane : lane + LANES] = value.astype(jnp.bfloat16)
                return carry

            lax.fori_loop(0, cut // 8, block, 0)

    return order.call(
        kernel,
        "merge",
        place,
        pieces,
        [pl.BlockSpec((each, channels, width), lambda g, place: (0, 0, 0))] * parts,
        [jax.ShapeDtypeStruct((cut, rows, width), jnp.bfloat16)] * cuts,
        [pl.BlockSpec((cut, ROWS, width), lambda g, place: (0, position, 0))] * cuts,
        (1,),
        [pltpu.VMEM((width // LANES, ROWS * channels, LANES), jnp.float32)],
        after=after,
        aliased=into,
        micros=2.0,
    )


def turn(order, place, plain, after=()):
    channels, rows, width = plain.shape
    count = 16

    def kernel(place, ins, outs, scratch):
        low = lax.broadcasted_iota(jnp.int32, (rows, width), 1) < width // 2
        for k in range(count):
            other = pltpu.roll(ins[0][k].astype(jnp.float32), width // 2, 1)
            outs[0][k] = jnp.where(low, other, -other).astype(jnp.bfloat16)

    block = pl.BlockSpec((count, rows, width), lambda g, place: (g, 0, 0))
    shape = jax.ShapeDtypeStruct(plain.shape, jnp.bfloat16)
    return order.call(kernel, "turn", place, [plain], [block], [shape], [block], (channels // count,), after=after, micros=2.0)[0]


def correlate(order, place, out, left, sets, cut, cuts, groups, after=()):
    head, tail = left[0][0], left[0][1]
    rows_head, rows_tail, width = head.shape[1], tail.shape[1], head.shape[2]
    half = rows_head + rows_tail
    channels = head.shape[0]
    count = 16
    steps = channels // cuts // count
    average = 2.0 / width
    sizes = [len(candidates) for _, candidates in sets]

    def kernel(place, ins, outs, scratch):
        left_refs, right = ins[:4], list(ins[4:])
        (out_ref,), (columns,), core = outs, scratch, place[1]
        for s, size in enumerate(sizes):
            mine, theirs, *options = right[: 2 + 2 * size]
            del right[: 2 + 2 * size]
            base = place[2 + 2 * s] * (2 * half) if len(sizes) > 1 else 0
            first = pl.multiple_of(base + core * half, ROWS)
            second = pl.multiple_of(base + (1 - core) * half, ROWS)
            for k in range(count):
                columns[k, pl.ds(first, rows_head), :] = mine[k]
                columns[k, pl.ds(second, rows_head), :] = theirs[k]
            for which in range(size):

                @pl.when(place[3 + 2 * s] == which)
                def _(which=which, options=options, first=first, second=second):
                    for k in range(count):
                        columns[k, pl.ds(first + rows_head, rows_tail), :] = options[2 * which][k]
                        columns[k, pl.ds(second + rows_head, rows_tail), :] = options[2 * which + 1][k]

        for k in range(count):
            rows = jnp.concatenate([ref[k] for ref in left_refs], axis=0)
            result = lax.dot_general(rows, columns[k], (((1,), (1,)), ((), ())), preferred_element_type=jnp.float32)
            out_ref[0, k] = result[:half] * average
            out_ref[1, k] = result[half:] * average

    def early(g, place):
        return (cut * steps + g, 0, 0)

    def spec(s, which):
        return pl.BlockSpec((count, rows_tail, width), lambda g, place: (jnp.where(place[3 + 2 * s] == which, g, 0), 0, 0))

    head_spec = pl.BlockSpec((count, rows_head, width), early)
    tail_spec = pl.BlockSpec((count, rows_tail, width), lambda g, place: (g, 0, 0))
    operands = [left[0][0], left[0][1], left[1][0], left[1][1]]
    specs = [head_spec, tail_spec, head_spec, tail_spec]
    for s, (heads, candidates) in enumerate(sets):
        operands += heads
        specs += [head_spec] * 2
        for which, pair in enumerate(candidates):
            operands += pair
            specs += [spec(s, which)] * 2
    lanes = len(sets) * 2 * half
    if len(sets) > 1:
        out_spec = pl.BlockSpec((2, count, half, lanes), lambda g, place: (0, cut * steps + g, 0, 0))
    else:
        out_spec = pl.BlockSpec((2, count, half, lanes), lambda g, place: (0, cut * steps + g, 0, place[2]))
    return order.call(
        kernel,
        "correlate",
        place,
        operands,
        specs,
        [jax.ShapeDtypeStruct((2, channels, half, groups * 2 * half), jnp.float32)],
        [out_spec],
        (steps,),
        [pltpu.VMEM((count, lanes, width), jnp.bfloat16)],
        after=after,
        aliased=[] if out is None else [out],
        micros=10.0,
    )[0]


def exchange(pieces):
    count = len(pieces)
    return [pieces[0]] + [
        lax.ppermute(pieces[slot], "chan", [(i, i ^ slot) for i in range(count)]) for slot in range(1, count)
    ]


def body(voltages, history, filter_taps, table):
    parts = lax.axis_size("chan")
    tiles = lax.axis_size("tile")
    groups = tiles // 2
    me = lax.axis_index("chan")
    tile = lax.axis_index("tile")
    core, level = lax.rem(tile, 2), tile // 2
    taps, fft = filter_taps.shape
    spectra = voltages.shape[1] // fft
    chunks = voltages.shape[0] // ROWS
    later = (chunks - 1) * ROWS
    cuts = 2
    order = Order()

    def place(*pairs):
        return jnp.stack([jnp.asarray(x, jnp.int32) for x in (me, core, *[x for pair in pairs for x in pair])])

    def along(value, lowest, highest, step):
        pairs = [(2 * g + c, 2 * (g + step) + c) for g in range(lowest, highest + 1) for c in range(2)]
        return lax.ppermute(value, "tile", pairs)

    def hops(value):
        up, down = {0: value}, {0: value}
        for hop in range(1, groups):
            up[hop] = along(up[hop - 1], hop - 1, groups - 2, 1)
            down[hop] = along(down[hop - 1], 1, groups - hop, -1)
        return up, down

    def swap(value):
        return lax.ppermute(value, "tile", [(i, i ^ 1) for i in range(tiles)])

    here = place((level, 0))

    def pick(hop):
        below, above = level >= hop, level + hop < groups
        source = jnp.where(below, level - hop, jnp.where(above, level + hop, level + groups - hop))
        return source, jnp.where(below, 0, jnp.where(above, 1, 2))

    raw = {}

    def read(chunk, count):
        pieces = exchange(convert(order, here, voltages, chunk, count, parts, spectra, fft))
        for inner in range(count):
            raw[chunk + inner] = (pieces, inner)

    def filter_chunk(chunk, split, after=()):
        return channelize(order, here, filter_taps, hist, *raw[chunk], table, chunk, split, after)

    def arrived(hop):
        return (early_up[hop], early_down[hop]) if hop < groups else ()

    read(0, 1)
    if chunks > 1:
        read(1, 1)
    hist = own_history(order, here, history, parts, taps, fft)
    (early,) = filter_chunk(0, False)
    early_up, early_down = hops(early)
    if chunks > 2:
        read(2, chunks - 2)
    sent, plain = {}, []
    for chunk in range(1, chunks):
        sent[chunk] = exchange(filter_chunk(chunk, True, arrived(1) if chunk == chunks - 1 else ()))
        if chunk > 1:
            plain = merge(order, here, sent[chunk - 1], cuts, chunk - 2, later, plain)
    plain = merge(order, here, sent[chunks - 1], cuts, chunks - 2, later, plain, arrived(2))
    lines = [hops(value) for value in plain]

    (head,) = merge(order, here, exchange(choose(order, here, [early])))
    head_turned = turn(order, here, head, arrived(3))
    turned = [turn(order, here, value) for value in plain]
    lefts = [((head, plain[cut]), (head_turned, turned[cut])) for cut in range(cuts)]

    swapped = {}

    def both(kind, hop, cut):
        key = (kind, hop, cut)
        if key not in swapped:
            swapped[key] = swap(lines[cut][kind][hop])
        return swapped[key]

    def work(hop):
        if hop == 0:
            heads = [head, swap(head)]
            return (level, 0), [(heads, [(plain[cut], swap(plain[cut]))]) for cut in range(cuts)]
        chip = pick(hop)
        options = [(0, hop), (1, hop)] + ([(1, groups - hop)] if 2 * hop > groups else [])
        arrays = [(early_up, early_down)[kind][h] for kind, h in options]
        (own,) = merge(order, here, exchange(choose(order, place(chip), arrays)))
        heads = [own, swap(own)]
        return chip, [
            (heads, [(lines[cut][kind][h], both(kind, h, cut)) for kind, h in options]) for cut in range(cuts)
        ]

    out = None
    if 2 * voltages.shape[0] % LANES == 0:
        for hop in range(groups):
            chip, sets = work(hop)
            for cut in range(cuts):
                out = correlate(order, place(chip), out, lefts[cut], [sets[cut]], cut, cuts, groups)
    else:
        chips, sets = zip(*[work(hop) for hop in range(groups)])
        for cut in range(cuts):
            out = correlate(order, place(*chips), out, lefts[cut], [s[cut] for s in sets], cut, cuts, groups)
    return out


def solution(mesh):
    in_specs = (P("tile", "chan"), P("tile", None), P(), P())
    out_specs = P(None, "chan", "tile", None)
    mapped = jax.shard_map(body, mesh=mesh, in_specs=in_specs, out_specs=out_specs, check_vma=False)

    def run(voltages, history, filter_taps):
        return mapped(voltages, history, filter_taps, jnp.asarray(dft_rows(filter_taps.shape[1])))

    return run
```

time: 1000 us -> 389 us (0.39)
  waiting for transfers between devices: 570 us -> 149 us
  Pallas kernels: 0 us -> 158 us
  other arithmetic: 153 us -> 0.15 us
  local copies, waits for them, and re-layouts: 137 us -> 3.93 us
  starting transfers between devices: 6.85 us -> 75 us
  matrix products: 63.4 us -> 0 us
  blocking collectives: 54.1 us -> 0 us
  between operations: 13.4 us -> 0.64 us
    all_gather x1 -> x0, waiting for transfers between devices: 535 us -> none  [body(): lax.all_gather(turned, 'tile', axis=0, tiled=True)]
    pallas_call x0 -> x30, Pallas kernels: none -> 158 us  [call(): pl.pallas_call(wrapped, out_shape=[*out_shape, jax.ShapeDtypeStruct((8, L...]
    ppermute x1 -> x66, waiting for transfers between devices: 35.1 us -> 149 us  [the longest x18 83.9 us: along(): return lax.ppermute(value, 'tile', pairs)]
    dot_general x1 -> x0, other arithmetic: 69 us -> none  [body(): jnp.dot(filtered.reshape(-1, FFT), dft_table(FFT, CH), preferred_element_...]
    ppermute x1 -> x66, starting transfers between devices: 6.85 us -> 75 us  [the longest x18 36.6 us: along(): return lax.ppermute(value, 'tile', pairs)]
    dot_general x2 -> x0, matrix products: 63.4 us -> none  [the longest x1 50.7 us: body(): jnp.einsum('qaspc,bspc->qcab', row_sets, lax.all_gather(turned, 'tile', a...]
    all_to_all x1 -> x0, blocking collectives: 54.1 us -> none  [body(): lax.all_to_all(spectra, 'chan', split_axis=3, concat_axis=1, tiled=True)]
    another operation x3 -> x2, other arithmetic: 49.4 us -> 0.15 us  [place(): jnp.stack([jnp.asarray(x, jnp.int32) for x in (me, core, *[x for pair in...]
  transfers between devices with their start and end apart: 2 -> 66, of which waited for: 2 -> 19; matrix products, arithmetic and copies ran while one was open for 8% -> 0% of each run, Pallas kernels for 0% -> 36%
where the time goes in v1:
time: 389 us; the launch traced here: 387 us
  Pallas kernels  158 us (41%)
  waiting for transfers between devices  149 us (38%)
  starting transfers between devices  75 us (19%)
  local copies, waits for them, and re-layouts  3.93 us (1%)
    pallas_call x30, Pallas kernels, call(): pl.pallas_call(wrapped, out_shape=[*out_shape, jax.ShapeDtypeStruct((8, L...  158 us
    ppermute x18, waiting for transfers between devices, along(): return lax.ppermute(value, 'tile', pairs)  83.9 us
    ppermute x30, waiting for transfers between devices, exchange(): lax.ppermute(pieces[slot], 'chan', [(i, i ^ slot) for i in range(count)])  65.4 us
    ppermute x18, starting transfers between devices, along(): return lax.ppermute(value, 'tile', pairs)  36.6 us
    ppermute x30, starting transfers between devices, exchange(): lax.ppermute(pieces[slot], 'chan', [(i, i ^ slot) for i in range(count)])  35.7 us
  transfers between devices with their start and end apart: 66, of which 19 were waited for; matrix products, arithmetic and copies ran while one was open for 0% of the time, Pallas kernels for 36%

profile of v1, /device:TPU:0, one launch (start us, length us, event | category | flops | bytes accessed | tf_op | source)
XLA Modules:
  0.0 386.8 jit_solution(13370301133354193645)
XLA Ops:
  0.2 3.3 convert.3
  3.5 3.0 collective-permute-start
  6.5 1.6 collective-permute-start.1
  8.0 3.3 convert.4
  11.3 3.0 collective-permute-start.10
  14.9 4.6 %history.1 = (bf16[4,4,16,2048]{3,2,1,0:T(8,128)(2,1)S(1)}, f32[8,128]{1,0:T(8,128)S(1)}) custom-call(s32[4]{0:T(128)S(1)} %get-tuple-element.192.place_ref, s32[64,30720]{1,0:T(8,128)} %refs_0_.10, f32[8,128]{1,0:T(8,128)S(1)} %get-tuple-element.98.refs_1_), custom_call_target="tpu_custom_call" | custom-call | flops 5175000064 | tf_op jit(solution)/shard_map/history/pallas_call | solution.py:47
  19.7 6.2 %collective-permute-done.1.refs_4_ = bf16[1,4,16,2048]{3,2,1,0:T(8,128)(2,1)S(1)} collective-permute-done((bf16[1,4,16,2048]{3,2,1,0:T(8,128)(2,1)S(1)}, bf16[1,4,16,2048]{3,2,1,0:T(8,128)(2,1)S(1)}, u32[]{:S(2)}, u32[]{:S(2)}) %collective-permute-start.1) | collective-permute-done | bytes 262176 | tf_op jit(solution)/shard_map/ppermute | solution.py:390
  25.9 9.1 %channelize.4 = (bf16[4,4,256,128]{3,2,1,0:T(8,128)(2,1)S(1)}, f32[8,128]{1,0:T(8,128)S(1)}) custom-call(s32[4]{0:T(128)S(1)} %get-tuple-element.192.place_ref, s32[16,2048]{1,0:T(8,128)S(1)} %copy-done.8, bf16[4,4,16,2048]{3,2,1,0:T(8,128)(2,1)S(1)} %get-tuple-element.99.refs_1_, bf16[1,4,16,2048]{3,2,1,0:T(8,128)(2,1)S(1)} %get-tuple-element.100.refs_2_, ...), custom_call_target="tpu_custom_call" | custom-call | flops 10350000128 | tf_op jit(solution)/shard_map/channelize/pallas_call | solution.py:47
  35.0 3.3 collective-permute-start.6
  39.6 4.5 %convert.5 = (bf16[2,4,16,2048]{3,2,1,0:T(8,128)(2,1)S(1)}, bf16[2,4,16,2048]{3,2,1,0:T(8,128)(2,1)S(1)}, bf16[2,4,16,2048]{3,2,1,0:T(8,128)(2,1)S(1)}, bf16[2,4,16,2048]{3,2,1,0:T(8,128)(2,1)S(1)}, f32[8,128]{1,0:T(8,128)S(1)}) custom-call(s32[4]{0:T(128)S(1)} %get-tuple-element.192.place_ref, s32[64,32768]{1,0:T(8,128)} %refs_0_.12, ...), custom_call_target="tpu_custom_call" | custom-call | flops 5750000128 | tf_op jit(solution)/shard_map/convert/pallas_call | solution.py:47
  44.2 2.6 collective-permute-start.4
  46.9 1.4 collective-permute-start.5
  48.3 9.2 %channelize.5 = (bf16[4,256,128]{2,1,0:T(8,128)(2,1)S(1)}, bf16[4,256,128]{2,1,0:T(8,128)(2,1)S(1)}, bf16[4,256,128]{2,1,0:T(8,128)(2,1)S(1)}, bf16[4,256,128]{2,1,0:T(8,128)(2,1)S(1)}, f32[8,128]{1,0:T(8,128)S(1)}) custom-call(s32[4]{0:T(128)S(1)} %get-tuple-element.192.place_ref, s32[16,2048]{1,0:T(8,128)S(1)} %copy-done.8, ...), custom_call_target="tpu_custom_call" | custom-call | flops 10350000128 | tf_op jit(solution)/shard_map/channelize/pallas_call | solution.py:47
  57.5 1.6 collective-permute-done.3.refs_3_
  59.1 9.7 %collective-permute-done.4.refs_4_ = bf16[2,4,16,2048]{3,2,1,0:T(8,128)(2,1)S(1)} collective-permute-done((bf16[2,4,16,2048]{3,2,1,0:T(8,128)(2,1)S(1)}, bf16[2,4,16,2048]{3,2,1,0:T(8,128)(2,1)S(1)}, u32[]{:S(2)}, u32[]{:S(2)}) %collective-permute-start.4) | collective-permute-done | bytes 524320 | tf_op jit(solution)/shard_map/ppermute | solution.py:390
  70.1 2.5 collective-permute-start.13
  72.6 9.2 %channelize.6 = (bf16[4,256,128]{2,1,0:T(8,128)(2,1)S(1)}, bf16[4,256,128]{2,1,0:T(8,128)(2,1)S(1)}, bf16[4,256,128]{2,1,0:T(8,128)(2,1)S(1)}, bf16[4,256,128]{2,1,0:T(8,128)(2,1)S(1)}, f32[8,128]{1,0:T(8,128)S(1)}) custom-call(s32[4]{0:T(128)S(1)} %get-tuple-element.192.place_ref, s32[16,2048]{1,0:T(8,128)S(1)} %copy-done.8, ...), custom_call_target="tpu_custom_call" | custom-call | flops 10350000128 | tf_op jit(solution)/shard_map/channelize/pallas_call | solution.py:47
  82.4 1.5 collective-permute-start.18
  85.4 2.1 merge.7
  89.6 9.2 %channelize.7 = (bf16[4,256,128]{2,1,0:T(8,128)(2,1)S(1)}, bf16[4,256,128]{2,1,0:T(8,128)(2,1)S(1)}, bf16[4,256,128]{2,1,0:T(8,128)(2,1)S(1)}, bf16[4,256,128]{2,1,0:T(8,128)(2,1)S(1)}, f32[8,128]{1,0:T(8,128)S(1)}) custom-call(s32[4]{0:T(128)S(1)} %get-tuple-element.192.place_ref, s32[16,2048]{1,0:T(8,128)S(1)} %copy-done.8, ...), custom_call_target="tpu_custom_call" | custom-call | flops 10350000128 | tf_op jit(solution)/shard_map/channelize/pallas_call | solution.py:47
  99.4 1.5 collective-permute-start.15
  102.4 2.1 merge.8
  106.8 5.5 %collective-permute-done.16.refs_3_ = bf16[4,256,128]{2,1,0:T(8,128)(2,1)S(1)} collective-permute-done((bf16[4,256,128]{2,1,0:T(8,128)(2,1)S(1)}, bf16[4,256,128]{2,1,0:T(8,128)(2,1)S(1)}, u32[]{:S(2)}, u32[]{:S(2)}) %collective-permute-start.16) | collective-permute-done | bytes 262176 | tf_op jit(solution)/shard_map/ppermute | solution.py:390
  112.3 2.9 merge.9
  118.8 3.6 collective-permute-done.22.refs_1_
  122.4 10.1 %collective-permute-done.23.refs_2_ = bf16[4,256,128]{2,1,0:T(8,128)(2,1)S(1)} collective-permute-done((bf16[4,256,128]{2,1,0:T(8,128)(2,1)S(1)}, bf16[4,256,128]{2,1,0:T(8,128)(2,1)S(1)}, u32[]{:S(2)}, u32[]{:S(2)}) %collective-permute-start.23) | collective-permute-done | bytes 262176 | tf_op jit(solution)/shard_map/ppermute | solution.py:390
  132.5 2.1 merge.10
  134.7 8.4 %collective-permute-start.38 = (bf16[128,48,128]{2,1,0:T(8,128)(2,1)S(1)}, bf16[128,48,128]{2,1,0:T(8,128)(2,1)}, u32[]{:S(2)}, u32[]{:S(2)}) collective-permute-start(bf16[128,48,128]{2,1,0:T(8,128)(2,1)S(1)} %get-tuple-element.147.refs_0_.refs_1_.refs_6_), channel_id=1, source_target_pairs={{0,8},{4,12},{8,16},{12,20},{16,24},{20,28},{1,9},{5,13},{9,17},{1... | collective-permute-start | bytes 4718600 | tf_op jit(solution)/shard_map/ppermute | solution.py:413
  144.6 2.1 turn.3
  146.7 1.6 turn.4
  148.3 1.6 turn.5
  151.1 5.5 %collective-permute-start.34 = (bf16[128,48,128]{2,1,0:T(8,128)(2,1)S(1)}, bf16[128,48,128]{2,1,0:T(8,128)(2,1)}, u32[]{:S(2)}, u32[]{:S(2)}) collective-permute-start(bf16[128,48,128]{2,1,0:T(8,128)(2,1)S(1)} %copy-done.1), channel_id=1, source_target_pairs={{0,8},{4,12},{8,16},{12,20},{16,24},{20,28},{1,9},{5,13},{9,17},{1... | collective-permute-start | bytes 4718600 | tf_op jit(solution)/shard_map/ppermute | solution.py:413
  157.9 9.7 %correlate.8 = (f32[2,256,64,512]{3,2,1,0:T(8,128)}, f32[8,128]{1,0:T(8,128)S(1)}) custom-call(s32[4]{0:T(128)S(1)} %get-tuple-element.192.place_ref, bf16[256,16,128]{2,1,0:T(8,128)(2,1)S(1)} %get-tuple-element.143.refs_0_.refs_4_, bf16[128,48,128]{2,1,0:T(8,128)(2,1)S(1)} %get-tuple-element.147.refs_0_.refs_1_.refs_6_, ...), custom_call_target="tpu_custom_call" | custom-call | flops 11500000256 | tf_op jit(solution)/shard_map/correlate/pallas_call | solution.py:47
  167.6 9.7 %correlate.9 = (f32[2,256,64,512]{3,2,1,0:T(8,128)}, f32[8,128]{1,0:T(8,128)S(1)}) custom-call(s32[4]{0:T(128)S(1)} %get-tuple-element.192.place_ref, bf16[256,16,128]{2,1,0:T(8,128)(2,1)S(1)} %get-tuple-element.143.refs_0_.refs_4_, bf16[128,48,128]{2,1,0:T(8,128)(2,1)S(1)} %copy-done.1, ...), custom_call_target="tpu_custom_call", output_to_operand_aliasing={{0}: (9, {})} | custom-call | flops 11500000256 | tf_op jit(solution)/shard_map/correlate/pallas_call | solution.py:47
  178.6 1.8 collective-permute-start.31
  180.3 1.9 collective-permute-done.40.refs_8_.refs_10_
  182.3 4.3 %collective-permute-done.30.refs_1_ = bf16[4,256,128]{2,1,0:T(8,128)(2,1)S(1)} collective-permute-done((bf16[4,256,128]{2,1,0:T(8,128)(2,1)S(1)}, bf16[4,256,128]{2,1,0:T(8,128)(2,1)S(1)}, u32[]{:S(2)}, u32[]{:S(2)}) %collective-permute-start.30) | collective-permute-done | bytes 262176 | tf_op jit(solution)/shard_map/ppermute | solution.py:390
  186.7 1.5 collective-permute-start.32
  188.3 7.9 %collective-permute-done.32.refs_3_ = bf16[4,256,128]{2,1,0:T(8,128)(2,1)S(1)} collective-permute-done((bf16[4,256,128]{2,1,0:T(8,128)(2,1)S(1)}, bf16[4,256,128]{2,1,0:T(8,128)(2,1)S(1)}, u32[]{:S(2)}, u32[]{:S(2)}) %collective-permute-start.32) | collective-permute-done | bytes 262176 | tf_op jit(solution)/shard_map/ppermute | solution.py:390
  196.2 2.1 merge.11
  198.3 11.5 %collective-permute-done.34.refs_6_ = bf16[128,48,128]{2,1,0:T(8,128)(2,1)} collective-permute-done((bf16[128,48,128]{2,1,0:T(8,128)(2,1)S(1)}, bf16[128,48,128]{2,1,0:T(8,128)(2,1)}, u32[]{:S(2)}, u32[]{:S(2)}) %collective-permute-start.34) | collective-permute-done | bytes 1572896 | tf_op jit(solution)/shard_map/ppermute | solution.py:413
  209.9 5.4 %collective-permute-done.36.refs_8_.refs_10_ = bf16[128,48,128]{2,1,0:T(8,128)(2,1)} collective-permute-done((bf16[128,48,128]{2,1,0:T(8,128)(2,1)S(1)}, bf16[128,48,128]{2,1,0:T(8,128)(2,1)}, u32[]{:S(2)}, u32[]{:S(2)}) %collective-permute-start.36) | collective-permute-done | bytes 1572896 | tf_op jit(solution)/shard_map/ppermute | solution.py:413
  215.2 1.8 collective-permute-start.50
  218.3 1.8 collective-permute-start.46
  220.2 10.3 %correlate.10 = (f32[2,256,64,512]{3,2,1,0:T(8,128)}, f32[8,128]{1,0:T(8,128)S(1)}) custom-call(s32[4]{0:T(128)S(1)} %get-tuple-element.189.place_ref, bf16[256,16,128]{2,1,0:T(8,128)(2,1)S(1)} %get-tuple-element.143.refs_0_.refs_4_, bf16[128,48,128]{2,1,0:T(8,128)(2,1)S(1)} %get-tuple-element.147.refs_0_.refs_1_.refs_6_, ...), custom_call_target="tpu_custom_call", output_to_operand_aliasing={{0}: (11, {})} | custom-call | flops 11500000256 | tf_op jit(solution)/shard_map/correlate/pallas_call | solution.py:47
  230.5 1.5 collective-permute-start.48
  232.0 10.4 %correlate.11 = (f32[2,256,64,512]{3,2,1,0:T(8,128)}, f32[8,128]{1,0:T(8,128)S(1)}) custom-call(s32[4]{0:T(128)S(1)} %get-tuple-element.189.place_ref, bf16[256,16,128]{2,1,0:T(8,128)(2,1)S(1)} %get-tuple-element.143.refs_0_.refs_4_, bf16[128,48,128]{2,1,0:T(8,128)(2,1)S(1)} %copy-done.1, ...), custom_call_target="tpu_custom_call", output_to_operand_aliasing={{0}: (11, {})} | custom-call | flops 11500000256 | tf_op jit(solution)/shard_map/correlate/pallas_call | solution.py:47
  243.7 1.7 collective-permute-start.43
  245.5 11.0 %collective-permute-done.52.refs_8_ = bf16[128,48,128]{2,1,0:T(8,128)(2,1)} collective-permute-done((bf16[128,48,128]{2,1,0:T(8,128)(2,1)}, bf16[128,48,128]{2,1,0:T(8,128)(2,1)}, u32[]{:S(2)}, u32[]{:S(2)}) %collective-permute-start.52) | collective-permute-done | bytes 1572896 | tf_op jit(solution)/shard_map/ppermute | solution.py:413
  256.9 1.6 collective-permute-start.44
  258.6 7.6 %collective-permute-done.44.refs_3_ = bf16[4,256,128]{2,1,0:T(8,128)(2,1)S(1)} collective-permute-done((bf16[4,256,128]{2,1,0:T(8,128)(2,1)S(1)}, bf16[4,256,128]{2,1,0:T(8,128)(2,1)S(1)}, u32[]{:S(2)}, u32[]{:S(2)}) %collective-permute-start.44) | collective-permute-done | bytes 262176 | tf_op jit(solution)/shard_map/ppermute | solution.py:390
  266.1 2.1 merge.12
  268.8 21.0 %collective-permute-done.48.refs_8_ = bf16[128,48,128]{2,1,0:T(8,128)(2,1)} collective-permute-done((bf16[128,48,128]{2,1,0:T(8,128)(2,1)}, bf16[128,48,128]{2,1,0:T(8,128)(2,1)}, u32[]{:S(2)}, u32[]{:S(2)}) %collective-permute-start.48) | collective-permute-done | bytes 1572896 | tf_op jit(solution)/shard_map/ppermute | solution.py:413
  289.8 1.8 collective-permute-start.62
  293.7 10.4 %correlate.12 = (f32[2,256,64,512]{3,2,1,0:T(8,128)}, f32[8,128]{1,0:T(8,128)S(1)}) custom-call(s32[4]{0:T(128)S(1)} %get-tuple-element.191.place_ref, bf16[256,16,128]{2,1,0:T(8,128)(2,1)S(1)} %get-tuple-element.143.refs_0_.refs_4_, bf16[128,48,128]{2,1,0:T(8,128)(2,1)S(1)} %get-tuple-element.147.refs_0_.refs_1_.refs_6_, ...), custom_call_target="tpu_custom_call", output_to_operand_aliasing={{0}: (11, {})} | custom-call | flops 11500000256 | tf_op jit(solution)/shard_map/correlate/pallas_call | solution.py:47
  305.3 10.4 %correlate.13 = (f32[2,256,64,512]{3,2,1,0:T(8,128)}, f32[8,128]{1,0:T(8,128)S(1)}) custom-call(s32[4]{0:T(128)S(1)} %get-tuple-element.191.place_ref, bf16[256,16,128]{2,1,0:T(8,128)(2,1)S(1)} %get-tuple-element.143.refs_0_.refs_4_, bf16[128,48,128]{2,1,0:T(8,128)(2,1)S(1)} %copy-done.1, ...), custom_call_target="tpu_custom_call", output_to_operand_aliasing={{0}: (11, {})} | custom-call | flops 11500000256 | tf_op jit(solution)/shard_map/correlate/pallas_call | solution.py:47
  316.6 1.7 collective-permute-start.54
  318.9 12.1 %collective-permute-done.64.refs_8_ = bf16[128,48,128]{2,1,0:T(8,128)(2,1)} collective-permute-done((bf16[128,48,128]{2,1,0:T(8,128)(2,1)}, bf16[128,48,128]{2,1,0:T(8,128)(2,1)}, u32[]{:S(2)}, u32[]{:S(2)}) %collective-permute-start.64) | collective-permute-done | bytes 1572896 | tf_op jit(solution)/shard_map/ppermute | solution.py:413
  331.5 1.6 collective-permute-start.56
  333.1 7.6 %collective-permute-done.56.refs_3_ = bf16[4,256,128]{2,1,0:T(8,128)(2,1)S(1)} collective-permute-done((bf16[4,256,128]{2,1,0:T(8,128)(2,1)S(1)}, bf16[4,256,128]{2,1,0:T(8,128)(2,1)S(1)}, u32[]{:S(2)}, u32[]{:S(2)}) %collective-permute-start.56) | collective-permute-done | bytes 262176 | tf_op jit(solution)/shard_map/ppermute | solution.py:390
  340.7 2.1 merge.13
  343.3 21.0 %collective-permute-done.60.refs_8_ = bf16[128,48,128]{2,1,0:T(8,128)(2,1)} collective-permute-done((bf16[128,48,128]{2,1,0:T(8,128)(2,1)}, bf16[128,48,128]{2,1,0:T(8,128)(2,1)}, u32[]{:S(2)}, u32[]{:S(2)}) %collective-permute-start.60) | collective-permute-done | bytes 1572896 | tf_op jit(solution)/shard_map/ppermute | solution.py:413
  366.0 10.4 %correlate.14 = (f32[2,256,64,512]{3,2,1,0:T(8,128)}, f32[8,128]{1,0:T(8,128)S(1)}) custom-call(s32[4]{0:T(128)S(1)} %get-tuple-element.193.place_ref, bf16[256,16,128]{2,1,0:T(8,128)(2,1)S(1)} %get-tuple-element.143.refs_0_.refs_4_, bf16[128,48,128]{2,1,0:T(8,128)(2,1)S(1)} %get-tuple-element.147.refs_0_.refs_1_.refs_6_, ...), custom_call_target="tpu_custom_call", output_to_operand_aliasing={{0}: (13, {})} | custom-call | flops 11500000256 | tf_op jit(solution)/shard_map/correlate/pallas_call | solution.py:47
  376.4 10.4 %correlate.15 = (f32[2,256,64,512]{3,2,1,0:T(8,128)}, f32[8,128]{1,0:T(8,128)}) custom-call(s32[4]{0:T(128)S(1)} %get-tuple-element.193.place_ref, bf16[256,16,128]{2,1,0:T(8,128)(2,1)S(1)} %get-tuple-element.143.refs_0_.refs_4_, bf16[128,48,128]{2,1,0:T(8,128)(2,1)S(1)} %copy-done.1, ...), custom_call_target="tpu_custom_call", output_to_operand_aliasing={{0}: (13, {})} | custom-call | flops 11500000256 | tf_op jit(solution)/shard_map/correlate/pallas_call | solution.py:47
  (132 shorter events, 32.4 us)
Async XLA Ops:
  3.5 16.0 %collective-permute-start = (bf16[1,4,16,2048]{3,2,1,0:T(8,128)(2,1)S(1)}, bf16[1,4,16,2048]{3,2,1,0:T(8,128)(2,1)S(1)}, u32[]{:S(2)}, u32[]{:S(2)}) collective-permute-start(bf16[1,4,16,2048]{3,2,1,0:T(8,128)(2,1)S(1)} %get-tuple-element.101), channel_id=1, source_target_pairs={{0,1},{1,0},{2,3},{3,2},{4,5},{5,4},{6,7},{7,6},{8,9},{9,8},{10,11... | collective-permute-start | bytes 786440 | tf_op jit(solution)/shard_map/ppermute | solution.py:390
  6.5 19.5 %collective-permute-start.1 = (bf16[1,4,16,2048]{3,2,1,0:T(8,128)(2,1)S(1)}, bf16[1,4,16,2048]{3,2,1,0:T(8,128)(2,1)S(1)}, u32[]{:S(2)}, u32[]{:S(2)}) collective-permute-start(bf16[1,4,16,2048]{3,2,1,0:T(8,128)(2,1)S(1)} %get-tuple-element.102), channel_id=1, source_target_pairs={{0,2},{1,3},{2,0},{3,1},{4,6},{5,7},{6,4},{7,5},{8,10},{9,11},{10,... | collective-permute-start | bytes 786440 | tf_op jit(solution)/shard_map/ppermute | solution.py:390
  8.0 17.9 %collective-permute-start.2 = (bf16[1,4,16,2048]{3,2,1,0:T(8,128)(2,1)S(1)}, bf16[1,4,16,2048]{3,2,1,0:T(8,128)(2,1)S(1)}, u32[]{:S(2)}, u32[]{:S(2)}) collective-permute-start(bf16[1,4,16,2048]{3,2,1,0:T(8,128)(2,1)S(1)} %get-tuple-element.103), channel_id=1, source_target_pairs={{0,3},{1,2},{2,1},{3,0},{4,7},{5,6},{6,5},{7,4},{8,11},{9,10},{10,... | collective-permute-start | bytes 786440 | tf_op jit(solution)/shard_map/ppermute | solution.py:390
  11.3 32.8 %collective-permute-start.10 = (bf16[1,4,16,2048]{3,2,1,0:T(8,128)(2,1)S(1)}, bf16[1,4,16,2048]{3,2,1,0:T(8,128)(2,1)S(1)}, u32[]{:S(2)}, u32[]{:S(2)}) collective-permute-start(bf16[1,4,16,2048]{3,2,1,0:T(8,128)(2,1)S(1)} %get-tuple-element.114), channel_id=1, source_target_pairs={{0,3},{1,2},{2,1},{3,0},{4,7},{5,6},{6,5},{7,4},{8,11},{9,10},{10,... | collective-permute-start | bytes 786440 | tf_op jit(solution)/shard_map/ppermute | solution.py:390
  14.4 29.9 %collective-permute-start.8 = (bf16[1,4,16,2048]{3,2,1,0:T(8,128)(2,1)S(1)}, bf16[1,4,16,2048]{3,2,1,0:T(8,128)(2,1)S(1)}, u32[]{:S(2)}, u32[]{:S(2)}) collective-permute-start(bf16[1,4,16,2048]{3,2,1,0:T(8,128)(2,1)S(1)} %get-tuple-element.112), channel_id=1, source_target_pairs={{0,1},{1,0},{2,3},{3,2},{4,5},{5,4},{6,7},{7,6},{8,9},{9,8},{10,11... | collective-permute-start | bytes 786440 | tf_op jit(solution)/shard_map/ppermute | solution.py:390
  19.5 27.4 %collective-permute-start.9 = (bf16[1,4,16,2048]{3,2,1,0:T(8,128)(2,1)S(1)}, bf16[1,4,16,2048]{3,2,1,0:T(8,128)(2,1)S(1)}, u32[]{:S(2)}, u32[]{:S(2)}) collective-permute-start(bf16[1,4,16,2048]{3,2,1,0:T(8,128)(2,1)S(1)} %get-tuple-element.113), channel_id=1, source_target_pairs={{0,2},{1,3},{2,0},{3,1},{4,6},{5,7},{6,4},{7,5},{8,10},{9,11},{10,... | collective-permute-start | bytes 786440 | tf_op jit(solution)/shard_map/ppermute | solution.py:390
  35.0 52.5 %collective-permute-start.6 = (bf16[4,4,256,128]{3,2,1,0:T(8,128)(2,1)S(1)}, bf16[4,4,256,128]{3,2,1,0:T(8,128)(2,1)S(1)}, u32[]{:S(2)}, u32[]{:S(2)}) collective-permute-start(bf16[4,4,256,128]{3,2,1,0:T(8,128)(2,1)S(1)} %get-tuple-element.105.refs_0_), channel_id=1, source_target_pairs={{0,8},{4,12},{8,16},{12,20},{16,24},{20,28},{1,9},{5,13},{9,17},{1... | collective-permute-start | bytes 3145736 | tf_op jit(solution)/shard_map/ppermute | solution.py:413
  38.3 49.9 %collective-permute-start.7 = (bf16[4,4,256,128]{3,2,1,0:T(8,128)(2,1)S(1)}, bf16[4,4,256,128]{3,2,1,0:T(8,128)(2,1)S(1)}, u32[]{:S(2)}, u32[]{:S(2)}) collective-permute-start(bf16[4,4,256,128]{3,2,1,0:T(8,128)(2,1)S(1)} %get-tuple-element.105.refs_0_), channel_id=1, source_target_pairs={{8,0},{12,4},{16,8},{20,12},{24,16},{28,20},{9,1},{13,5},{17,9},{2... | collective-permute-start | bytes 3145736 | tf_op jit(solution)/shard_map/ppermute | solution.py:413
  44.1 14.9 %collective-permute-start.3 = (bf16[2,4,16,2048]{3,2,1,0:T(8,128)(2,1)S(1)}, bf16[2,4,16,2048]{3,2,1,0:T(8,128)(2,1)S(1)}, u32[]{:S(2)}, u32[]{:S(2)}) collective-permute-start(bf16[2,4,16,2048]{3,2,1,0:T(8,128)(2,1)S(1)} %get-tuple-element.108), channel_id=1, source_target_pairs={{0,1},{1,0},{2,3},{3,2},{4,5},{5,4},{6,7},{7,6},{8,9},{9,8},{10,11... | collective-permute-start | bytes 1572872 | tf_op jit(solution)/shard_map/ppermute | solution.py:390
  44.2 24.5 %collective-permute-start.4 = (bf16[2,4,16,2048]{3,2,1,0:T(8,128)(2,1)S(1)}, bf16[2,4,16,2048]{3,2,1,0:T(8,128)(2,1)S(1)}, u32[]{:S(2)}, u32[]{:S(2)}) collective-permute-start(bf16[2,4,16,2048]{3,2,1,0:T(8,128)(2,1)S(1)} %get-tuple-element.109), channel_id=1, source_target_pairs={{0,2},{1,3},{2,0},{3,1},{4,6},{5,7},{6,4},{7,5},{8,10},{9,11},{10,... | collective-permute-start | bytes 1572872 | tf_op jit(solution)/shard_map/ppermute | solution.py:390
  46.9 23.2 %collective-permute-start.5 = (bf16[2,4,16,2048]{3,2,1,0:T(8,128)(2,1)S(1)}, bf16[2,4,16,2048]{3,2,1,0:T(8,128)(2,1)S(1)}, u32[]{:S(2)}, u32[]{:S(2)}) collective-permute-start(bf16[2,4,16,2048]{3,2,1,0:T(8,128)(2,1)S(1)} %get-tuple-element.110), channel_id=1, source_target_pairs={{0,3},{1,2},{2,1},{3,0},{4,7},{5,6},{6,5},{7,4},{8,11},{9,10},{10,... | collective-permute-start | bytes 1572872 | tf_op jit(solution)/shard_map/ppermute | solution.py:390
  59.1 22.7 %collective-permute-start.11 = (bf16[4,256,128]{2,1,0:T(8,128)(2,1)S(1)}, bf16[4,256,128]{2,1,0:T(8,128)(2,1)S(1)}, u32[]{:S(2)}, u32[]{:S(2)}) collective-permute-start(bf16[4,256,128]{2,1,0:T(8,128)(2,1)S(1)} %get-tuple-element.117), channel_id=1, source_target_pairs={{0,1},{1,0},{2,3},{3,2},{4,5},{5,4},{6,7},{7,6},{8,9},{9,8},{10,11... | collective-permute-start | bytes 786440 | tf_op jit(solution)/shard_map/ppermute | solution.py:390
  68.8 13.7 %collective-permute-start.12 = (bf16[4,256,128]{2,1,0:T(8,128)(2,1)S(1)}, bf16[4,256,128]{2,1,0:T(8,128)(2,1)S(1)}, u32[]{:S(2)}, u32[]{:S(2)}) collective-permute-start(bf16[4,256,128]{2,1,0:T(8,128)(2,1)S(1)} %get-tuple-element.118), channel_id=1, source_target_pairs={{0,2},{1,3},{2,0},{3,1},{4,6},{5,7},{6,4},{7,5},{8,10},{9,11},{10,... | collective-permute-start | bytes 786440 | tf_op jit(solution)/shard_map/ppermute | solution.py:390
  70.1 13.9 %collective-permute-start.13 = (bf16[4,256,128]{2,1,0:T(8,128)(2,1)S(1)}, bf16[4,256,128]{2,1,0:T(8,128)(2,1)S(1)}, u32[]{:S(2)}, u32[]{:S(2)}) collective-permute-start(bf16[4,256,128]{2,1,0:T(8,128)(2,1)S(1)} %get-tuple-element.119), channel_id=1, source_target_pairs={{0,3},{1,2},{2,1},{3,0},{4,7},{5,6},{6,5},{7,4},{8,11},{9,10},{10,... | collective-permute-start | bytes 786440 | tf_op jit(solution)/shard_map/ppermute | solution.py:390
  81.8 17.0 %collective-permute-start.17 = (bf16[4,256,128]{2,1,0:T(8,128)(2,1)S(1)}, bf16[4,256,128]{2,1,0:T(8,128)(2,1)S(1)}, u32[]{:S(2)}, u32[]{:S(2)}) collective-permute-start(bf16[4,256,128]{2,1,0:T(8,128)(2,1)S(1)} %get-tuple-element.128), channel_id=1, source_target_pairs={{0,1},{1,0},{2,3},{3,2},{4,5},{5,4},{6,7},{7,6},{8,9},{9,8},{10,11... | collective-permute-start | bytes 786440 | tf_op jit(solution)/shard_map/ppermute | solution.py:390
  82.4 17.0 %collective-permute-start.18 = (bf16[4,256,128]{2,1,0:T(8,128)(2,1)S(1)}, bf16[4,256,128]{2,1,0:T(8,128)(2,1)S(1)}, u32[]{:S(2)}, u32[]{:S(2)}) collective-permute-start(bf16[4,256,128]{2,1,0:T(8,128)(2,1)S(1)} %get-tuple-element.129), channel_id=1, source_target_pairs={{0,2},{1,3},{2,0},{3,1},{4,6},{5,7},{6,4},{7,5},{8,10},{9,11},{10,... | collective-permute-start | bytes 786440 | tf_op jit(solution)/shard_map/ppermute | solution.py:390
  83.9 17.0 %collective-permute-start.19 = (bf16[4,256,128]{2,1,0:T(8,128)(2,1)S(1)}, bf16[4,256,128]{2,1,0:T(8,128)(2,1)S(1)}, u32[]{:S(2)}, u32[]{:S(2)}) collective-permute-start(bf16[4,256,128]{2,1,0:T(8,128)(2,1)S(1)} %get-tuple-element.130), channel_id=1, source_target_pairs={{0,3},{1,2},{2,1},{3,0},{4,7},{5,6},{6,5},{7,4},{8,11},{9,10},{10,... | collective-permute-start | bytes 786440 | tf_op jit(solution)/shard_map/ppermute | solution.py:390
  87.5 24.7 %collective-permute-start.20 = (bf16[4,4,256,128]{3,2,1,0:T(8,128)(2,1)S(1)}, bf16[4,4,256,128]{3,2,1,0:T(8,128)(2,1)S(1)}, u32[]{:S(2)}, u32[]{:S(2)}) collective-permute-start(bf16[4,4,256,128]{3,2,1,0:T(8,128)(2,1)S(1)} %collective-permute-done.6.refs_8_.refs_0_), channel_id=1, source_target_pairs={{8,16},{12,20},{16,24},{20,28},{9,17},{13,21},{17,25},{21,29},{10,... | collective-permute-start | bytes 3145736 | tf_op jit(solution)/shard_map/ppermute | solution.py:413
  88.3 24.0 %collective-permute-start.21 = (bf16[4,4,256,128]{3,2,1,0:T(8,128)(2,1)S(1)}, bf16[4,4,256,128]{3,2,1,0:T(8,128)(2,1)S(1)}, u32[]{:S(2)}, u32[]{:S(2)}) collective-permute-start(bf16[4,4,256,128]{3,2,1,0:T(8,128)(2,1)S(1)} %collective-permute-done.7.refs_9_.refs_1_.refs_2_), channel_id=1, source_target_pairs={{8,0},{12,4},{16,8},{20,12},{9,1},{13,5},{17,9},{21,13},{10,2},{14... | collective-permute-start | bytes 3145736 | tf_op jit(solution)/shard_map/ppermute | solution.py:413
  98.8 8.0 %collective-permute-start.14 = (bf16[4,256,128]{2,1,0:T(8,128)(2,1)S(1)}, bf16[4,256,128]{2,1,0:T(8,128)(2,1)S(1)}, u32[]{:S(2)}, u32[]{:S(2)}) collective-permute-start(bf16[4,256,128]{2,1,0:T(8,128)(2,1)S(1)} %get-tuple-element.124), channel_id=1, source_target_pairs={{0,1},{1,0},{2,3},{3,2},{4,5},{5,4},{6,7},{7,6},{8,9},{9,8},{10,11... | collective-permute-start | bytes 786440 | tf_op jit(solution)/shard_map/ppermute | solution.py:390
  100.9 11.3 %collective-permute-start.16 = (bf16[4,256,128]{2,1,0:T(8,128)(2,1)S(1)}, bf16[4,256,128]{2,1,0:T(8,128)(2,1)S(1)}, u32[]{:S(2)}, u32[]{:S(2)}) collective-permute-start(bf16[4,256,128]{2,1,0:T(8,128)(2,1)S(1)} %get-tuple-element.126), channel_id=1, source_target_pairs={{0,3},{1,2},{2,1},{3,0},{4,7},{5,6},{6,5},{7,4},{8,11},{9,10},{10,... | collective-permute-start | bytes 786440 | tf_op jit(solution)/shard_map/ppermute | solution.py:390
  116.1 27.0 %collective-permute-start.25 = (bf16[4,4,256,128]{3,2,1,0:T(8,128)(2,1)S(1)}, bf16[4,4,256,128]{3,2,1,0:T(8,128)(2,1)S(1)}, u32[]{:S(2)}, u32[]{:S(2)}) collective-permute-start(bf16[4,4,256,128]{3,2,1,0:T(8,128)(2,1)S(1)} %collective-permute-done.20.refs_6_.refs_0_), channel_id=1, source_target_pairs={{16,24},{20,28},{17,25},{21,29},{18,26},{22,30},{19,27},{23,31}} | collective-permute-start | bytes 3145736 | tf_op jit(solution)/shard_map/ppermute | solution.py:413
  116.8 27.5 %collective-permute-start.26 = (bf16[4,4,256,128]{3,2,1,0:T(8,128)(2,1)S(1)}, bf16[4,4,256,128]{3,2,1,0:T(8,128)(2,1)S(1)}, u32[]{:S(2)}, u32[]{:S(2)}) collective-permute-start(bf16[4,4,256,128]{3,2,1,0:T(8,128)(2,1)S(1)} %collective-permute-done.21.refs_7_.refs_1_), channel_id=1, source_target_pairs={{8,0},{12,4},{9,1},{13,5},{10,2},{14,6},{11,3},{15,7}} | collective-permute-start | bytes 3145736 | tf_op jit(solution)/shard_map/ppermute | solution.py:413
  118.1 38.6 %collective-permute-start.29 = (bf16[128,48,128]{2,1,0:T(8,128)(2,1)S(1)}, bf16[128,48,128]{2,1,0:T(8,128)(2,1)S(1)}, u32[]{:S(2)}, u32[]{:S(2)}) collective-permute-start(bf16[128,48,128]{2,1,0:T(8,128)(2,1)S(1)} %get-tuple-element.147.refs_0_.refs_1_.refs_6_), channel_id=1, source_target_pairs={{0,4},{4,0},{8,12},{12,8},{16,20},{20,16},{24,28},{28,24},{1,5},{5... | collective-permute-start | bytes 4718600 | tf_op jit(solution)/shard_map/ppermute | solution.py:423
  118.2 14.3 %collective-permute-start.23 = (bf16[4,256,128]{2,1,0:T(8,128)(2,1)S(1)}, bf16[4,256,128]{2,1,0:T(8,128)(2,1)S(1)}, u32[]{:S(2)}, u32[]{:S(2)}) collective-permute-start(bf16[4,256,128]{2,1,0:T(8,128)(2,1)S(1)} %get-tuple-element.140), channel_id=1, source_target_pairs={{0,2},{1,3},{2,0},{3,1},{4,6},{5,7},{6,4},{7,5},{8,10},{9,11},{10,... | collective-permute-start | bytes 786440 | tf_op jit(solution)/shard_map/ppermute | solution.py:390
  122.3 10.2 %collective-permute-start.24 = (bf16[4,256,128]{2,1,0:T(8,128)(2,1)S(1)}, bf16[4,256,128]{2,1,0:T(8,128)(2,1)S(1)}, u32[]{:S(2)}, u32[]{:S(2)}) collective-permute-start(bf16[4,256,128]{2,1,0:T(8,128)(2,1)S(1)} %get-tuple-element.141), channel_id=1, source_target_pairs={{0,3},{1,2},{2,1},{3,0},{4,7},{5,6},{6,5},{7,4},{8,11},{9,10},{10,... | collective-permute-start | bytes 786440 | tf_op jit(solution)/shard_map/ppermute | solution.py:390
  134.6 16.5 %collective-permute-start.27 = (bf16[256,16,128]{2,1,0:T(8,128)(2,1)S(1)}, bf16[256,16,128]{2,1,0:T(8,128)(2,1)S(1)}, u32[]{:S(2)}, u32[]{:S(2)}) collective-permute-start(bf16[256,16,128]{2,1,0:T(8,128)(2,1)S(1)} %get-tuple-element.143.refs_0_.refs_4_), channel_id=1, source_target_pairs={{0,4},{4,0},{8,12},{12,8},{16,20},{20,16},{24,28},{28,24},{1,5},{5... | collective-permute-start | bytes 3145736 | tf_op jit(solution)/shard_map/ppermute | solution.py:423
  134.7 43.9 %collective-permute-start.38 = (bf16[128,48,128]{2,1,0:T(8,128)(2,1)S(1)}, bf16[128,48,128]{2,1,0:T(8,128)(2,1)}, u32[]{:S(2)}, u32[]{:S(2)}) collective-permute-start(bf16[128,48,128]{2,1,0:T(8,128)(2,1)S(1)} %get-tuple-element.147.refs_0_.refs_1_.refs_6_), channel_id=1, source_target_pairs={{0,8},{4,12},{8,16},{12,20},{16,24},{20,28},{1,9},{5,13},{9,17},{1... | collective-permute-start | bytes 4718600 | tf_op jit(solution)/shard_map/ppermute | solution.py:413
  143.0 39.2 %collective-permute-start.40 = (bf16[128,48,128]{2,1,0:T(8,128)(2,1)S(1)}, bf16[128,48,128]{2,1,0:T(8,128)(2,1)}, u32[]{:S(2)}, u32[]{:S(2)}) collective-permute-start(bf16[128,48,128]{2,1,0:T(8,128)(2,1)S(1)} %get-tuple-element.147.refs_0_.refs_1_.refs_6_), channel_id=1, source_target_pairs={{8,0},{12,4},{16,8},{20,12},{24,16},{28,20},{9,1},{13,5},{17,9},{2... | collective-permute-start | bytes 4718600 | tf_op jit(solution)/shard_map/ppermute | solution.py:413
  144.3 23.3 %collective-permute-start.28 = (bf16[128,48,128]{2,1,0:T(8,128)(2,1)S(1)}, bf16[128,48,128]{2,1,0:T(8,128)(2,1)}, u32[]{:S(2)}, u32[]{:S(2)}) collective-permute-start(bf16[128,48,128]{2,1,0:T(8,128)(2,1)S(1)} %copy-done.1), channel_id=1, source_target_pairs={{0,4},{4,0},{8,12},{12,8},{16,20},{20,16},{24,28},{28,24},{1,5},{5... | collective-permute-start | bytes 4718600 | tf_op jit(solution)/shard_map/ppermute | solution.py:423
  151.1 58.7 %collective-permute-start.34 = (bf16[128,48,128]{2,1,0:T(8,128)(2,1)S(1)}, bf16[128,48,128]{2,1,0:T(8,128)(2,1)}, u32[]{:S(2)}, u32[]{:S(2)}) collective-permute-start(bf16[128,48,128]{2,1,0:T(8,128)(2,1)S(1)} %copy-done.1), channel_id=1, source_target_pairs={{0,8},{4,12},{8,16},{12,20},{16,24},{20,28},{1,9},{5,13},{9,17},{1... | collective-permute-start | bytes 4718600 | tf_op jit(solution)/shard_map/ppermute | solution.py:413
  156.6 58.6 %collective-permute-start.36 = (bf16[128,48,128]{2,1,0:T(8,128)(2,1)S(1)}, bf16[128,48,128]{2,1,0:T(8,128)(2,1)}, u32[]{:S(2)}, u32[]{:S(2)}) collective-permute-start(bf16[128,48,128]{2,1,0:T(8,128)(2,1)S(1)} %copy-done.1), channel_id=1, source_target_pairs={{8,0},{12,4},{16,8},{20,12},{24,16},{28,20},{9,1},{13,5},{17,9},{2... | collective-permute-start | bytes 4718600 | tf_op jit(solution)/shard_map/ppermute | solution.py:413
  178.1 8.5 %collective-permute-start.30 = (bf16[4,256,128]{2,1,0:T(8,128)(2,1)S(1)}, bf16[4,256,128]{2,1,0:T(8,128)(2,1)S(1)}, u32[]{:S(2)}, u32[]{:S(2)}) collective-permute-start(bf16[4,256,128]{2,1,0:T(8,128)(2,1)S(1)} %get-tuple-element.157), channel_id=1, source_target_pairs={{0,1},{1,0},{2,3},{3,2},{4,5},{5,4},{6,7},{7,6},{8,9},{9,8},{10,11... | collective-permute-start | bytes 786440 | tf_op jit(solution)/shard_map/ppermute | solution.py:390
  178.6 8.2 %collective-permute-start.31 = (bf16[4,256,128]{2,1,0:T(8,128)(2,1)S(1)}, bf16[4,256,128]{2,1,0:T(8,128)(2,1)S(1)}, u32[]{:S(2)}, u32[]{:S(2)}) collective-permute-start(bf16[4,256,128]{2,1,0:T(8,128)(2,1)S(1)} %get-tuple-element.158), channel_id=1, source_target_pairs={{0,2},{1,3},{2,0},{3,1},{4,6},{5,7},{6,4},{7,5},{8,10},{9,11},{10,... | collective-permute-start | bytes 786440 | tf_op jit(solution)/shard_map/ppermute | solution.py:390
  182.3 34.8 %collective-permute-start.39 = (bf16[128,48,128]{2,1,0:T(8,128)(2,1)}, bf16[128,48,128]{2,1,0:T(8,128)(2,1)}, u32[]{:S(2)}, u32[]{:S(2)}) collective-permute-start(bf16[128,48,128]{2,1,0:T(8,128)(2,1)} %collective-permute-done.38.refs_6_), channel_id=1, source_target_pairs={{0,4},{4,0},{8,12},{12,8},{16,20},{20,16},{24,28},{28,24},{1,5},{5... | collective-permute-start | bytes 4718600 | tf_op jit(solution)/shard_map/ppermute | solution.py:423
  186.6 31.8 %collective-permute-start.41 = (bf16[128,48,128]{2,1,0:T(8,128)(2,1)}, bf16[128,48,128]{2,1,0:T(8,128)(2,1)}, u32[]{:S(2)}, u32[]{:S(2)}) collective-permute-start(bf16[128,48,128]{2,1,0:T(8,128)(2,1)} %collective-permute-done.40.refs_8_.refs_10_), channel_id=1, source_target_pairs={{0,4},{4,0},{8,12},{12,8},{16,20},{20,16},{24,28},{28,24},{1,5},{5... | collective-permute-start | bytes 4718600 | tf_op jit(solution)/shard_map/ppermute | solution.py:423
  186.7 9.5 %collective-permute-start.32 = (bf16[4,256,128]{2,1,0:T(8,128)(2,1)S(1)}, bf16[4,256,128]{2,1,0:T(8,128)(2,1)S(1)}, u32[]{:S(2)}, u32[]{:S(2)}) collective-permute-start(bf16[4,256,128]{2,1,0:T(8,128)(2,1)S(1)} %get-tuple-element.159), channel_id=1, source_target_pairs={{0,3},{1,2},{2,1},{3,0},{4,7},{5,6},{6,5},{7,4},{8,11},{9,10},{10,... | collective-permute-start | bytes 786440 | tf_op jit(solution)/shard_map/ppermute | solution.py:390
  198.3 17.0 %collective-permute-start.33 = (bf16[256,16,128]{2,1,0:T(8,128)(2,1)S(1)}, bf16[256,16,128]{2,1,0:T(8,128)(2,1)S(1)}, u32[]{:S(2)}, u32[]{:S(2)}) collective-permute-start(bf16[256,16,128]{2,1,0:T(8,128)(2,1)S(1)} %get-tuple-element.161.refs_4_), channel_id=1, source_target_pairs={{0,4},{4,0},{8,12},{12,8},{16,20},{20,16},{24,28},{28,24},{1,5},{5... | collective-permute-start | bytes 3145736 | tf_op jit(solution)/shard_map/ppermute | solution.py:423
  209.8 20.7 %collective-permute-start.35 = (bf16[128,48,128]{2,1,0:T(8,128)(2,1)}, bf16[128,48,128]{2,1,0:T(8,128)(2,1)}, u32[]{:S(2)}, u32[]{:S(2)}) collective-permute-start(bf16[128,48,128]{2,1,0:T(8,128)(2,1)} %collective-permute-done.34.refs_6_), channel_id=1, source_target_pairs={{0,4},{4,0},{8,12},{12,8},{16,20},{20,16},{24,28},{28,24},{1,5},{5... | collective-permute-start | bytes 4718600 | tf_op jit(solution)/shard_map/ppermute | solution.py:423
  215.2 16.7 %collective-permute-start.37 = (bf16[128,48,128]{2,1,0:T(8,128)(2,1)}, bf16[128,48,128]{2,1,0:T(8,128)(2,1)}, u32[]{:S(2)}, u32[]{:S(2)}) collective-permute-start(bf16[128,48,128]{2,1,0:T(8,128)(2,1)} %collective-permute-done.36.refs_8_.refs_10_), channel_id=1, source_target_pairs={{0,4},{4,0},{8,12},{12,8},{16,20},{20,16},{24,28},{28,24},{1,5},{5... | collective-permute-start | bytes 4718600 | tf_op jit(solution)/shard_map/ppermute | solution.py:423
  215.2 28.5 %collective-permute-start.50 = (bf16[128,48,128]{2,1,0:T(8,128)(2,1)}, bf16[128,48,128]{2,1,0:T(8,128)(2,1)}, u32[]{:S(2)}, u32[]{:S(2)}) collective-permute-start(bf16[128,48,128]{2,1,0:T(8,128)(2,1)} %collective-permute-done.38.refs_6_), channel_id=1, source_target_pairs={{8,16},{12,20},{16,24},{20,28},{9,17},{13,21},{17,25},{21,29},{10,... | collective-permute-start | bytes 4718600 | tf_op jit(solution)/shard_map/ppermute | solution.py:413
  217.0 39.4 %collective-permute-start.52 = (bf16[128,48,128]{2,1,0:T(8,128)(2,1)}, bf16[128,48,128]{2,1,0:T(8,128)(2,1)}, u32[]{:S(2)}, u32[]{:S(2)}) collective-permute-start(bf16[128,48,128]{2,1,0:T(8,128)(2,1)} %collective-permute-done.40.refs_8_.refs_10_), channel_id=1, source_target_pairs={{8,0},{12,4},{16,8},{20,12},{9,1},{13,5},{17,9},{21,13},{10,2},{14... | collective-permute-start | bytes 4718600 | tf_op jit(solution)/shard_map/ppermute | solution.py:413
  218.3 49.9 %collective-permute-start.46 = (bf16[128,48,128]{2,1,0:T(8,128)(2,1)}, bf16[128,48,128]{2,1,0:T(8,128)(2,1)}, u32[]{:S(2)}, u32[]{:S(2)}) collective-permute-start(bf16[128,48,128]{2,1,0:T(8,128)(2,1)} %collective-permute-done.34.refs_6_), channel_id=1, source_target_pairs={{8,16},{12,20},{16,24},{20,28},{9,17},{13,21},{17,25},{21,29},{10,... | collective-permute-start | bytes 4718600 | tf_op jit(solution)/shard_map/ppermute | solution.py:413
  230.5 59.2 %collective-permute-start.48 = (bf16[128,48,128]{2,1,0:T(8,128)(2,1)}, bf16[128,48,128]{2,1,0:T(8,128)(2,1)}, u32[]{:S(2)}, u32[]{:S(2)}) collective-permute-start(bf16[128,48,128]{2,1,0:T(8,128)(2,1)} %collective-permute-done.36.refs_8_.refs_10_), channel_id=1, source_target_pairs={{8,0},{12,4},{16,8},{20,12},{9,1},{13,5},{17,9},{21,13},{10,2},{14... | collective-permute-start | bytes 4718600 | tf_op jit(solution)/shard_map/ppermute | solution.py:413
  243.2 13.2 %collective-permute-start.42 = (bf16[4,256,128]{2,1,0:T(8,128)(2,1)S(1)}, bf16[4,256,128]{2,1,0:T(8,128)(2,1)S(1)}, u32[]{:S(2)}, u32[]{:S(2)}) collective-permute-start(bf16[4,256,128]{2,1,0:T(8,128)(2,1)S(1)} %get-tuple-element.168), channel_id=1, source_target_pairs={{0,1},{1,0},{2,3},{3,2},{4,5},{5,4},{6,7},{7,6},{8,9},{9,8},{10,11... | collective-permute-start | bytes 786440 | tf_op jit(solution)/shard_map/ppermute | solution.py:390
  243.7 13.2 %collective-permute-start.43 = (bf16[4,256,128]{2,1,0:T(8,128)(2,1)S(1)}, bf16[4,256,128]{2,1,0:T(8,128)(2,1)S(1)}, u32[]{:S(2)}, u32[]{:S(2)}) collective-permute-start(bf16[4,256,128]{2,1,0:T(8,128)(2,1)S(1)} %get-tuple-element.169), channel_id=1, source_target_pairs={{0,2},{1,3},{2,0},{3,1},{4,6},{5,7},{6,4},{7,5},{8,10},{9,11},{10,... | collective-permute-start | bytes 786440 | tf_op jit(solution)/shard_map/ppermute | solution.py:390
  256.4 35.2 %collective-permute-start.51 = (bf16[128,48,128]{2,1,0:T(8,128)(2,1)}, bf16[128,48,128]{2,1,0:T(8,128)(2,1)S(1)}, u32[]{:S(2)}, u32[]{:S(2)}) collective-permute-start(bf16[128,48,128]{2,1,0:T(8,128)(2,1)} %collective-permute-done.50.refs_6_), channel_id=1, source_target_pairs={{0,4},{4,0},{8,12},{12,8},{16,20},{20,16},{24,28},{28,24},{1,5},{5... | collective-permute-start | bytes 4718600 | tf_op jit(solution)/shard_map/ppermute | solution.py:423
  256.4 36.5 %collective-permute-start.53 = (bf16[128,48,128]{2,1,0:T(8,128)(2,1)}, bf16[128,48,128]{2,1,0:T(8,128)(2,1)}, u32[]{:S(2)}, u32[]{:S(2)}) collective-permute-start(bf16[128,48,128]{2,1,0:T(8,128)(2,1)} %collective-permute-done.52.refs_8_), channel_id=1, source_target_pairs={{0,4},{4,0},{8,12},{12,8},{16,20},{20,16},{24,28},{28,24},{1,5},{5... | collective-permute-start | bytes 4718600 | tf_op jit(solution)/shard_map/ppermute | solution.py:423
  256.9 9.2 %collective-permute-start.44 = (bf16[4,256,128]{2,1,0:T(8,128)(2,1)S(1)}, bf16[4,256,128]{2,1,0:T(8,128)(2,1)S(1)}, u32[]{:S(2)}, u32[]{:S(2)}) collective-permute-start(bf16[4,256,128]{2,1,0:T(8,128)(2,1)S(1)} %get-tuple-element.170), channel_id=1, source_target_pairs={{0,3},{1,2},{2,1},{3,0},{4,7},{5,6},{6,5},{7,4},{8,11},{9,10},{10,... | collective-permute-start | bytes 786440 | tf_op jit(solution)/shard_map/ppermute | solution.py:390
  268.2 21.6 %collective-permute-start.45 = (bf16[256,16,128]{2,1,0:T(8,128)(2,1)S(1)}, bf16[256,16,128]{2,1,0:T(8,128)(2,1)S(1)}, u32[]{:S(2)}, u32[]{:S(2)}) collective-permute-start(bf16[256,16,128]{2,1,0:T(8,128)(2,1)S(1)} %get-tuple-element.172.refs_4_), channel_id=1, source_target_pairs={{0,4},{4,0},{8,12},{12,8},{16,20},{20,16},{24,28},{28,24},{1,5},{5... | collective-permute-start | bytes 3145736 | tf_op jit(solution)/shard_map/ppermute | solution.py:423
  268.3 35.8 %collective-permute-start.47 = (bf16[128,48,128]{2,1,0:T(8,128)(2,1)}, bf16[128,48,128]{2,1,0:T(8,128)(2,1)}, u32[]{:S(2)}, u32[]{:S(2)}) collective-permute-start(bf16[128,48,128]{2,1,0:T(8,128)(2,1)} %collective-permute-done.46.refs_6_), channel_id=1, source_target_pairs={{0,4},{4,0},{8,12},{12,8},{16,20},{20,16},{24,28},{28,24},{1,5},{5... | collective-permute-start | bytes 4718600 | tf_op jit(solution)/shard_map/ppermute | solution.py:423
  289.8 15.6 %collective-permute-start.49 = (bf16[128,48,128]{2,1,0:T(8,128)(2,1)}, bf16[128,48,128]{2,1,0:T(8,128)(2,1)}, u32[]{:S(2)}, u32[]{:S(2)}) collective-permute-start(bf16[128,48,128]{2,1,0:T(8,128)(2,1)} %collective-permute-done.48.refs_8_), channel_id=1, source_target_pairs={{0,4},{4,0},{8,12},{12,8},{16,20},{20,16},{24,28},{28,24},{1,5},{5... | collective-permute-start | bytes 4718600 | tf_op jit(solution)/shard_map/ppermute | solution.py:423
  289.8 28.5 %collective-permute-start.62 = (bf16[128,48,128]{2,1,0:T(8,128)(2,1)}, bf16[128,48,128]{2,1,0:T(8,128)(2,1)}, u32[]{:S(2)}, u32[]{:S(2)}) collective-permute-start(bf16[128,48,128]{2,1,0:T(8,128)(2,1)} %collective-permute-done.50.refs_6_), channel_id=1, source_target_pairs={{16,24},{20,28},{17,25},{21,29},{18,26},{22,30},{19,27},{23,31}} | collective-permute-start | bytes 4718600 | tf_op jit(solution)/shard_map/ppermute | solution.py:413
  291.6 39.4 %collective-permute-start.64 = (bf16[128,48,128]{2,1,0:T(8,128)(2,1)}, bf16[128,48,128]{2,1,0:T(8,128)(2,1)}, u32[]{:S(2)}, u32[]{:S(2)}) collective-permute-start(bf16[128,48,128]{2,1,0:T(8,128)(2,1)} %collective-permute-done.52.refs_8_), channel_id=1, source_target_pairs={{8,0},{12,4},{9,1},{13,5},{10,2},{14,6},{11,3},{15,7}} | collective-permute-start | bytes 4718600 | tf_op jit(solution)/shard_map/ppermute | solution.py:413
  292.9 49.9 %collective-permute-start.58 = (bf16[128,48,128]{2,1,0:T(8,128)(2,1)}, bf16[128,48,128]{2,1,0:T(8,128)(2,1)S(1)}, u32[]{:S(2)}, u32[]{:S(2)}) collective-permute-start(bf16[128,48,128]{2,1,0:T(8,128)(2,1)} %collective-permute-done.46.refs_6_), channel_id=1, source_target_pairs={{16,24},{20,28},{17,25},{21,29},{18,26},{22,30},{19,27},{23,31}} | collective-permute-start | bytes 4718600 | tf_op jit(solution)/shard_map/ppermute | solution.py:413
  304.0 60.3 %collective-permute-start.60 = (bf16[128,48,128]{2,1,0:T(8,128)(2,1)}, bf16[128,48,128]{2,1,0:T(8,128)(2,1)}, u32[]{:S(2)}, u32[]{:S(2)}) collective-permute-start(bf16[128,48,128]{2,1,0:T(8,128)(2,1)} %collective-permute-done.48.refs_8_), channel_id=1, source_target_pairs={{8,0},{12,4},{9,1},{13,5},{10,2},{14,6},{11,3},{15,7}} | collective-permute-start | bytes 4718600 | tf_op jit(solution)/shard_map/ppermute | solution.py:413
  316.6 14.4 %collective-permute-start.54 = (bf16[4,256,128]{2,1,0:T(8,128)(2,1)S(1)}, bf16[4,256,128]{2,1,0:T(8,128)(2,1)S(1)}, u32[]{:S(2)}, u32[]{:S(2)}) collective-permute-start(bf16[4,256,128]{2,1,0:T(8,128)(2,1)S(1)} %get-tuple-element.179), channel_id=1, source_target_pairs={{0,1},{1,0},{2,3},{3,2},{4,5},{5,4},{6,7},{7,6},{8,9},{9,8},{10,11... | collective-permute-start | bytes 786440 | tf_op jit(solution)/shard_map/ppermute | solution.py:390
  318.3 13.2 %collective-permute-start.55 = (bf16[4,256,128]{2,1,0:T(8,128)(2,1)S(1)}, bf16[4,256,128]{2,1,0:T(8,128)(2,1)S(1)}, u32[]{:S(2)}, u32[]{:S(2)}) collective-permute-start(bf16[4,256,128]{2,1,0:T(8,128)(2,1)S(1)} %get-tuple-element.180), channel_id=1, source_target_pairs={{0,2},{1,3},{2,0},{3,1},{4,6},{5,7},{6,4},{7,5},{8,10},{9,11},{10,... | collective-permute-start | bytes 786440 | tf_op jit(solution)/shard_map/ppermute | solution.py:390
  331.0 33.3 %collective-permute-start.63 = (bf16[128,48,128]{2,1,0:T(8,128)(2,1)}, bf16[128,48,128]{2,1,0:T(8,128)(2,1)S(1)}, u32[]{:S(2)}, u32[]{:S(2)}) collective-permute-start(bf16[128,48,128]{2,1,0:T(8,128)(2,1)} %collective-permute-done.62.refs_6_), channel_id=1, source_target_pairs={{0,4},{4,0},{8,12},{12,8},{16,20},{20,16},{24,28},{28,24},{1,5},{5... | collective-permute-start | bytes 4718600 | tf_op jit(solution)/shard_map/ppermute | solution.py:423
  331.0 33.3 %collective-permute-start.65 = (bf16[128,48,128]{2,1,0:T(8,128)(2,1)}, bf16[128,48,128]{2,1,0:T(8,128)(2,1)S(1)}, u32[]{:S(2)}, u32[]{:S(2)}) collective-permute-start(bf16[128,48,128]{2,1,0:T(8,128)(2,1)} %collective-permute-done.64.refs_8_), channel_id=1, source_target_pairs={{0,4},{4,0},{8,12},{12,8},{16,20},{20,16},{24,28},{28,24},{1,5},{5... | collective-permute-start | bytes 4718600 | tf_op jit(solution)/shard_map/ppermute | solution.py:423
  331.5 9.2 %collective-permute-start.56 = (bf16[4,256,128]{2,1,0:T(8,128)(2,1)S(1)}, bf16[4,256,128]{2,1,0:T(8,128)(2,1)S(1)}, u32[]{:S(2)}, u32[]{:S(2)}) collective-permute-start(bf16[4,256,128]{2,1,0:T(8,128)(2,1)S(1)} %get-tuple-element.181), channel_id=1, source_target_pairs={{0,3},{1,2},{2,1},{3,0},{4,7},{5,6},{6,5},{7,4},{8,11},{9,10},{10,... | collective-permute-start | bytes 786440 | tf_op jit(solution)/shard_map/ppermute | solution.py:390
  342.7 21.6 %collective-permute-start.57 = (bf16[256,16,128]{2,1,0:T(8,128)(2,1)S(1)}, bf16[256,16,128]{2,1,0:T(8,128)(2,1)S(1)}, u32[]{:S(2)}, u32[]{:S(2)}) collective-permute-start(bf16[256,16,128]{2,1,0:T(8,128)(2,1)S(1)} %get-tuple-element.183.refs_4_), channel_id=1, source_target_pairs={{0,4},{4,0},{8,12},{12,8},{16,20},{20,16},{24,28},{28,24},{1,5},{5... | collective-permute-start | bytes 3145736 | tf_op jit(solution)/shard_map/ppermute | solution.py:423
  342.8 33.5 %collective-permute-start.59 = (bf16[128,48,128]{2,1,0:T(8,128)(2,1)S(1)}, bf16[128,48,128]{2,1,0:T(8,128)(2,1)}, u32[]{:S(2)}, u32[]{:S(2)}) collective-permute-start(bf16[128,48,128]{2,1,0:T(8,128)(2,1)S(1)} %collective-permute-done.58.refs_6_), channel_id=1, source_target_pairs={{0,4},{4,0},{8,12},{12,8},{16,20},{20,16},{24,28},{28,24},{1,5},{5... | collective-permute-start | bytes 4718600 | tf_op jit(solution)/shard_map/ppermute | solution.py:423
  364.3 12.1 %collective-permute-start.61 = (bf16[128,48,128]{2,1,0:T(8,128)(2,1)}, bf16[128,48,128]{2,1,0:T(8,128)(2,1)}, u32[]{:S(2)}, u32[]{:S(2)}) collective-permute-start(bf16[128,48,128]{2,1,0:T(8,128)(2,1)} %collective-permute-done.60.refs_8_), channel_id=1, source_target_pairs={{0,4},{4,0},{8,12},{12,8},{16,20},{20,16},{24,28},{28,24},{1,5},{5... | collective-permute-start | bytes 4718600 | tf_op jit(solution)/shard_map/ppermute | solution.py:423
  (18 other events, 162.8 us)

commit v2 on v1

--- a/solution.py
+++ b/solution.py
@@ -14,6 +14,8 @@
 ROWS = 16
 VMEM = 48 * 1024 * 1024
 FLOPS_A_MICROSECOND = 1.15e9
+CORRELATE_MICROS = 7.0
+HOP_MICROS = 40.0
 filter_norm = 1.0 / 16384.0
 
 
@@ -142,12 +144,18 @@
 
     def kernel(place, ins, outs, scratch):
         taps_ref, hist_ref, *refs = ins
-        blocks, (cos_ref, sin_ref) = refs[:parts], refs[parts:]
-        extended, filtered = scratch
-        me, step = place[0], pl.program_id(0)
-
-        @pl.when(step == 0)
-        def _():
+        blocks, table_ref = refs[:parts], refs[parts]
+        extended, filtered, rows_of, arrived = scratch
+        me = place[0]
+        copies = []
+        for slot in range(parts):
+            for part in range(2):
+                first = pl.multiple_of((part * parts + (me ^ slot)) * channels, channels)
+                source, target = table_ref.at[pl.ds(first, channels), :], rows_of.at[slot, part]
+                copies.append(pltpu.make_async_copy(source, target, arrived.at[slot, part]))
+                copies[-1].start()
+
+        def fill():
             def block(nb, carry):
                 lane = pl.multiple_of(nb * LANES, LANES)
                 columns = pl.ds(lane, LANES)
@@ -166,33 +174,32 @@
 
             lax.fori_loop(0, fft // LANES, block, 0)
 
+        fill()
         dims = (((1,), (1,)), ((), ()))
         block = filtered[...]
-        real = lax.dot_general(cos_ref[...], block, dims, preferred_element_type=jnp.float32)
-        imag = lax.dot_general(sin_ref[...], block, dims, preferred_element_type=jnp.float32)
-        results = []
-        if 2 * total == LANES and each % 2 == 0:
-            low = lax.broadcasted_iota(jnp.int32, (real.shape[0], LANES), 1) < total
-            for pair in range(each // 2):
-                r = real[:, pair * LANES : (pair + 1) * LANES]
-                m = imag[:, pair * LANES : (pair + 1) * LANES]
-                results.append(jnp.where(low, r, pltpu.roll(m, total, 1)))
-                results.append(jnp.where(low, pltpu.roll(r, total, 1), m))
-        else:
+        low = lax.broadcasted_iota(jnp.int32, (channels, LANES), 1) < total
+        for slot in range(parts):
+            for part in range(2):
+                copies[2 * slot + part].wait()
+            real = lax.dot_general(rows_of[slot, 0], block, dims, preferred_element_type=jnp.float32)
+            imag = lax.dot_general(rows_of[slot, 1], block, dims, preferred_element_type=jnp.float32)
+            results = []
+            if 2 * total == LANES and each % 2 == 0:
+                for pair in range(each // 2):
+                    r = real[:, pair * LANES : (pair + 1) * LANES]
+                    m = imag[:, pair * LANES : (pair + 1) * LANES]
+                    results.append(jnp.where(low, r, pltpu.roll(m, total, 1)))
+                    results.append(jnp.where(low, pltpu.roll(r, total, 1), m))
+            else:
+                for i in range(each):
+                    cut = slice(i * total, (i + 1) * total)
+                    results.append(jnp.concatenate([real[:, cut], imag[:, cut]], axis=1))
             for i in range(each):
-                cut = slice(i * total, (i + 1) * total)
-                results.append(jnp.concatenate([real[:, cut], imag[:, cut]], axis=1))
-        results = [value.astype(jnp.bfloat16) for value in results]
-        if not split:
-            for i in range(each):
-                outs[0][0, i] = results[i]
-            return
-        for slot in range(parts):
-
-            @pl.when(step == slot)
-            def _(slot=slot):
-                for i in range(each):
-                    outs[slot][i] = results[i]
+                value = results[i].astype(jnp.bfloat16)
+                if split:
+                    outs[slot][i] = value
+                else:
+                    outs[0][me ^ slot, i] = value
 
     shape = (each, channels, 2 * total)
     if split:
@@ -200,58 +207,57 @@
         out_specs = [pl.BlockSpec(shape, lambda g, place: (0, 0, 0))] * parts
     else:
         out_shape = [jax.ShapeDtypeStruct((parts, *shape), jnp.bfloat16)]
-        out_specs = [pl.BlockSpec((1, *shape), lambda g, place: (g, 0, 0, 0))]
+        out_specs = [pl.BlockSpec((parts, *shape), lambda g, place: (0, 0, 0, 0))]
     return order.call(
         kernel,
         "channelize",
         place,
-        [filter_taps, hist, *pieces, table, table],
+        [filter_taps, hist, *pieces, table],
         [
             pl.BlockSpec((taps, fft), lambda g, place: (0, 0)),
             pl.BlockSpec((1, each, taps, fft), lambda g, place: (chunk, 0, 0, 0)),
             *[pl.BlockSpec((1, each, spectra, fft), lambda g, place: (inner, 0, 0, 0))] * parts,
-            pl.BlockSpec((channels, fft), lambda g, place: (place[0] ^ g, 0)),
-            pl.BlockSpec((channels, fft), lambda g, place: (parts + (place[0] ^ g), 0)),
+            pl.BlockSpec(memory_space=pl.ANY),
         ],
         out_shape,
         out_specs,
-        (parts,),
-        [pltpu.VMEM((each, taps + total, LANES), jnp.float32), pltpu.VMEM((each * total, fft), jnp.bfloat16)],
+        (1,),
+        [
+            pltpu.VMEM((each, taps + total, LANES), jnp.float32),
+            pltpu.VMEM((each * total, fft), jnp.bfloat16),
+            pltpu.VMEM((parts, 2, channels, fft), jnp.bfloat16),
+            pltpu.SemaphoreType.DMA((parts, 2)),
+        ],
         after=after,
         micros=9.0,
     )
 
 
-def choose(order, place, candidates, after=()):
-    parts, each, channels, width = candidates[0].shape
+def select(order, place, candidates, after=()):
+    channels, rows, width = candidates[0].shape
+    count = channels // 4
 
     def kernel(place, ins, outs, scratch):
         for which, ref in enumerate(ins):
 
-            @pl.when(place[3] == which)
+            @pl.when(place[4] == which)
             def _(ref=ref):
-                for slot in range(parts):
-
-                    @pl.when(pl.program_id(0) == slot)
-                    def _(slot=slot):
-                        outs[slot][...] = ref[0]
+                outs[0][...] = ref[...]
 
     def spec(which):
-        return pl.BlockSpec(
-            (1, each, channels, width), lambda g, place: (jnp.where(place[3] == which, g, 0), 0, 0, 0)
-        )
+        return pl.BlockSpec((count, rows, width), lambda g, place: (jnp.where(place[4] == which, g, 0), 0, 0))
 
     return order.call(
         kernel,
-        "choose",
+        "select",
         place,
         candidates,
         [spec(which) for which in range(len(candidates))],
-        [jax.ShapeDtypeStruct((each, channels, width), jnp.bfloat16)] * parts,
-        [pl.BlockSpec((each, channels, width), lambda g, place: (0, 0, 0))] * parts,
-        (parts,),
+        [jax.ShapeDtypeStruct((channels, rows, width), jnp.bfloat16)],
+        [pl.BlockSpec((count, rows, width), lambda g, place: (g, 0, 0))],
+        (channels // count,),
         after=after,
-    )
+    )[0]
 
 
 def merge(order, place, pieces, cuts=1, position=0, rows=ROWS, into=(), after=()):
@@ -296,27 +302,82 @@
     )
 
 
+def gate(order, place, values, after=(), micros=0.1):
+    return order.call(
+        lambda place, ins, outs, scratch: None,
+        "gate",
+        place,
+        [],
+        [],
+        [jax.ShapeDtypeStruct(value.shape, value.dtype) for value in values],
+        [pl.BlockSpec(memory_space=pl.ANY)] * len(values),
+        (1,),
+        after=after,
+        aliased=values,
+        micros=micros,
+    )
+
+
+def merge_early(order, place, pieces, after=()):
+    parts, groups, each, channels, width = pieces.shape
+
+    def kernel(place, ins, outs, scratch):
+        (work,) = scratch
+        for source in range(parts):
+            for i in range(each):
+                rows = slice((source * each + i) * channels, (source * each + i + 1) * channels)
+                for lane in range(0, width, LANES):
+                    work[lane // LANES, rows, :] = ins[0][source, 0, i, :, lane : lane + LANES].astype(jnp.float32)
+
+        def block(group, carry):
+            for inner in range(8):
+                k = group * 8 + inner
+                for lane in range(0, width, LANES):
+                    value = work[lane // LANES, pl.ds(k, ROWS, stride=channels), :]
+                    outs[0][0, k, :, lane : lane + LANES] = value.astype(jnp.bfloat16)
+            return carry
+
+        lax.fori_loop(0, channels // 8, block, 0)
+
+    return order.call(
+        kernel,
+        "merge_early",
+        place,
+        [pieces],
+        [pl.BlockSpec((parts, 1, each, channels, width), lambda g, place: (0, g, 0, 0, 0))],
+        [jax.ShapeDtypeStruct((groups, channels, ROWS, width), jnp.bfloat16)],
+        [pl.BlockSpec((1, channels, ROWS, width), lambda g, place: (g, 0, 0, 0))],
+        (groups,),
+        [pltpu.VMEM((width // LANES, ROWS * channels, LANES), jnp.float32)],
+        after=after,
+        micros=HOP_MICROS,
+    )[0]
+
+
 def turn(order, place, plain, after=()):
-    channels, rows, width = plain.shape
+    channels, rows, width = plain.shape[-3:]
+    stacked = plain.ndim == 4
     count = 16
 
     def kernel(place, ins, outs, scratch):
         low = lax.broadcasted_iota(jnp.int32, (rows, width), 1) < width // 2
         for k in range(count):
-            other = pltpu.roll(ins[0][k].astype(jnp.float32), width // 2, 1)
+            value = ins[0][0, k] if stacked else ins[0][k]
+            other = pltpu.roll(value.astype(jnp.float32), width // 2, 1)
             outs[0][k] = jnp.where(low, other, -other).astype(jnp.bfloat16)
 
     block = pl.BlockSpec((count, rows, width), lambda g, place: (g, 0, 0))
-    shape = jax.ShapeDtypeStruct(plain.shape, jnp.bfloat16)
-    return order.call(kernel, "turn", place, [plain], [block], [shape], [block], (channels // count,), after=after, micros=2.0)[0]
-
-
-def correlate(order, place, out, left, sets, cut, cuts, groups, after=()):
-    head, tail = left[0][0], left[0][1]
+    source = pl.BlockSpec((1, count, rows, width), lambda g, place: (place[2], g, 0, 0)) if stacked else block
+    shape = jax.ShapeDtypeStruct((channels, rows, width), jnp.bfloat16)
+    return order.call(kernel, "turn", place, [plain], [source], [shape], [block], (channels // count,), after=after, micros=0.1)[0]
+
+
+def correlate(order, place, out, left, sets, cut, cuts, groups, after=(), micros=CORRELATE_MICROS):
+    head, tail = left[1][0], left[0][1]
     rows_head, rows_tail, width = head.shape[1], tail.shape[1], head.shape[2]
     half = rows_head + rows_tail
     channels = head.shape[0]
-    count = 16
+    count = 32
     steps = channels // cuts // count
     average = 2.0 / width
     sizes = [len(candidates) for _, candidates in sets]
@@ -327,22 +388,23 @@
         for s, size in enumerate(sizes):
             mine, theirs, *options = right[: 2 + 2 * size]
             del right[: 2 + 2 * size]
-            base = place[2 + 2 * s] * (2 * half) if len(sizes) > 1 else 0
+            base = place[3 + 2 * s] * (2 * half) if len(sizes) > 1 else 0
             first = pl.multiple_of(base + core * half, ROWS)
             second = pl.multiple_of(base + (1 - core) * half, ROWS)
             for k in range(count):
-                columns[k, pl.ds(first, rows_head), :] = mine[k]
-                columns[k, pl.ds(second, rows_head), :] = theirs[k]
+                columns[k, pl.ds(first, rows_head), :] = mine[0, k]
+                columns[k, pl.ds(second, rows_head), :] = theirs[0, k]
             for which in range(size):
 
-                @pl.when(place[3 + 2 * s] == which)
+                @pl.when(place[4 + 2 * s] == which)
                 def _(which=which, options=options, first=first, second=second):
                     for k in range(count):
                         columns[k, pl.ds(first + rows_head, rows_tail), :] = options[2 * which][k]
                         columns[k, pl.ds(second + rows_head, rows_tail), :] = options[2 * which + 1][k]
 
         for k in range(count):
-            rows = jnp.concatenate([ref[k] for ref in left_refs], axis=0)
+            rows = [left_refs[0][0, k], *[ref[k] for ref in left_refs[1:]]]
+            rows = jnp.concatenate(rows, axis=0)
             result = lax.dot_general(rows, columns[k], (((1,), (1,)), ((), ())), preferred_element_type=jnp.float32)
             out_ref[0, k] = result[:half] * average
             out_ref[1, k] = result[half:] * average
@@ -351,15 +413,20 @@
         return (cut * steps + g, 0, 0)
 
     def spec(s, which):
-        return pl.BlockSpec((count, rows_tail, width), lambda g, place: (jnp.where(place[3 + 2 * s] == which, g, 0), 0, 0))
+        return pl.BlockSpec((count, rows_tail, width), lambda g, place: (jnp.where(place[4 + 2 * s] == which, g, 0), 0, 0))
+
+    def early_of(s):
+        return pl.BlockSpec(
+            (1, count, rows_head, width), lambda g, place: (place[2 if s is None else 3 + 2 * s], cut * steps + g, 0, 0)
+        )
 
     head_spec = pl.BlockSpec((count, rows_head, width), early)
     tail_spec = pl.BlockSpec((count, rows_tail, width), lambda g, place: (g, 0, 0))
     operands = [left[0][0], left[0][1], left[1][0], left[1][1]]
-    specs = [head_spec, tail_spec, head_spec, tail_spec]
+    specs = [early_of(None), tail_spec, head_spec, tail_spec]
     for s, (heads, candidates) in enumerate(sets):
         operands += heads
-        specs += [head_spec] * 2
+        specs += [early_of(s)] * 2
         for which, pair in enumerate(candidates):
             operands += pair
             specs += [spec(s, which)] * 2
@@ -367,7 +434,7 @@
     if len(sets) > 1:
         out_spec = pl.BlockSpec((2, count, half, lanes), lambda g, place: (0, cut * steps + g, 0, 0))
     else:
-        out_spec = pl.BlockSpec((2, count, half, lanes), lambda g, place: (0, cut * steps + g, 0, place[2]))
+        out_spec = pl.BlockSpec((2, count, half, lanes), lambda g, place: (0, cut * steps + g, 0, place[3]))
     return order.call(
         kernel,
         "correlate",
@@ -380,7 +447,7 @@
         [pltpu.VMEM((count, lanes, width), jnp.bfloat16)],
         after=after,
         aliased=[] if out is None else [out],
-        micros=10.0,
+        micros=micros,
     )[0]
 
 
@@ -406,28 +473,25 @@
     order = Order()
 
     def place(*pairs):
-        return jnp.stack([jnp.asarray(x, jnp.int32) for x in (me, core, *[x for pair in pairs for x in pair])])
+        return jnp.stack([jnp.asarray(x, jnp.int32) for x in (me, core, level, *[x for pair in pairs for x in pair])])
 
     def along(value, lowest, highest, step):
         pairs = [(2 * g + c, 2 * (g + step) + c) for g in range(lowest, highest + 1) for c in range(2)]
         return lax.ppermute(value, "tile", pairs)
 
-    def hops(value):
-        up, down = {0: value}, {0: value}
-        for hop in range(1, groups):
-            up[hop] = along(up[hop - 1], hop - 1, groups - 2, 1)
-            down[hop] = along(down[hop - 1], 1, groups - hop, -1)
-        return up, down
-
     def swap(value):
         return lax.ppermute(value, "tile", [(i, i ^ 1) for i in range(tiles)])
 
-    here = place((level, 0))
+    here = place()
+
+    middle = (groups + 1) // 2
 
     def pick(hop):
         below, above = level >= hop, level + hop < groups
         source = jnp.where(below, level - hop, jnp.where(above, level + hop, level + groups - hop))
-        return source, jnp.where(below, 0, jnp.where(above, 1, 2))
+        if hop < middle:
+            return source, jnp.where(below, 0, 1)
+        return source, jnp.where(jnp.logical_or(below, above), 0, 1)
 
     raw = {}
 
@@ -436,64 +500,104 @@
         for inner in range(count):
             raw[chunk + inner] = (pieces, inner)
 
-    def filter_chunk(chunk, split, after=()):
-        return channelize(order, here, filter_taps, hist, *raw[chunk], table, chunk, split, after)
-
-    def arrived(hop):
-        return (early_up[hop], early_down[hop]) if hop < groups else ()
+    def filter_chunk(chunk, split):
+        return channelize(order, here, filter_taps, hist, *raw[chunk], table, chunk, split)
 
     read(0, 1)
     if chunks > 1:
         read(1, 1)
     hist = own_history(order, here, history, parts, taps, fft)
-    (early,) = filter_chunk(0, False)
-    early_up, early_down = hops(early)
     if chunks > 2:
         read(2, chunks - 2)
+    (early,) = filter_chunk(0, False)
+    early = lax.all_gather(
+        early, "tile", axis_index_groups=[[2 * group + which for group in range(groups)] for which in range(2)]
+    )
     sent, plain = {}, []
     for chunk in range(1, chunks):
-        sent[chunk] = exchange(filter_chunk(chunk, True, arrived(1) if chunk == chunks - 1 else ()))
+        sent[chunk] = exchange(filter_chunk(chunk, True))
         if chunk > 1:
             plain = merge(order, here, sent[chunk - 1], cuts, chunk - 2, later, plain)
-    plain = merge(order, here, sent[chunks - 1], cuts, chunks - 2, later, plain, arrived(2))
-    lines = [hops(value) for value in plain]
-
-    (head,) = merge(order, here, exchange(choose(order, here, [early])))
-    head_turned = turn(order, here, head, arrived(3))
+    plain = merge(order, here, sent[chunks - 1], cuts, chunks - 2, later, plain)
+    lines = [({0: value}, {0: value}) for value in plain]
+
+    def step(hop, cut):
+        up, down = lines[cut]
+        if hop <= middle:
+            up[hop] = along(up[hop - 1], hop - 1, groups - 2, 1)
+            down[hop] = along(down[hop - 1], 1, groups - hop, -1)
+        else:
+            pairs = [(g, g + 1) for g in range(hop - 1, groups - 1)] + [(g, g - 1) for g in range(1, groups - hop + 1)]
+            up[hop] = lax.ppermute(up[hop - 1], "tile", [(2 * g + c, 2 * h + c) for g, h in pairs for c in range(2)])
+
+    def one_side(hop, cut):
+        up, down = lines[cut]
+        if hop == middle:
+            up[hop] = select(order, place((level, jnp.where(level >= hop, 0, 1))), [up[hop], down[hop]])
+
+    for cut in range(cuts):
+        step(1, cut)
+
+    (early,) = gate(order, here, [early])
+    early = lax.all_to_all(jnp.swapaxes(early, 0, 1), "chan", split_axis=0, concat_axis=0, tiled=True)
+    gate(order, here, [], [lines[cut][kind][1] for cut in range(cuts) for kind in range(2)], micros=HOP_MICROS)
+    early = merge_early(order, here, early)
+    heads = [early, swap(early)]
     turned = [turn(order, here, value) for value in plain]
-    lefts = [((head, plain[cut]), (head_turned, turned[cut])) for cut in range(cuts)]
+    head_turned = turn(order, here, early)
+    lefts = [((early, plain[cut]), (head_turned, turned[cut])) for cut in range(cuts)]
 
     swapped = {}
 
-    def both(kind, hop, cut):
-        key = (kind, hop, cut)
+    def both(key, value):
         if key not in swapped:
-            swapped[key] = swap(lines[cut][kind][hop])
-        return swapped[key]
-
-    def work(hop):
+            swapped[key] = swap(value)
+        return value, swapped[key]
+
+    def chip_of(hop):
+        return pick(hop) if hop > 0 else (level, 0)
+
+    def later_of(hop, cut):
         if hop == 0:
-            heads = [head, swap(head)]
-            return (level, 0), [(heads, [(plain[cut], swap(plain[cut]))]) for cut in range(cuts)]
-        chip = pick(hop)
-        options = [(0, hop), (1, hop)] + ([(1, groups - hop)] if 2 * hop > groups else [])
-        arrays = [(early_up, early_down)[kind][h] for kind, h in options]
-        (own,) = merge(order, here, exchange(choose(order, place(chip), arrays)))
-        heads = [own, swap(own)]
-        return chip, [
-            (heads, [(lines[cut][kind][h], both(kind, h, cut)) for kind, h in options]) for cut in range(cuts)
-        ]
+            return [both((0, 0, cut), plain[cut])]
+        if hop < middle:
+            return [both((kind, hop, cut), lines[cut][kind][hop]) for kind in range(2)]
+        result = [both((0, hop, cut), lines[cut][0][hop])]
+        if hop > groups - hop:
+            result.append(both((1, groups - hop, cut), lines[cut][1][groups - hop]))
+        return result
 
     out = None
     if 2 * voltages.shape[0] % LANES == 0:
-        for hop in range(groups):
-            chip, sets = work(hop)
+
+        def write(out, hop, cut, after=()):
+            sets = [(heads, later_of(hop, cut))]
+            micros = CORRELATE_MICROS if hop > 0 else 1.0
+            return correlate(order, place(chip_of(hop)), out, lefts[cut], sets, cut, cuts, groups, after, micros)
+
+        for cut in range(cuts):
+            out = write(out, 0, cut)
+        for hop in range(1, groups):
             for cut in range(cuts):
-                out = correlate(order, place(chip), out, lefts[cut], [sets[cut]], cut, cuts, groups)
+                ahead = []
+                if hop + 1 < groups:
+                    step(hop + 1, cut)
+                    if hop + 1 == middle:
+                        one_side(hop + 1, cut)
+                    elif hop + 2 < groups or cut == 0:
+                        ahead = [lines[cut][0][hop + 1]]
+                elif cut > 0:
+                    (lines[cut][0][hop],) = gate(order, here, [lines[cut][0][hop]])
+                out = write(out, hop, cut, ahead)
     else:
-        chips, sets = zip(*[work(hop) for hop in range(groups)])
+        for hop in range(2, groups):
+            for cut in range(cuts):
+                step(hop, cut)
+                one_side(hop, cut)
+        chips = [chip_of(hop) for hop in range(groups)]
         for cut in range(cuts):
-            out = correlate(order, place(*chips), out, lefts[cut], [s[cut] for s in sets], cut, cuts, groups)
+            sets = [(heads, later_of(hop, cut)) for hop in range(groups)]
+            out = correlate(order, place(*chips), out, lefts[cut], sets, cut, cuts, groups)
     return out
 
 

time: 389 us -> 365 us (0.938)
  waiting for transfers between devices: 149 us -> 127 us
  starting transfers between devices: 75 us -> 54.3 us
  local copies, waits for them, and re-layouts: 3.93 us -> 20.7 us
  between operations: 0.64 us -> 13.8 us
  Pallas kernels: 158 us -> 148 us
    ppermute x30 -> x18, waiting for transfers between devices: 65.4 us -> 26.9 us  [exchange(): lax.ppermute(pieces[slot], 'chan', [(i, i ^ slot) for i in range(count)])]
    ppermute x0 -> x2, waiting for transfers between devices: none -> 28 us  [step(): lax.ppermute(up[hop - 1], 'tile', [(2 * g + c, 2 * h + c) for g, h in pai...]
    ppermute x18 -> x8, waiting for transfers between devices: 83.9 us -> 62.8 us  [along(): return lax.ppermute(value, 'tile', pairs)]
    ppermute x18 -> x8, starting transfers between devices: 36.6 us -> 19 us  [along(): return lax.ppermute(value, 'tile', pairs)]
    unnamed x32 -> x40, local copies, waits for them, and re-layouts: 3.93 us -> 17.8 us
    ppermute x30 -> x18, starting transfers between devices: 35.7 us -> 25.6 us  [exchange(): lax.ppermute(pieces[slot], 'chan', [(i, i ^ slot) for i in range(count)])]
    pallas_call x30 -> x28, Pallas kernels: 158 us -> 148 us  [call(): pl.pallas_call(wrapped, out_shape=[*out_shape, jax.ShapeDtypeStruct((8, L...]
    ppermute x18 -> x11, waiting for transfers between devices: 0.05 us -> 9.07 us  [swap(): return lax.ppermute(value, 'tile', [(i, i ^ 1) for i in range(tiles)])]
  transfers between devices with their start and end apart: 66 -> 41, of which waited for: 19 -> 12; matrix products, arithmetic and copies ran while one was open for 0% -> 1% of each run, Pallas kernels for 36% -> 33%
where the time goes in v2:
time: 365 us; the launch traced here: 364 us
  Pallas kernels  148 us (41%)
  waiting for transfers between devices  127 us (35%)
  starting transfers between devices  54.3 us (15%)
  local copies, waits for them, and re-layouts  20.7 us (6%)
  between operations  13.8 us (4%)
    pallas_call x28, Pallas kernels, call(): pl.pallas_call(wrapped, out_shape=[*out_shape, jax.ShapeDtypeStruct((8, L...  148 us
    ppermute x8, waiting for transfers between devices, along(): return lax.ppermute(value, 'tile', pairs)  62.8 us
    ppermute x2, waiting for transfers between devices, step(): lax.ppermute(up[hop - 1], 'tile', [(2 * g + c, 2 * h + c) for g, h in pai...  28 us
    ppermute x18, waiting for transfers between devices, exchange(): lax.ppermute(pieces[slot], 'chan', [(i, i ^ slot) for i in range(count)])  26.9 us
    ppermute x18, starting transfers between devices, exchange(): lax.ppermute(pieces[slot], 'chan', [(i, i ^ slot) for i in range(count)])  25.6 us
    ppermute x8, starting transfers between devices, along(): return lax.ppermute(value, 'tile', pairs)  19 us
    unnamed x40, local copies, waits for them, and re-layouts  17.8 us
    ppermute x11, waiting for transfers between devices, swap(): return lax.ppermute(value, 'tile', [(i, i ^ 1) for i in range(tiles)])  9.07 us
  transfers between devices with their start and end apart: 41, of which 12 were waited for; matrix products, arithmetic and copies ran while one was open for 1% of the time, Pallas kernels for 33%

profile of v2, /device:TPU:0, one launch (start us, length us, event | category | flops | bytes accessed | tf_op | source)
XLA Modules:
  0.0 363.9 jit_solution(1606934343714589752)
XLA Ops:
  6.6 3.3 convert.3
  9.9 3.0 collective-permute-start
  13.0 1.6 collective-permute-start.1
  14.5 3.3 convert.4
  17.9 4.6 %history.1 = (bf16[4,4,16,2048]{3,2,1,0:T(8,128)(2,1)S(1)}, f32[8,128]{1,0:T(8,128)S(1)}) custom-call(s32[3]{0:T(128)S(1)} %pad_add_fusion.place_ref, s32[64,30720]{1,0:T(8,128)} %refs_0_.10, f32[8,128]{1,0:T(8,128)S(1)} %get-tuple-element.80.refs_1_), custom_call_target="tpu_custom_call" | custom-call | flops 5175000064 | tf_op jit(solution)/shard_map/history/pallas_call | solution.py:49
  22.5 4.6 %convert.5 = (bf16[2,4,16,2048]{3,2,1,0:T(8,128)(2,1)S(1)}, bf16[2,4,16,2048]{3,2,1,0:T(8,128)(2,1)S(1)}, bf16[2,4,16,2048]{3,2,1,0:T(8,128)(2,1)S(1)}, bf16[2,4,16,2048]{3,2,1,0:T(8,128)(2,1)S(1)}, f32[8,128]{1,0:T(8,128)S(1)}) custom-call(s32[3]{0:T(128)S(1)} %pad_add_fusion.place_ref, s32[64,32768]{1,0:T(8,128)} %refs_0_.11, ...), custom_call_target="tpu_custom_call" | custom-call | flops 5750000128 | tf_op jit(solution)/shard_map/convert/pallas_call | solution.py:49
  27.1 7.7 %channelize.4 = (bf16[4,4,256,128]{3,2,1,0:T(8,128)(2,1)}, f32[8,128]{1,0:T(8,128)S(1)}) custom-call(s32[3]{0:T(128)S(1)} %pad_add_fusion.place_ref, s32[16,2048]{1,0:T(8,128)S(1)} %copy-done.13, bf16[4,4,16,2048]{3,2,1,0:T(8,128)(2,1)S(1)} %get-tuple-element.81.refs_1_, bf16[1,4,16,2048]{3,2,1,0:T(8,128)(2,1)S(1)} %get-tuple-element.82.refs_2_, ...), custom_call_target="tpu_custom_call" | custom-call | flops 10350000128 | tf_op jit(solution)/shard_map/channelize/pallas_call | solution.py:49
  34.8 2.1 collective-permute-start.6
  36.9 1.7 collective-permute-start.7
  38.6 1.8 collective-permute-start.3
  40.4 1.7 collective-permute-start.4
  42.1 2.1 collective-permute-done.6.refs_3_
  44.1 3.1 collective-permute-start.5
  47.3 4.5 %collective-permute-done.7.refs_4_ = bf16[1,4,16,2048]{3,2,1,0:T(8,128)(2,1)S(1)} collective-permute-done((bf16[1,4,16,2048]{3,2,1,0:T(8,128)(2,1)S(1)}, bf16[1,4,16,2048]{3,2,1,0:T(8,128)(2,1)S(1)}, u32[]{:S(2)}, u32[]{:S(2)}) %collective-permute-start.7) | collective-permute-done | bytes 262176 | tf_op jit(solution)/shard_map/ppermute | solution.py:457
  53.0 6.7 %channelize.5 = (bf16[4,256,128]{2,1,0:T(8,128)(2,1)S(1)}, bf16[4,256,128]{2,1,0:T(8,128)(2,1)S(1)}, bf16[4,256,128]{2,1,0:T(8,128)(2,1)S(1)}, bf16[4,256,128]{2,1,0:T(8,128)(2,1)S(1)}, f32[8,128]{1,0:T(8,128)S(1)}) custom-call(s32[3]{0:T(128)S(1)} %pad_add_fusion.place_ref, s32[16,2048]{1,0:T(8,128)S(1)} %copy-done.13, ...), custom_call_target="tpu_custom_call" | custom-call | flops 10350000128 | tf_op jit(solution)/shard_map/channelize/pallas_call | solution.py:49
  59.7 1.7 collective-permute-start.10
  63.3 16.6 %collective-permute-done.4.refs_4_ = bf16[2,4,16,2048]{3,2,1,0:T(8,128)(2,1)S(1)} collective-permute-done((bf16[2,4,16,2048]{3,2,1,0:T(8,128)(2,1)S(1)}, bf16[2,4,16,2048]{3,2,1,0:T(8,128)(2,1)S(1)}, u32[]{:S(2)}, u32[]{:S(2)}) %collective-permute-start.4) | collective-permute-done | bytes 524320 | tf_op jit(solution)/shard_map/ppermute | solution.py:457
  79.9 6.8 %channelize.6 = (bf16[4,256,128]{2,1,0:T(8,128)(2,1)S(1)}, bf16[4,256,128]{2,1,0:T(8,128)(2,1)S(1)}, bf16[4,256,128]{2,1,0:T(8,128)(2,1)S(1)}, bf16[4,256,128]{2,1,0:T(8,128)(2,1)S(1)}, f32[8,128]{1,0:T(8,128)S(1)}) custom-call(s32[3]{0:T(128)S(1)} %pad_add_fusion.place_ref, s32[16,2048]{1,0:T(8,128)S(1)} %copy-done.13, ...), custom_call_target="tpu_custom_call" | custom-call | flops 10350000128 | tf_op jit(solution)/shard_map/channelize/pallas_call | solution.py:49
  86.7 2.1 collective-permute-start.16
  88.8 1.4 collective-permute-start.17
  90.2 3.0 merge.3
  93.2 6.7 %channelize.7 = (bf16[4,256,128]{2,1,0:T(8,128)(2,1)S(1)}, bf16[4,256,128]{2,1,0:T(8,128)(2,1)S(1)}, bf16[4,256,128]{2,1,0:T(8,128)(2,1)S(1)}, bf16[4,256,128]{2,1,0:T(8,128)(2,1)S(1)}, f32[8,128]{1,0:T(8,128)S(1)}) custom-call(s32[3]{0:T(128)S(1)} %pad_add_fusion.place_ref, s32[16,2048]{1,0:T(8,128)S(1)} %copy-done.13, ...), custom_call_target="tpu_custom_call" | custom-call | flops 10350000128 | tf_op jit(solution)/shard_map/channelize/pallas_call | solution.py:49
  102.0 1.4 collective-permute-start.14
  103.4 3.2 merge.4
  106.6 3.7 %collective-permute-done.13.refs_2_ = bf16[4,256,128]{2,1,0:T(8,128)(2,1)S(1)} collective-permute-done((bf16[4,256,128]{2,1,0:T(8,128)(2,1)S(1)}, bf16[4,256,128]{2,1,0:T(8,128)(2,1)S(1)}, u32[]{:S(2)}, u32[]{:S(2)}) %collective-permute-start.13) | collective-permute-done | bytes 262176 | tf_op jit(solution)/shard_map/ppermute | solution.py:457
  110.3 3.0 merge.5
  113.3 4.5 %collective-permute-start.18 = (bf16[128,48,128]{2,1,0:T(8,128)(2,1)S(1)}, bf16[128,48,128]{2,1,0:T(8,128)(2,1)}, u32[]{:S(2)}, u32[]{:S(2)}) collective-permute-start(bf16[128,48,128]{2,1,0:T(8,128)(2,1)S(1)} %get-tuple-element.121.refs_0_.refs_1_.refs_6_), channel_id=1, source_target_pairs={{0,8},{4,12},{8,16},{12,20},{16,24},{20,28},{1,9},{5,13},{9,17},{1... | collective-permute-start | bytes 4718600 | tf_op jit(solution)/shard_map/ppermute | solution.py:480
  117.9 1.3 collective-permute-start.19
  119.2 5.7 %collective-permute-start.20 = (bf16[128,48,128]{2,1,0:T(8,128)(2,1)}, bf16[128,48,128]{2,1,0:T(8,128)(2,1)}, u32[]{:S(2)}, u32[]{:S(2)}) collective-permute-start(bf16[128,48,128]{2,1,0:T(8,128)(2,1)} %get-tuple-element.122.refs_0_.refs_1_.refs_6_), channel_id=1, source_target_pairs={{0,8},{4,12},{8,16},{12,20},{16,24},{20,28},{1,9},{5,13},{9,17},{1... | collective-permute-start | bytes 4718600 | tf_op jit(solution)/shard_map/ppermute | solution.py:480
  126.2 2.2 copy-done.8
  128.9 2.5 copy.21
  131.5 4.8 %all-to-all-start = ((bf16[4,4,4,256,128]{4,3,2,1,0:T(8,128)(2,1)}), bf16[4,4,4,256,128]{4,3,2,1,0:T(8,128)(2,1)}, u32[]{:S(2)}, u32[]{:S(2)}) async-start(bf16[4,4,4,256,128]{4,3,2,1,0:T(8,128)(2,1)} %bitcast.15), calls=%async_computation | async-start | bytes 8388608 | tf_op jit(solution)/shard_map/all_to_all | solution.py:542
  136.3 15.2 %collective-permute-done.18.refs_0_.refs_6_ = bf16[128,48,128]{2,1,0:T(8,128)(2,1)} collective-permute-done((bf16[128,48,128]{2,1,0:T(8,128)(2,1)S(1)}, bf16[128,48,128]{2,1,0:T(8,128)(2,1)}, u32[]{:S(2)}, u32[]{:S(2)}) %collective-permute-start.18) | collective-permute-done | bytes 1572896 | tf_op jit(solution)/shard_map/ppermute | solution.py:480
  151.5 5.6 %collective-permute-done.19.refs_1_.refs_8_ = bf16[128,48,128]{2,1,0:T(8,128)(2,1)} collective-permute-done((bf16[128,48,128]{2,1,0:T(8,128)(2,1)S(1)}, bf16[128,48,128]{2,1,0:T(8,128)(2,1)}, u32[]{:S(2)}, u32[]{:S(2)}) %collective-permute-start.19) | collective-permute-done | bytes 1572896 | tf_op jit(solution)/shard_map/ppermute | solution.py:480
  157.2 24.0 %collective-permute-done.20.refs_2_.refs_6_ = bf16[128,48,128]{2,1,0:T(8,128)(2,1)} collective-permute-done((bf16[128,48,128]{2,1,0:T(8,128)(2,1)}, bf16[128,48,128]{2,1,0:T(8,128)(2,1)}, u32[]{:S(2)}, u32[]{:S(2)}) %collective-permute-start.20) | collective-permute-done | bytes 1572896 | tf_op jit(solution)/shard_map/ppermute | solution.py:480
  181.2 3.6 collective-permute-done.21.refs_3_.refs_8_
  185.3 7.9 %merge_early.1 = (bf16[4,256,16,128]{3,2,1,0:T(8,128)(2,1)S(1)}, f32[8,128]{1,0:T(8,128)S(1)}) custom-call(s32[3]{0:T(128)S(1)} %pad_add_fusion.place_ref, bf16[4,4,4,256,128]{4,3,2,1,0:T(8,128)(2,1)} %all-to-all-done.refs_0_, f32[8,128]{1,0:T(8,128)S(1)} %gate.4.refs_1_), custom_call_target="tpu_custom_call" | custom-call | flops 46000001024 | tf_op jit(solution)/shard_map/merge_early/pallas_call | solution.py:49
  193.3 2.0 copy-done
  195.9 1.8 collective-permute-start.29
  198.9 6.0 %collective-permute-done.28.refs_7_ = bf16[128,48,128]{2,1,0:T(8,128)(2,1)S(1)} collective-permute-done((bf16[128,48,128]{2,1,0:T(8,128)(2,1)S(1)}, bf16[128,48,128]{2,1,0:T(8,128)(2,1)S(1)}, u32[]{:S(2)}, u32[]{:S(2)}) %collective-permute-start.28) | collective-permute-done | bytes 1572896 | tf_op jit(solution)/shard_map/ppermute | solution.py:483
  207.8 2.0 copy-done.17
  209.9 1.8 collective-permute-start.23
  211.9 1.6 turn.3
  213.5 5.0 %turn.4 = (bf16[128,48,128]{2,1,0:T(8,128)(2,1)S(1)}, f32[8,128]{1,0:T(8,128)S(1)}) custom-call(s32[3]{0:T(128)S(1)} %pad_add_fusion.place_ref, bf16[128,48,128]{2,1,0:T(8,128)(2,1)} %get-tuple-element.122.refs_0_.refs_1_.refs_6_, f32[8,128]{1,0:T(8,128)S(1)} %get-tuple-element.126.refs_1_), custom_call_target="tpu_custom_call" | custom-call | flops 115000000 | tf_op jit(solution)/shard_map/turn/pallas_call | solution.py:49
  218.5 2.7 copy-done.1
  221.3 2.2 turn.5
  223.4 7.7 %correlate.8 = (f32[2,256,64,512]{3,2,1,0:T(8,128)}, f32[8,128]{1,0:T(8,128)S(1)}) custom-call(s32[5]{0:T(128)S(1)} %stack.44.place_ref, bf16[4,256,16,128]{3,2,1,0:T(8,128)(2,1)} %copy-done, bf16[128,48,128]{2,1,0:T(8,128)(2,1)S(1)} %get-tuple-element.121.refs_0_.refs_1_.refs_6_, bf16[256,16,128]{2,1,0:T(8,128)(2,1)S(1)} %get-tuple-element.128.refs_2_, ...), custom_call_target="tpu_custom_call" | custom-call | flops 1150000000 | tf_op jit(solution)/shard_map/correlate/pallas_call | solution.py:49
  231.1 1.3 collective-permute-start.24
  232.4 8.7 %correlate.9 = (f32[2,256,64,512]{3,2,1,0:T(8,128)}, f32[8,128]{1,0:T(8,128)S(1)}) custom-call(s32[5]{0:T(128)S(1)} %stack.44.place_ref, bf16[4,256,16,128]{3,2,1,0:T(8,128)(2,1)} %copy-done, bf16[128,48,128]{2,1,0:T(8,128)(2,1)} %get-tuple-element.122.refs_0_.refs_1_.refs_6_, ...), custom_call_target="tpu_custom_call", output_to_operand_aliasing={{0}: (9, {})} | custom-call | flops 1150000000 | tf_op jit(solution)/shard_map/correlate/pallas_call | solution.py:49
  241.3 4.3 %select.6 = (bf16[128,48,128]{2,1,0:T(8,128)(2,1)}, f32[8,128]{1,0:T(8,128)S(1)}) custom-call(s32[5]{0:T(128)S(1)} %stack.40.place_ref, bf16[128,48,128]{2,1,0:T(8,128)(2,1)} %collective-permute-done.29.refs_0_, bf16[128,48,128]{2,1,0:T(8,128)(2,1)} %collective-permute-done.30.refs_1_, f32[8,128]{1,0:T(8,128)S(1)} %get-tuple-element.135.refs_2_), custom_call_target="tpu_custom_call" | custom-call | flops 1150000000 | tf_op jit(solution)/shard_map/select/pallas_call | solution.py:49
  245.6 1.3 collective-permute-start.32
  247.6 1.4 copy-done.3
  249.0 8.6 %correlate.10 = (f32[2,256,64,512]{3,2,1,0:T(8,128)}, f32[8,128]{1,0:T(8,128)S(1)}) custom-call(s32[5]{0:T(128)S(1)} %stack.43.place_ref, bf16[4,256,16,128]{3,2,1,0:T(8,128)(2,1)} %copy-done, bf16[128,48,128]{2,1,0:T(8,128)(2,1)S(1)} %get-tuple-element.121.refs_0_.refs_1_.refs_6_, ...), custom_call_target="tpu_custom_call", output_to_operand_aliasing={{0}: (11, {})} | custom-call | flops 8049999872 | tf_op jit(solution)/shard_map/correlate/pallas_call | solution.py:49
  257.6 14.3 %collective-permute-done.24.refs_1_ = bf16[128,48,128]{2,1,0:T(8,128)(2,1)} collective-permute-done((bf16[128,48,128]{2,1,0:T(8,128)(2,1)}, bf16[128,48,128]{2,1,0:T(8,128)(2,1)}, u32[]{:S(2)}, u32[]{:S(2)}) %collective-permute-start.24) | collective-permute-done | bytes 1572896 | tf_op jit(solution)/shard_map/ppermute | solution.py:480
  271.9 4.3 %select.7 = (bf16[128,48,128]{2,1,0:T(8,128)(2,1)}, f32[8,128]{1,0:T(8,128)S(1)}) custom-call(s32[5]{0:T(128)S(1)} %stack.40.place_ref, bf16[128,48,128]{2,1,0:T(8,128)(2,1)} %collective-permute-done.23.refs_0_, bf16[128,48,128]{2,1,0:T(8,128)(2,1)} %collective-permute-done.24.refs_1_, f32[8,128]{1,0:T(8,128)S(1)} %get-tuple-element.137.refs_2_), custom_call_target="tpu_custom_call" | custom-call | flops 1150000000 | tf_op jit(solution)/shard_map/select/pallas_call | solution.py:49
  276.3 1.3 collective-permute-start.31
  277.6 28.0 %collective-permute-done.32.refs_9_.refs_6_ = bf16[128,48,128]{2,1,0:T(8,128)(2,1)} collective-permute-done((bf16[128,48,128]{2,1,0:T(8,128)(2,1)}, bf16[128,48,128]{2,1,0:T(8,128)(2,1)}, u32[]{:S(2)}, u32[]{:S(2)}) %collective-permute-start.32) | collective-permute-done | bytes 1572896 | tf_op jit(solution)/shard_map/ppermute | solution.py:531
  305.6 1.4 copy-done.6
  307.0 9.1 %correlate.11 = (f32[2,256,64,512]{3,2,1,0:T(8,128)}, f32[8,128]{1,0:T(8,128)S(1)}) custom-call(s32[5]{0:T(128)S(1)} %stack.43.place_ref, bf16[4,256,16,128]{3,2,1,0:T(8,128)(2,1)} %copy-done, bf16[128,48,128]{2,1,0:T(8,128)(2,1)} %get-tuple-element.122.refs_0_.refs_1_.refs_6_, ...), custom_call_target="tpu_custom_call", output_to_operand_aliasing={{0}: (11, {})} | custom-call | flops 8049999872 | tf_op jit(solution)/shard_map/correlate/pallas_call | solution.py:49
  316.1 8.4 %correlate.12 = (f32[2,256,64,512]{3,2,1,0:T(8,128)}, f32[8,128]{1,0:T(8,128)S(1)}) custom-call(s32[5]{0:T(128)S(1)} %stack.47.place_ref, bf16[4,256,16,128]{3,2,1,0:T(8,128)(2,1)} %copy-done, bf16[128,48,128]{2,1,0:T(8,128)(2,1)S(1)} %get-tuple-element.121.refs_0_.refs_1_.refs_6_, ...), custom_call_target="tpu_custom_call", output_to_operand_aliasing={{0}: (9, {})} | custom-call | flops 8049999872 | tf_op jit(solution)/shard_map/correlate/pallas_call | solution.py:49
  324.5 8.9 %correlate.13 = (f32[2,256,64,512]{3,2,1,0:T(8,128)}, f32[8,128]{1,0:T(8,128)S(1)}) custom-call(s32[5]{0:T(128)S(1)} %stack.47.place_ref, bf16[4,256,16,128]{3,2,1,0:T(8,128)(2,1)} %copy-done, bf16[128,48,128]{2,1,0:T(8,128)(2,1)} %get-tuple-element.122.refs_0_.refs_1_.refs_6_, ...), custom_call_target="tpu_custom_call", output_to_operand_aliasing={{0}: (9, {})} | custom-call | flops 8049999872 | tf_op jit(solution)/shard_map/correlate/pallas_call | solution.py:49
  334.6 8.6 %correlate.14 = (f32[2,256,64,512]{3,2,1,0:T(8,128)}, f32[8,128]{1,0:T(8,128)S(1)}) custom-call(s32[5]{0:T(128)S(1)} %stack.37.place_ref, bf16[4,256,16,128]{3,2,1,0:T(8,128)(2,1)} %copy-done, bf16[128,48,128]{2,1,0:T(8,128)(2,1)S(1)} %get-tuple-element.121.refs_0_.refs_1_.refs_6_, ...), custom_call_target="tpu_custom_call", output_to_operand_aliasing={{0}: (11, {})} | custom-call | flops 8049999872 | tf_op jit(solution)/shard_map/correlate/pallas_call | solution.py:49
  344.3 3.0 collective-permute-done.38.refs_7_
  348.5 8.6 %correlate.15 = (f32[2,256,64,512]{3,2,1,0:T(8,128)}, f32[8,128]{1,0:T(8,128)}) custom-call(s32[5]{0:T(128)S(1)} %stack.37.place_ref, bf16[4,256,16,128]{3,2,1,0:T(8,128)(2,1)} %copy-done, bf16[128,48,128]{2,1,0:T(8,128)(2,1)} %get-tuple-element.122.refs_0_.refs_1_.refs_6_, ...), custom_call_target="tpu_custom_call", output_to_operand_aliasing={{0}: (11, {})} | custom-call | flops 8049999872 | tf_op jit(solution)/shard_map/correlate/pallas_call | solution.py:49
  (94 shorter events, 17.2 us)
Async XLA Ops:
  6.5 119.7 %all-gather.3.cloned.1.call-start = ((), (), s32[]{:S(2)}) async-start(), calls=%async_computation.1 | async-start | bytes 5242880 | tf_op jit(solution)/shard_map/all_gather | solution.py:513
  9.9 17.1 %collective-permute-start = (bf16[1,4,16,2048]{3,2,1,0:T(8,128)(2,1)S(1)}, bf16[1,4,16,2048]{3,2,1,0:T(8,128)(2,1)S(1)}, u32[]{:S(2)}, u32[]{:S(2)}) collective-permute-start(bf16[1,4,16,2048]{3,2,1,0:T(8,128)(2,1)S(1)} %get-tuple-element.83), channel_id=1, source_target_pairs={{0,1},{1,0},{2,3},{3,2},{4,5},{5,4},{6,7},{7,6},{8,9},{9,8},{10,11... | collective-permute-start | bytes 786440 | tf_op jit(solution)/shard_map/ppermute | solution.py:457
  13.0 14.1 %collective-permute-start.1 = (bf16[1,4,16,2048]{3,2,1,0:T(8,128)(2,1)S(1)}, bf16[1,4,16,2048]{3,2,1,0:T(8,128)(2,1)S(1)}, u32[]{:S(2)}, u32[]{:S(2)}) collective-permute-start(bf16[1,4,16,2048]{3,2,1,0:T(8,128)(2,1)S(1)} %get-tuple-element.84), channel_id=1, source_target_pairs={{0,2},{1,3},{2,0},{3,1},{4,6},{5,7},{6,4},{7,5},{8,10},{9,11},{10,... | collective-permute-start | bytes 786440 | tf_op jit(solution)/shard_map/ppermute | solution.py:457
  14.5 12.6 %collective-permute-start.2 = (bf16[1,4,16,2048]{3,2,1,0:T(8,128)(2,1)S(1)}, bf16[1,4,16,2048]{3,2,1,0:T(8,128)(2,1)S(1)}, u32[]{:S(2)}, u32[]{:S(2)}) collective-permute-start(bf16[1,4,16,2048]{3,2,1,0:T(8,128)(2,1)S(1)} %get-tuple-element.85), channel_id=1, source_target_pairs={{0,3},{1,2},{2,1},{3,0},{4,7},{5,6},{6,5},{7,4},{8,11},{9,10},{10,... | collective-permute-start | bytes 786440 | tf_op jit(solution)/shard_map/ppermute | solution.py:457
  22.5 4.6 %copy-start.14 = (bf16[4,4,16,2048]{3,2,1,0:T(8,128)(2,1)}, bf16[4,4,16,2048]{3,2,1,0:T(8,128)(2,1)S(1)}, u32[]{:S(2)}) copy-start(bf16[4,4,16,2048]{3,2,1,0:T(8,128)(2,1)S(1)} %get-tuple-element.81.refs_1_) | copy-start | bytes 3145732
  22.5 4.6 %copy-start.13 = (s32[16,2048]{1,0:T(8,128)S(1)}, s32[16,2048]{1,0:T(8,128)}, u32[]{:S(2)}) copy-start(s32[16,2048]{1,0:T(8,128)} %refs_0_.15) | copy-start | bytes 393220
  34.8 9.3 %collective-permute-start.6 = (bf16[1,4,16,2048]{3,2,1,0:T(8,128)(2,1)S(1)}, bf16[1,4,16,2048]{3,2,1,0:T(8,128)(2,1)S(1)}, u32[]{:S(2)}, u32[]{:S(2)}) collective-permute-start(bf16[1,4,16,2048]{3,2,1,0:T(8,128)(2,1)S(1)} %get-tuple-element.94), channel_id=1, source_target_pairs={{0,1},{1,0},{2,3},{3,2},{4,5},{5,4},{6,7},{7,6},{8,9},{9,8},{10,11... | collective-permute-start | bytes 786440 | tf_op jit(solution)/shard_map/ppermute | solution.py:457
  36.9 14.9 %collective-permute-start.7 = (bf16[1,4,16,2048]{3,2,1,0:T(8,128)(2,1)S(1)}, bf16[1,4,16,2048]{3,2,1,0:T(8,128)(2,1)S(1)}, u32[]{:S(2)}, u32[]{:S(2)}) collective-permute-start(bf16[1,4,16,2048]{3,2,1,0:T(8,128)(2,1)S(1)} %get-tuple-element.95), channel_id=1, source_target_pairs={{0,2},{1,3},{2,0},{3,1},{4,6},{5,7},{6,4},{7,5},{8,10},{9,11},{10,... | collective-permute-start | bytes 786440 | tf_op jit(solution)/shard_map/ppermute | solution.py:457
  38.6 13.2 %collective-permute-start.8 = (bf16[1,4,16,2048]{3,2,1,0:T(8,128)(2,1)S(1)}, bf16[1,4,16,2048]{3,2,1,0:T(8,128)(2,1)S(1)}, u32[]{:S(2)}, u32[]{:S(2)}) collective-permute-start(bf16[1,4,16,2048]{3,2,1,0:T(8,128)(2,1)S(1)} %get-tuple-element.96), channel_id=1, source_target_pairs={{0,3},{1,2},{2,1},{3,0},{4,7},{5,6},{6,5},{7,4},{8,11},{9,10},{10,... | collective-permute-start | bytes 786440 | tf_op jit(solution)/shard_map/ppermute | solution.py:457
  38.6 23.8 %collective-permute-start.3 = (bf16[2,4,16,2048]{3,2,1,0:T(8,128)(2,1)S(1)}, bf16[2,4,16,2048]{3,2,1,0:T(8,128)(2,1)S(1)}, u32[]{:S(2)}, u32[]{:S(2)}) collective-permute-start(bf16[2,4,16,2048]{3,2,1,0:T(8,128)(2,1)S(1)} %get-tuple-element.90), channel_id=1, source_target_pairs={{0,1},{1,0},{2,3},{3,2},{4,5},{5,4},{6,7},{7,6},{8,9},{9,8},{10,11... | collective-permute-start | bytes 1572872 | tf_op jit(solution)/shard_map/ppermute | solution.py:457
  40.4 39.5 %collective-permute-start.4 = (bf16[2,4,16,2048]{3,2,1,0:T(8,128)(2,1)S(1)}, bf16[2,4,16,2048]{3,2,1,0:T(8,128)(2,1)S(1)}, u32[]{:S(2)}, u32[]{:S(2)}) collective-permute-start(bf16[2,4,16,2048]{3,2,1,0:T(8,128)(2,1)S(1)} %get-tuple-element.91), channel_id=1, source_target_pairs={{0,2},{1,3},{2,0},{3,1},{4,6},{5,7},{6,4},{7,5},{8,10},{9,11},{10,... | collective-permute-start | bytes 1572872 | tf_op jit(solution)/shard_map/ppermute | solution.py:457
  44.1 35.7 %collective-permute-start.5 = (bf16[2,4,16,2048]{3,2,1,0:T(8,128)(2,1)S(1)}, bf16[2,4,16,2048]{3,2,1,0:T(8,128)(2,1)S(1)}, u32[]{:S(2)}, u32[]{:S(2)}) collective-permute-start(bf16[2,4,16,2048]{3,2,1,0:T(8,128)(2,1)S(1)} %get-tuple-element.92), channel_id=1, source_target_pairs={{0,3},{1,2},{2,1},{3,0},{4,7},{5,6},{6,5},{7,4},{8,11},{9,10},{10,... | collective-permute-start | bytes 1572872 | tf_op jit(solution)/shard_map/ppermute | solution.py:457
  51.8 1.2 copy-start.15
  53.0 26.9 %copy-start.16 = (bf16[4,4,16,2048]{3,2,1,0:T(8,128)(2,1)S(1)}, bf16[4,4,16,2048]{3,2,1,0:T(8,128)(2,1)}, u32[]{:S(2)}) copy-start(bf16[4,4,16,2048]{3,2,1,0:T(8,128)(2,1)} %copy-done.14) | copy-start | bytes 3145732
  59.7 29.1 %collective-permute-start.10 = (bf16[4,256,128]{2,1,0:T(8,128)(2,1)S(1)}, bf16[4,256,128]{2,1,0:T(8,128)(2,1)S(1)}, u32[]{:S(2)}, u32[]{:S(2)}) collective-permute-start(bf16[4,256,128]{2,1,0:T(8,128)(2,1)S(1)} %get-tuple-element.100), channel_id=1, source_target_pairs={{0,2},{1,3},{2,0},{3,1},{4,6},{5,7},{6,4},{7,5},{8,10},{9,11},{10,... | collective-permute-start | bytes 786440 | tf_op jit(solution)/shard_map/ppermute | solution.py:457
  61.5 28.8 %collective-permute-start.11 = (bf16[4,256,128]{2,1,0:T(8,128)(2,1)S(1)}, bf16[4,256,128]{2,1,0:T(8,128)(2,1)S(1)}, u32[]{:S(2)}, u32[]{:S(2)}) collective-permute-start(bf16[4,256,128]{2,1,0:T(8,128)(2,1)S(1)} %get-tuple-element.101), channel_id=1, source_target_pairs={{0,3},{1,2},{2,1},{3,0},{4,7},{5,6},{6,5},{7,4},{8,11},{9,10},{10,... | collective-permute-start | bytes 786440 | tf_op jit(solution)/shard_map/ppermute | solution.py:457
  62.4 27.8 %collective-permute-start.9 = (bf16[4,256,128]{2,1,0:T(8,128)(2,1)S(1)}, bf16[4,256,128]{2,1,0:T(8,128)(2,1)S(1)}, u32[]{:S(2)}, u32[]{:S(2)}) collective-permute-start(bf16[4,256,128]{2,1,0:T(8,128)(2,1)S(1)} %get-tuple-element.99), channel_id=1, source_target_pairs={{0,1},{1,0},{2,3},{3,2},{4,5},{5,4},{6,7},{7,6},{8,9},{9,8},{10,11... | collective-permute-start | bytes 786440 | tf_op jit(solution)/shard_map/ppermute | solution.py:457
  86.7 15.4 %collective-permute-start.15 = (bf16[4,256,128]{2,1,0:T(8,128)(2,1)S(1)}, bf16[4,256,128]{2,1,0:T(8,128)(2,1)S(1)}, u32[]{:S(2)}, u32[]{:S(2)}) collective-permute-start(bf16[4,256,128]{2,1,0:T(8,128)(2,1)S(1)} %get-tuple-element.110), channel_id=1, source_target_pairs={{0,1},{1,0},{2,3},{3,2},{4,5},{5,4},{6,7},{7,6},{8,9},{9,8},{10,11... | collective-permute-start | bytes 786440 | tf_op jit(solution)/shard_map/ppermute | solution.py:457
  86.7 16.7 %collective-permute-start.16 = (bf16[4,256,128]{2,1,0:T(8,128)(2,1)S(1)}, bf16[4,256,128]{2,1,0:T(8,128)(2,1)S(1)}, u32[]{:S(2)}, u32[]{:S(2)}) collective-permute-start(bf16[4,256,128]{2,1,0:T(8,128)(2,1)S(1)} %get-tuple-element.111), channel_id=1, source_target_pairs={{0,2},{1,3},{2,0},{3,1},{4,6},{5,7},{6,4},{7,5},{8,10},{9,11},{10,... | collective-permute-start | bytes 786440 | tf_op jit(solution)/shard_map/ppermute | solution.py:457
  88.8 14.6 %collective-permute-start.17 = (bf16[4,256,128]{2,1,0:T(8,128)(2,1)S(1)}, bf16[4,256,128]{2,1,0:T(8,128)(2,1)S(1)}, u32[]{:S(2)}, u32[]{:S(2)}) collective-permute-start(bf16[4,256,128]{2,1,0:T(8,128)(2,1)S(1)} %get-tuple-element.112), channel_id=1, source_target_pairs={{0,3},{1,2},{2,1},{3,0},{4,7},{5,6},{6,5},{7,4},{8,11},{9,10},{10,... | collective-permute-start | bytes 786440 | tf_op jit(solution)/shard_map/ppermute | solution.py:457
  99.9 6.7 %collective-permute-start.12 = (bf16[4,256,128]{2,1,0:T(8,128)(2,1)S(1)}, bf16[4,256,128]{2,1,0:T(8,128)(2,1)S(1)}, u32[]{:S(2)}, u32[]{:S(2)}) collective-permute-start(bf16[4,256,128]{2,1,0:T(8,128)(2,1)S(1)} %get-tuple-element.106), channel_id=1, source_target_pairs={{0,1},{1,0},{2,3},{3,2},{4,5},{5,4},{6,7},{7,6},{8,9},{9,8},{10,11... | collective-permute-start | bytes 786440 | tf_op jit(solution)/shard_map/ppermute | solution.py:457
  101.2 9.2 %collective-permute-start.13 = (bf16[4,256,128]{2,1,0:T(8,128)(2,1)S(1)}, bf16[4,256,128]{2,1,0:T(8,128)(2,1)S(1)}, u32[]{:S(2)}, u32[]{:S(2)}) collective-permute-start(bf16[4,256,128]{2,1,0:T(8,128)(2,1)S(1)} %get-tuple-element.107), channel_id=1, source_target_pairs={{0,2},{1,3},{2,0},{3,1},{4,6},{5,7},{6,4},{7,5},{8,10},{9,11},{10,... | collective-permute-start | bytes 786440 | tf_op jit(solution)/shard_map/ppermute | solution.py:457
  102.0 8.3 %collective-permute-start.14 = (bf16[4,256,128]{2,1,0:T(8,128)(2,1)S(1)}, bf16[4,256,128]{2,1,0:T(8,128)(2,1)S(1)}, u32[]{:S(2)}, u32[]{:S(2)}) collective-permute-start(bf16[4,256,128]{2,1,0:T(8,128)(2,1)S(1)} %get-tuple-element.108), channel_id=1, source_target_pairs={{0,3},{1,2},{2,1},{3,0},{4,7},{5,6},{6,5},{7,4},{8,11},{9,10},{10,... | collective-permute-start | bytes 786440 | tf_op jit(solution)/shard_map/ppermute | solution.py:457
  113.3 38.2 %collective-permute-start.18 = (bf16[128,48,128]{2,1,0:T(8,128)(2,1)S(1)}, bf16[128,48,128]{2,1,0:T(8,128)(2,1)}, u32[]{:S(2)}, u32[]{:S(2)}) collective-permute-start(bf16[128,48,128]{2,1,0:T(8,128)(2,1)S(1)} %get-tuple-element.121.refs_0_.refs_1_.refs_6_), channel_id=1, source_target_pairs={{0,8},{4,12},{8,16},{12,20},{16,24},{20,28},{1,9},{5,13},{9,17},{1... | collective-permute-start | bytes 4718600 | tf_op jit(solution)/shard_map/ppermute | solution.py:480
  117.9 39.3 %collective-permute-start.19 = (bf16[128,48,128]{2,1,0:T(8,128)(2,1)S(1)}, bf16[128,48,128]{2,1,0:T(8,128)(2,1)}, u32[]{:S(2)}, u32[]{:S(2)}) collective-permute-start(bf16[128,48,128]{2,1,0:T(8,128)(2,1)S(1)} %get-tuple-element.121.refs_0_.refs_1_.refs_6_), channel_id=1, source_target_pairs={{8,0},{12,4},{16,8},{20,12},{24,16},{28,20},{9,1},{13,5},{17,9},{2... | collective-permute-start | bytes 4718600 | tf_op jit(solution)/shard_map/ppermute | solution.py:480
  119.2 62.0 %collective-permute-start.20 = (bf16[128,48,128]{2,1,0:T(8,128)(2,1)}, bf16[128,48,128]{2,1,0:T(8,128)(2,1)}, u32[]{:S(2)}, u32[]{:S(2)}) collective-permute-start(bf16[128,48,128]{2,1,0:T(8,128)(2,1)} %get-tuple-element.122.refs_0_.refs_1_.refs_6_), channel_id=1, source_target_pairs={{0,8},{4,12},{8,16},{12,20},{16,24},{20,28},{1,9},{5,13},{9,17},{1... | collective-permute-start | bytes 4718600 | tf_op jit(solution)/shard_map/ppermute | solution.py:480
  124.9 59.9 %collective-permute-start.21 = (bf16[128,48,128]{2,1,0:T(8,128)(2,1)}, bf16[128,48,128]{2,1,0:T(8,128)(2,1)}, u32[]{:S(2)}, u32[]{:S(2)}) collective-permute-start(bf16[128,48,128]{2,1,0:T(8,128)(2,1)} %get-tuple-element.122.refs_0_.refs_1_.refs_6_), channel_id=1, source_target_pairs={{8,0},{12,4},{16,8},{20,12},{24,16},{28,20},{9,1},{13,5},{17,9},{2... | collective-permute-start | bytes 4718600 | tf_op jit(solution)/shard_map/ppermute | solution.py:480
  126.2 2.2 copy-start.8
  131.5 53.8 %all-to-all-start = ((bf16[4,4,4,256,128]{4,3,2,1,0:T(8,128)(2,1)}), bf16[4,4,4,256,128]{4,3,2,1,0:T(8,128)(2,1)}, u32[]{:S(2)}, u32[]{:S(2)}) async-start(bf16[4,4,4,256,128]{4,3,2,1,0:T(8,128)(2,1)} %bitcast.15), calls=%async_computation | async-start | bytes 8388608 | tf_op jit(solution)/shard_map/all_to_all | solution.py:542
  193.2 14.6 %collective-permute-start.22 = (bf16[4,256,16,128]{3,2,1,0:T(8,128)(2,1)S(1)}, bf16[4,256,16,128]{3,2,1,0:T(8,128)(2,1)S(1)}, u32[]{:S(2)}, u32[]{:S(2)}) collective-permute-start(bf16[4,256,16,128]{3,2,1,0:T(8,128)(2,1)S(1)} %get-tuple-element.124.refs_0_.refs_4_), channel_id=1, source_target_pairs={{0,4},{4,0},{8,12},{12,8},{16,20},{20,16},{24,28},{28,24},{1,5},{5... | collective-permute-start | bytes 12582920 | tf_op jit(solution)/shard_map/ppermute | solution.py:483
  193.3 2.0 copy-start
  195.3 9.6 %collective-permute-start.28 = (bf16[128,48,128]{2,1,0:T(8,128)(2,1)S(1)}, bf16[128,48,128]{2,1,0:T(8,128)(2,1)S(1)}, u32[]{:S(2)}, u32[]{:S(2)}) collective-permute-start(bf16[128,48,128]{2,1,0:T(8,128)(2,1)S(1)} %get-tuple-element.121.refs_0_.refs_1_.refs_6_), channel_id=1, source_target_pairs={{0,4},{4,0},{8,12},{12,8},{16,20},{20,16},{24,28},{28,24},{1,5},{5... | collective-permute-start | bytes 4718600 | tf_op jit(solution)/shard_map/ppermute | solution.py:483
  195.8 10.4 %collective-permute-start.27 = (bf16[128,48,128]{2,1,0:T(8,128)(2,1)}, bf16[128,48,128]{2,1,0:T(8,128)(2,1)S(1)}, u32[]{:S(2)}, u32[]{:S(2)}) collective-permute-start(bf16[128,48,128]{2,1,0:T(8,128)(2,1)} %get-tuple-element.122.refs_0_.refs_1_.refs_6_), channel_id=1, source_target_pairs={{0,4},{4,0},{8,12},{12,8},{16,20},{20,16},{24,28},{28,24},{1,5},{5... | collective-permute-start | bytes 4718600 | tf_op jit(solution)/shard_map/ppermute | solution.py:483
  195.9 35.3 %collective-permute-start.29 = (bf16[128,48,128]{2,1,0:T(8,128)(2,1)}, bf16[128,48,128]{2,1,0:T(8,128)(2,1)}, u32[]{:S(2)}, u32[]{:S(2)}) collective-permute-start(bf16[128,48,128]{2,1,0:T(8,128)(2,1)} %collective-permute-done.18.refs_0_.refs_6_), channel_id=1, source_target_pairs={{8,16},{12,20},{16,24},{20,28},{9,17},{13,21},{17,25},{21,29},{10,... | collective-permute-start | bytes 4718600 | tf_op jit(solution)/shard_map/ppermute | solution.py:480
  197.7 43.5 %collective-permute-start.30 = (bf16[128,48,128]{2,1,0:T(8,128)(2,1)}, bf16[128,48,128]{2,1,0:T(8,128)(2,1)}, u32[]{:S(2)}, u32[]{:S(2)}) collective-permute-start(bf16[128,48,128]{2,1,0:T(8,128)(2,1)} %collective-permute-done.19.refs_1_.refs_8_), channel_id=1, source_target_pairs={{8,0},{12,4},{16,8},{20,12},{9,1},{13,5},{17,9},{21,13},{10,2},{14... | collective-permute-start | bytes 4718600 | tf_op jit(solution)/shard_map/ppermute | solution.py:480
  205.0 1.1 copy-start.9
  206.1 39.5 %collective-permute-start.25 = (bf16[128,48,128]{2,1,0:T(8,128)(2,1)}, bf16[128,48,128]{2,1,0:T(8,128)(2,1)}, u32[]{:S(2)}, u32[]{:S(2)}) collective-permute-start(bf16[128,48,128]{2,1,0:T(8,128)(2,1)} %collective-permute-done.18.refs_0_.refs_6_), channel_id=1, source_target_pairs={{0,4},{4,0},{8,12},{12,8},{16,20},{20,16},{24,28},{28,24},{1,5},{5... | collective-permute-start | bytes 4718600 | tf_op jit(solution)/shard_map/ppermute | solution.py:483
  206.2 1.2 copy-start.11
  207.5 39.4 %collective-permute-start.26 = (bf16[128,48,128]{2,1,0:T(8,128)(2,1)}, bf16[128,48,128]{2,1,0:T(8,128)(2,1)}, u32[]{:S(2)}, u32[]{:S(2)}) collective-permute-start(bf16[128,48,128]{2,1,0:T(8,128)(2,1)} %collective-permute-done.19.refs_1_.refs_8_), channel_id=1, source_target_pairs={{0,4},{4,0},{8,12},{12,8},{16,20},{20,16},{24,28},{28,24},{1,5},{5... | collective-permute-start | bytes 4718600 | tf_op jit(solution)/shard_map/ppermute | solution.py:483
  207.8 2.0 copy-start.17
  209.9 37.6 %collective-permute-start.23 = (bf16[128,48,128]{2,1,0:T(8,128)(2,1)}, bf16[128,48,128]{2,1,0:T(8,128)(2,1)}, u32[]{:S(2)}, u32[]{:S(2)}) collective-permute-start(bf16[128,48,128]{2,1,0:T(8,128)(2,1)} %collective-permute-done.20.refs_2_.refs_6_), channel_id=1, source_target_pairs={{8,16},{12,20},{16,24},{20,28},{9,17},{13,21},{17,25},{21,29},{10,... | collective-permute-start | bytes 4718600 | tf_op jit(solution)/shard_map/ppermute | solution.py:480
  213.5 9.9 %copy-start.2 = (bf16[128,48,128]{2,1,0:T(8,128)(2,1)}, bf16[128,48,128]{2,1,0:T(8,128)(2,1)S(1)}, u32[]{:S(2)}) copy-start(bf16[128,48,128]{2,1,0:T(8,128)(2,1)S(1)} %get-tuple-element.130.refs_3_) | copy-start | bytes 4718596
  218.5 13.9 %copy-start.5 = (bf16[128,48,128]{2,1,0:T(8,128)(2,1)}, bf16[128,48,128]{2,1,0:T(8,128)(2,1)S(1)}, u32[]{:S(2)}) copy-start(bf16[128,48,128]{2,1,0:T(8,128)(2,1)S(1)} %get-tuple-element.129.refs_3_) | copy-start | bytes 4718596
  218.5 2.8 copy-start.1
  221.2 2.2 copy-start.10
  223.4 9.0 %copy-start.12 = (bf16[128,48,128]{2,1,0:T(8,128)(2,1)S(1)}, bf16[128,48,128]{2,1,0:T(8,128)(2,1)}, u32[]{:S(2)}) copy-start(bf16[128,48,128]{2,1,0:T(8,128)(2,1)} %copy-done.11) | copy-start | bytes 4718596
  231.1 40.7 %collective-permute-start.24 = (bf16[128,48,128]{2,1,0:T(8,128)(2,1)}, bf16[128,48,128]{2,1,0:T(8,128)(2,1)}, u32[]{:S(2)}, u32[]{:S(2)}) collective-permute-start(bf16[128,48,128]{2,1,0:T(8,128)(2,1)} %collective-permute-done.21.refs_3_.refs_8_), channel_id=1, source_target_pairs={{8,0},{12,4},{16,8},{20,12},{9,1},{13,5},{17,9},{21,13},{10,2},{14... | collective-permute-start | bytes 4718600 | tf_op jit(solution)/shard_map/ppermute | solution.py:480
  241.2 35.1 %collective-permute-start.36 = (bf16[128,48,128]{2,1,0:T(8,128)(2,1)}, bf16[128,48,128]{2,1,0:T(8,128)(2,1)}, u32[]{:S(2)}, u32[]{:S(2)}) collective-permute-start(bf16[128,48,128]{2,1,0:T(8,128)(2,1)} %collective-permute-done.20.refs_2_.refs_6_), channel_id=1, source_target_pairs={{0,4},{4,0},{8,12},{12,8},{16,20},{20,16},{24,28},{28,24},{1,5},{5... | collective-permute-start | bytes 4718600 | tf_op jit(solution)/shard_map/ppermute | solution.py:483
  245.6 60.0 %collective-permute-start.32 = (bf16[128,48,128]{2,1,0:T(8,128)(2,1)}, bf16[128,48,128]{2,1,0:T(8,128)(2,1)}, u32[]{:S(2)}, u32[]{:S(2)}) collective-permute-start(bf16[128,48,128]{2,1,0:T(8,128)(2,1)} %get-tuple-element.139.refs_6_), channel_id=1, source_target_pairs={{16,24},{20,28},{8,0},{12,4},{17,25},{21,29},{9,1},{13,5},{18,26},... | collective-permute-start | bytes 4718600 | tf_op jit(solution)/shard_map/ppermute | solution.py:531
  246.9 58.7 %collective-permute-start.37 = (bf16[128,48,128]{2,1,0:T(8,128)(2,1)}, bf16[128,48,128]{2,1,0:T(8,128)(2,1)}, u32[]{:S(2)}, u32[]{:S(2)}) collective-permute-start(bf16[128,48,128]{2,1,0:T(8,128)(2,1)} %collective-permute-done.21.refs_3_.refs_8_), channel_id=1, source_target_pairs={{0,4},{4,0},{8,12},{12,8},{16,20},{20,16},{24,28},{28,24},{1,5},{5... | collective-permute-start | bytes 4718600 | tf_op jit(solution)/shard_map/ppermute | solution.py:483
  247.5 68.6 %collective-permute-start.35 = (bf16[128,48,128]{2,1,0:T(8,128)(2,1)}, bf16[128,48,128]{2,1,0:T(8,128)(2,1)}, u32[]{:S(2)}, u32[]{:S(2)}) collective-permute-start(bf16[128,48,128]{2,1,0:T(8,128)(2,1)} %get-tuple-element.139.refs_6_), channel_id=1, source_target_pairs={{0,4},{4,0},{8,12},{12,8},{16,20},{20,16},{24,28},{28,24},{1,5},{5... | collective-permute-start | bytes 4718600 | tf_op jit(solution)/shard_map/ppermute | solution.py:483
  247.6 1.4 copy-start.3
  276.1 48.4 %collective-permute-start.34 = (bf16[128,48,128]{2,1,0:T(8,128)(2,1)}, bf16[128,48,128]{2,1,0:T(8,128)(2,1)}, u32[]{:S(2)}, u32[]{:S(2)}) collective-permute-start(bf16[128,48,128]{2,1,0:T(8,128)(2,1)} %get-tuple-element.138.refs_6_), channel_id=1, source_target_pairs={{0,4},{4,0},{8,12},{12,8},{16,20},{20,16},{24,28},{28,24},{1,5},{5... | collective-permute-start | bytes 4718600 | tf_op jit(solution)/shard_map/ppermute | solution.py:483
  276.3 66.8 %collective-permute-start.31 = (bf16[128,48,128]{2,1,0:T(8,128)(2,1)}, bf16[128,48,128]{2,1,0:T(8,128)(2,1)S(1)}, u32[]{:S(2)}, u32[]{:S(2)}) collective-permute-start(bf16[128,48,128]{2,1,0:T(8,128)(2,1)} %get-tuple-element.138.refs_6_), channel_id=1, source_target_pairs={{16,24},{20,28},{8,0},{12,4},{17,25},{21,29},{9,1},{13,5},{18,26},... | collective-permute-start | bytes 4718600 | tf_op jit(solution)/shard_map/ppermute | solution.py:531
  305.6 27.8 %collective-permute-start.33 = (bf16[128,48,128]{2,1,0:T(8,128)(2,1)}, bf16[128,48,128]{2,1,0:T(8,128)(2,1)S(1)}, u32[]{:S(2)}, u32[]{:S(2)}) collective-permute-start(bf16[128,48,128]{2,1,0:T(8,128)(2,1)} %collective-permute-done.32.refs_9_.refs_6_), channel_id=1, source_target_pairs={{0,4},{4,0},{8,12},{12,8},{16,20},{20,16},{24,28},{28,24},{1,5},{5... | collective-permute-start | bytes 4718600 | tf_op jit(solution)/shard_map/ppermute | solution.py:483
  305.6 1.4 copy-start.6
  307.0 9.1 %copy-start.4 = (bf16[128,48,128]{2,1,0:T(8,128)(2,1)S(1)}, bf16[128,48,128]{2,1,0:T(8,128)(2,1)}, u32[]{:S(2)}) copy-start(bf16[128,48,128]{2,1,0:T(8,128)(2,1)} %copy-done.2) | copy-start | bytes 4718596
  316.1 8.4 %copy-start.7 = (bf16[128,48,128]{2,1,0:T(8,128)(2,1)S(1)}, bf16[128,48,128]{2,1,0:T(8,128)(2,1)}, u32[]{:S(2)}) copy-start(bf16[128,48,128]{2,1,0:T(8,128)(2,1)} %copy-done.5) | copy-start | bytes 4718596
  333.4 1.2 copy-start.18
  343.7 3.6 collective-permute-start.38
  347.3 1.2 copy-start.19
Sparse Core Ops, SparseCore 0:
  35.0 83.9 all-gather.2

commit v3 on v2

--- a/solution.py
+++ b/solution.py
@@ -541,8 +541,9 @@
     (early,) = gate(order, here, [early])
     early = lax.all_to_all(jnp.swapaxes(early, 0, 1), "chan", split_axis=0, concat_axis=0, tiled=True)
     gate(order, here, [], [lines[cut][kind][1] for cut in range(cuts) for kind in range(2)], micros=HOP_MICROS)
+    other = swap(early)
     early = merge_early(order, here, early)
-    heads = [early, swap(early)]
+    heads = [early, merge_early(order, here, other)]
     turned = [turn(order, here, value) for value in plain]
     head_turned = turn(order, here, early)
     lefts = [((early, plain[cut]), (head_turned, turned[cut])) for cut in range(cuts)]

time: 365 us -> 362 us (level)
  Pallas kernels: 148 us -> 157 us
  local copies, waits for them, and re-layouts: 20.7 us -> 13.7 us
  waiting for transfers between devices: 127 us -> 121 us
    pallas_call x28 -> x29, Pallas kernels: 148 us -> 157 us  [call(): pl.pallas_call(wrapped, out_shape=[*out_shape, jax.ShapeDtypeStruct((8, L...]
    unnamed x40 -> x32, local copies, waits for them, and re-layouts: 17.8 us -> 10.8 us
    ppermute x11, waiting for transfers between devices: 9.07 us -> 3.06 us  [swap(): return lax.ppermute(value, 'tile', [(i, i ^ 1) for i in range(tiles)])]
  transfers between devices with their start and end apart: 41 -> 41, of which waited for: 12 -> 11; matrix products, arithmetic and copies ran while one was open for 1% -> 1% of each run, Pallas kernels for 33% -> 38%
where the time goes in v3:
time: 362 us; the launch traced here: 361 us
  Pallas kernels  157 us (43%)
  waiting for transfers between devices  121 us (33%)
  starting transfers between devices  54.9 us (15%)
  between operations  13.8 us (4%)
  local copies, waits for them, and re-layouts  13.7 us (4%)
    pallas_call x29, Pallas kernels, call(): pl.pallas_call(wrapped, out_shape=[*out_shape, jax.ShapeDtypeStruct((8, L...  157 us
    ppermute x8, waiting for transfers between devices, along(): return lax.ppermute(value, 'tile', pairs)  63.3 us
    ppermute x2, waiting for transfers between devices, step(): lax.ppermute(up[hop - 1], 'tile', [(2 * g + c, 2 * h + c) for g, h in pai...  28 us
    ppermute x18, waiting for transfers between devices, exchange(): lax.ppermute(pieces[slot], 'chan', [(i, i ^ slot) for i in range(count)])  26.8 us
    ppermute x18, starting transfers between devices, exchange(): lax.ppermute(pieces[slot], 'chan', [(i, i ^ slot) for i in range(count)])  25.6 us
    ppermute x8, starting transfers between devices, along(): return lax.ppermute(value, 'tile', pairs)  19.5 us
    unnamed x32, local copies, waits for them, and re-layouts  10.8 us
  transfers between devices with their start and end apart: 41, of which 11 were waited for; matrix products, arithmetic and copies ran while one was open for 1% of the time, Pallas kernels for 38%

profile of v3, /device:TPU:0, one launch (start us, length us, event | category | flops | bytes accessed | tf_op | source)
XLA Modules:
  0.0 360.6 jit_solution(13692420640634166228)
XLA Ops:
  6.6 3.3 convert.3
  9.9 3.0 collective-permute-start
  13.0 1.6 collective-permute-start.1
  14.5 3.3 convert.4
  17.9 4.6 %history.1 = (bf16[4,4,16,2048]{3,2,1,0:T(8,128)(2,1)S(1)}, f32[8,128]{1,0:T(8,128)S(1)}) custom-call(s32[3]{0:T(128)S(1)} %pad_add_fusion.place_ref, s32[64,30720]{1,0:T(8,128)} %refs_0_.10, f32[8,128]{1,0:T(8,128)S(1)} %get-tuple-element.82.refs_1_), custom_call_target="tpu_custom_call" | custom-call | flops 5175000064 | tf_op jit(solution)/shard_map/history/pallas_call | solution.py:49
  22.5 4.6 %convert.5 = (bf16[2,4,16,2048]{3,2,1,0:T(8,128)(2,1)S(1)}, bf16[2,4,16,2048]{3,2,1,0:T(8,128)(2,1)S(1)}, bf16[2,4,16,2048]{3,2,1,0:T(8,128)(2,1)S(1)}, bf16[2,4,16,2048]{3,2,1,0:T(8,128)(2,1)S(1)}, f32[8,128]{1,0:T(8,128)S(1)}) custom-call(s32[3]{0:T(128)S(1)} %pad_add_fusion.place_ref, s32[64,32768]{1,0:T(8,128)} %refs_0_.11, ...), custom_call_target="tpu_custom_call" | custom-call | flops 5750000128 | tf_op jit(solution)/shard_map/convert/pallas_call | solution.py:49
  27.1 7.7 %channelize.4 = (bf16[4,4,256,128]{3,2,1,0:T(8,128)(2,1)}, f32[8,128]{1,0:T(8,128)S(1)}) custom-call(s32[3]{0:T(128)S(1)} %pad_add_fusion.place_ref, s32[16,2048]{1,0:T(8,128)S(1)} %copy-done.9, bf16[4,4,16,2048]{3,2,1,0:T(8,128)(2,1)S(1)} %get-tuple-element.83.refs_1_, bf16[1,4,16,2048]{3,2,1,0:T(8,128)(2,1)S(1)} %get-tuple-element.84.refs_2_, ...), custom_call_target="tpu_custom_call" | custom-call | flops 10350000128 | tf_op jit(solution)/shard_map/channelize/pallas_call | solution.py:49
  34.8 2.1 collective-permute-start.6
  36.9 1.7 collective-permute-start.7
  38.6 1.8 collective-permute-start.3
  40.4 1.7 collective-permute-start.4
  42.1 2.1 collective-permute-done.6.refs_3_
  44.1 3.1 collective-permute-start.5
  47.3 4.5 %collective-permute-done.7.refs_4_ = bf16[1,4,16,2048]{3,2,1,0:T(8,128)(2,1)S(1)} collective-permute-done((bf16[1,4,16,2048]{3,2,1,0:T(8,128)(2,1)S(1)}, bf16[1,4,16,2048]{3,2,1,0:T(8,128)(2,1)S(1)}, u32[]{:S(2)}, u32[]{:S(2)}) %collective-permute-start.7) | collective-permute-done | bytes 262176 | tf_op jit(solution)/shard_map/ppermute | solution.py:457
  53.0 6.7 %channelize.5 = (bf16[4,256,128]{2,1,0:T(8,128)(2,1)S(1)}, bf16[4,256,128]{2,1,0:T(8,128)(2,1)S(1)}, bf16[4,256,128]{2,1,0:T(8,128)(2,1)S(1)}, bf16[4,256,128]{2,1,0:T(8,128)(2,1)S(1)}, f32[8,128]{1,0:T(8,128)S(1)}) custom-call(s32[3]{0:T(128)S(1)} %pad_add_fusion.place_ref, s32[16,2048]{1,0:T(8,128)S(1)} %copy-done.9, ...), custom_call_target="tpu_custom_call" | custom-call | flops 10350000128 | tf_op jit(solution)/shard_map/channelize/pallas_call | solution.py:49
  59.7 1.7 collective-permute-start.10
  63.3 16.6 %collective-permute-done.4.refs_4_ = bf16[2,4,16,2048]{3,2,1,0:T(8,128)(2,1)S(1)} collective-permute-done((bf16[2,4,16,2048]{3,2,1,0:T(8,128)(2,1)S(1)}, bf16[2,4,16,2048]{3,2,1,0:T(8,128)(2,1)S(1)}, u32[]{:S(2)}, u32[]{:S(2)}) %collective-permute-start.4) | collective-permute-done | bytes 524320 | tf_op jit(solution)/shard_map/ppermute | solution.py:457
  79.9 6.8 %channelize.6 = (bf16[4,256,128]{2,1,0:T(8,128)(2,1)S(1)}, bf16[4,256,128]{2,1,0:T(8,128)(2,1)S(1)}, bf16[4,256,128]{2,1,0:T(8,128)(2,1)S(1)}, bf16[4,256,128]{2,1,0:T(8,128)(2,1)S(1)}, f32[8,128]{1,0:T(8,128)S(1)}) custom-call(s32[3]{0:T(128)S(1)} %pad_add_fusion.place_ref, s32[16,2048]{1,0:T(8,128)S(1)} %copy-done.9, ...), custom_call_target="tpu_custom_call" | custom-call | flops 10350000128 | tf_op jit(solution)/shard_map/channelize/pallas_call | solution.py:49
  86.7 2.1 collective-permute-start.16
  88.8 1.4 collective-permute-start.17
  90.2 3.0 merge.3
  93.2 6.8 %channelize.7 = (bf16[4,256,128]{2,1,0:T(8,128)(2,1)S(1)}, bf16[4,256,128]{2,1,0:T(8,128)(2,1)S(1)}, bf16[4,256,128]{2,1,0:T(8,128)(2,1)S(1)}, bf16[4,256,128]{2,1,0:T(8,128)(2,1)S(1)}, f32[8,128]{1,0:T(8,128)S(1)}) custom-call(s32[3]{0:T(128)S(1)} %pad_add_fusion.place_ref, s32[16,2048]{1,0:T(8,128)S(1)} %copy-done.9, ...), custom_call_target="tpu_custom_call" | custom-call | flops 10350000128 | tf_op jit(solution)/shard_map/channelize/pallas_call | solution.py:49
  102.0 1.5 collective-permute-start.14
  103.5 3.2 merge.4
  106.7 3.6 %collective-permute-done.13.refs_2_ = bf16[4,256,128]{2,1,0:T(8,128)(2,1)S(1)} collective-permute-done((bf16[4,256,128]{2,1,0:T(8,128)(2,1)S(1)}, bf16[4,256,128]{2,1,0:T(8,128)(2,1)S(1)}, u32[]{:S(2)}, u32[]{:S(2)}) %collective-permute-start.13) | collective-permute-done | bytes 262176 | tf_op jit(solution)/shard_map/ppermute | solution.py:457
  110.3 3.0 merge.5
  113.3 4.5 %collective-permute-start.18 = (bf16[128,48,128]{2,1,0:T(8,128)(2,1)S(1)}, bf16[128,48,128]{2,1,0:T(8,128)(2,1)}, u32[]{:S(2)}, u32[]{:S(2)}) collective-permute-start(bf16[128,48,128]{2,1,0:T(8,128)(2,1)S(1)} %get-tuple-element.123.refs_0_.refs_1_.refs_6_), channel_id=1, source_target_pairs={{0,8},{4,12},{8,16},{12,20},{16,24},{20,28},{1,9},{5,13},{9,17},{1... | collective-permute-start | bytes 4718600 | tf_op jit(solution)/shard_map/ppermute | solution.py:480
  117.8 1.3 collective-permute-start.19
  119.1 5.7 %collective-permute-start.20 = (bf16[128,48,128]{2,1,0:T(8,128)(2,1)}, bf16[128,48,128]{2,1,0:T(8,128)(2,1)}, u32[]{:S(2)}, u32[]{:S(2)}) collective-permute-start(bf16[128,48,128]{2,1,0:T(8,128)(2,1)} %get-tuple-element.124.refs_0_.refs_1_.refs_6_), channel_id=1, source_target_pairs={{0,8},{4,12},{8,16},{12,20},{16,24},{20,28},{1,9},{5,13},{9,17},{1... | collective-permute-start | bytes 4718600 | tf_op jit(solution)/shard_map/ppermute | solution.py:480
  124.9 1.3 collective-permute-start.21
  126.4 2.2 copy-done.8
  129.1 2.5 copy.21
  131.6 4.9 %all-to-all-start = ((bf16[4,4,4,256,128]{4,3,2,1,0:T(8,128)(2,1)}), bf16[4,4,4,256,128]{4,3,2,1,0:T(8,128)(2,1)}, u32[]{:S(2)}, u32[]{:S(2)}) async-start(bf16[4,4,4,256,128]{4,3,2,1,0:T(8,128)(2,1)} %bitcast.15), calls=%async_computation | async-start | bytes 8388608 | tf_op jit(solution)/shard_map/all_to_all | solution.py:542
  136.5 15.0 %collective-permute-done.18.refs_0_.refs_6_ = bf16[128,48,128]{2,1,0:T(8,128)(2,1)} collective-permute-done((bf16[128,48,128]{2,1,0:T(8,128)(2,1)S(1)}, bf16[128,48,128]{2,1,0:T(8,128)(2,1)}, u32[]{:S(2)}, u32[]{:S(2)}) %collective-permute-start.18) | collective-permute-done | bytes 1572896 | tf_op jit(solution)/shard_map/ppermute | solution.py:480
  151.5 5.6 %collective-permute-done.19.refs_1_.refs_8_ = bf16[128,48,128]{2,1,0:T(8,128)(2,1)} collective-permute-done((bf16[128,48,128]{2,1,0:T(8,128)(2,1)S(1)}, bf16[128,48,128]{2,1,0:T(8,128)(2,1)}, u32[]{:S(2)}, u32[]{:S(2)}) %collective-permute-start.19) | collective-permute-done | bytes 1572896 | tf_op jit(solution)/shard_map/ppermute | solution.py:480
  157.2 1.8 collective-permute-start.29
  159.0 22.2 %collective-permute-done.20.refs_2_.refs_6_ = bf16[128,48,128]{2,1,0:T(8,128)(2,1)} collective-permute-done((bf16[128,48,128]{2,1,0:T(8,128)(2,1)}, bf16[128,48,128]{2,1,0:T(8,128)(2,1)}, u32[]{:S(2)}, u32[]{:S(2)}) %collective-permute-start.20) | collective-permute-done | bytes 1572896 | tf_op jit(solution)/shard_map/ppermute | solution.py:480
  181.2 1.3 collective-permute-start.30
  182.5 4.3 %collective-permute-done.21.refs_3_.refs_8_ = bf16[128,48,128]{2,1,0:T(8,128)(2,1)} collective-permute-done((bf16[128,48,128]{2,1,0:T(8,128)(2,1)}, bf16[128,48,128]{2,1,0:T(8,128)(2,1)}, u32[]{:S(2)}, u32[]{:S(2)}) %collective-permute-start.21) | collective-permute-done | bytes 1572896 | tf_op jit(solution)/shard_map/ppermute | solution.py:480
  187.4 7.9 %merge_early.2 = (bf16[4,256,16,128]{3,2,1,0:T(8,128)(2,1)S(1)}, f32[8,128]{1,0:T(8,128)S(1)}) custom-call(s32[3]{0:T(128)S(1)} %pad_add_fusion.place_ref, bf16[4,4,4,256,128]{4,3,2,1,0:T(8,128)(2,1)} %all-to-all-done.refs_0_, f32[8,128]{1,0:T(8,128)S(1)} %gate.4.refs_1_), custom_call_target="tpu_custom_call" | custom-call | flops 46000001024 | tf_op jit(solution)/shard_map/merge_early/pallas_call | solution.py:49
  196.0 2.3 collective-permute-start.23
  198.5 7.9 %merge_early.3 = (bf16[4,256,16,128]{3,2,1,0:T(8,128)(2,1)S(1)}, f32[8,128]{1,0:T(8,128)S(1)}) custom-call(s32[3]{0:T(128)S(1)} %pad_add_fusion.place_ref, bf16[4,4,4,256,128]{4,3,2,1,0:T(8,128)(2,1)} %copy-done.15, f32[8,128]{1,0:T(8,128)S(1)} %get-tuple-element.127.refs_1_), custom_call_target="tpu_custom_call" | custom-call | flops 46000001024 | tf_op jit(solution)/shard_map/merge_early/pallas_call | solution.py:49
  206.4 2.0 copy-done.1
  208.4 1.6 turn.3
  210.1 5.0 %turn.4 = (bf16[128,48,128]{2,1,0:T(8,128)(2,1)S(1)}, f32[8,128]{1,0:T(8,128)S(1)}) custom-call(s32[3]{0:T(128)S(1)} %pad_add_fusion.place_ref, bf16[128,48,128]{2,1,0:T(8,128)(2,1)} %get-tuple-element.124.refs_0_.refs_1_.refs_6_, f32[8,128]{1,0:T(8,128)S(1)} %get-tuple-element.129.refs_1_), custom_call_target="tpu_custom_call" | custom-call | flops 115000000 | tf_op jit(solution)/shard_map/turn/pallas_call | solution.py:49
  215.1 2.2 turn.5
  217.2 8.1 %correlate.8 = (f32[2,256,64,512]{3,2,1,0:T(8,128)}, f32[8,128]{1,0:T(8,128)S(1)}) custom-call(s32[5]{0:T(128)S(1)} %stack.44.place_ref, bf16[4,256,16,128]{3,2,1,0:T(8,128)(2,1)} %copy-done, bf16[128,48,128]{2,1,0:T(8,128)(2,1)S(1)} %get-tuple-element.123.refs_0_.refs_1_.refs_6_, bf16[256,16,128]{2,1,0:T(8,128)(2,1)S(1)} %get-tuple-element.131.refs_2_, ...), custom_call_target="tpu_custom_call" | custom-call | flops 1150000000 | tf_op jit(solution)/shard_map/correlate/pallas_call | solution.py:49
  225.3 1.3 collective-permute-start.24
  226.6 9.1 %correlate.9 = (f32[2,256,64,512]{3,2,1,0:T(8,128)}, f32[8,128]{1,0:T(8,128)S(1)}) custom-call(s32[5]{0:T(128)S(1)} %stack.44.place_ref, bf16[4,256,16,128]{3,2,1,0:T(8,128)(2,1)} %copy-done, bf16[128,48,128]{2,1,0:T(8,128)(2,1)} %get-tuple-element.124.refs_0_.refs_1_.refs_6_, ...), custom_call_target="tpu_custom_call", output_to_operand_aliasing={{0}: (9, {})} | custom-call | flops 1150000000 | tf_op jit(solution)/shard_map/correlate/pallas_call | solution.py:49
  236.2 4.3 %select.6 = (bf16[128,48,128]{2,1,0:T(8,128)(2,1)}, f32[8,128]{1,0:T(8,128)S(1)}) custom-call(s32[5]{0:T(128)S(1)} %stack.40.place_ref, bf16[128,48,128]{2,1,0:T(8,128)(2,1)} %collective-permute-done.29.refs_0_, bf16[128,48,128]{2,1,0:T(8,128)(2,1)} %collective-permute-done.30.refs_1_, f32[8,128]{1,0:T(8,128)S(1)} %get-tuple-element.139.refs_2_), custom_call_target="tpu_custom_call" | custom-call | flops 1150000000 | tf_op jit(solution)/shard_map/select/pallas_call | solution.py:49
  240.5 1.3 collective-permute-start.32
  242.4 1.4 copy-done.3
  243.8 8.6 %correlate.10 = (f32[2,256,64,512]{3,2,1,0:T(8,128)}, f32[8,128]{1,0:T(8,128)S(1)}) custom-call(s32[5]{0:T(128)S(1)} %stack.43.place_ref, bf16[4,256,16,128]{3,2,1,0:T(8,128)(2,1)} %copy-done, bf16[128,48,128]{2,1,0:T(8,128)(2,1)S(1)} %get-tuple-element.123.refs_0_.refs_1_.refs_6_, ...), custom_call_target="tpu_custom_call", output_to_operand_aliasing={{0}: (11, {})} | custom-call | flops 8049999872 | tf_op jit(solution)/shard_map/correlate/pallas_call | solution.py:49
  252.4 16.2 %collective-permute-done.24.refs_1_ = bf16[128,48,128]{2,1,0:T(8,128)(2,1)} collective-permute-done((bf16[128,48,128]{2,1,0:T(8,128)(2,1)}, bf16[128,48,128]{2,1,0:T(8,128)(2,1)}, u32[]{:S(2)}, u32[]{:S(2)}) %collective-permute-start.24) | collective-permute-done | bytes 1572896 | tf_op jit(solution)/shard_map/ppermute | solution.py:480
  268.6 4.2 %select.7 = (bf16[128,48,128]{2,1,0:T(8,128)(2,1)}, f32[8,128]{1,0:T(8,128)S(1)}) custom-call(s32[5]{0:T(128)S(1)} %stack.40.place_ref, bf16[128,48,128]{2,1,0:T(8,128)(2,1)} %collective-permute-done.23.refs_0_, bf16[128,48,128]{2,1,0:T(8,128)(2,1)} %collective-permute-done.24.refs_1_, f32[8,128]{1,0:T(8,128)S(1)} %get-tuple-element.141.refs_2_), custom_call_target="tpu_custom_call" | custom-call | flops 1150000000 | tf_op jit(solution)/shard_map/select/pallas_call | solution.py:49
  273.0 1.3 collective-permute-start.31
  274.2 28.0 %collective-permute-done.32.refs_9_.refs_6_ = bf16[128,48,128]{2,1,0:T(8,128)(2,1)} collective-permute-done((bf16[128,48,128]{2,1,0:T(8,128)(2,1)}, bf16[128,48,128]{2,1,0:T(8,128)(2,1)}, u32[]{:S(2)}, u32[]{:S(2)}) %collective-permute-start.32) | collective-permute-done | bytes 1572896 | tf_op jit(solution)/shard_map/ppermute | solution.py:531
  302.3 1.4 copy-done.6
  303.7 9.1 %correlate.11 = (f32[2,256,64,512]{3,2,1,0:T(8,128)}, f32[8,128]{1,0:T(8,128)S(1)}) custom-call(s32[5]{0:T(128)S(1)} %stack.43.place_ref, bf16[4,256,16,128]{3,2,1,0:T(8,128)(2,1)} %copy-done, bf16[128,48,128]{2,1,0:T(8,128)(2,1)} %get-tuple-element.124.refs_0_.refs_1_.refs_6_, ...), custom_call_target="tpu_custom_call", output_to_operand_aliasing={{0}: (11, {})} | custom-call | flops 8049999872 | tf_op jit(solution)/shard_map/correlate/pallas_call | solution.py:49
  312.8 8.4 %correlate.12 = (f32[2,256,64,512]{3,2,1,0:T(8,128)}, f32[8,128]{1,0:T(8,128)S(1)}) custom-call(s32[5]{0:T(128)S(1)} %stack.47.place_ref, bf16[4,256,16,128]{3,2,1,0:T(8,128)(2,1)} %copy-done, bf16[128,48,128]{2,1,0:T(8,128)(2,1)S(1)} %get-tuple-element.123.refs_0_.refs_1_.refs_6_, ...), custom_call_target="tpu_custom_call", output_to_operand_aliasing={{0}: (9, {})} | custom-call | flops 8049999872 | tf_op jit(solution)/shard_map/correlate/pallas_call | solution.py:49
  321.2 8.9 %correlate.13 = (f32[2,256,64,512]{3,2,1,0:T(8,128)}, f32[8,128]{1,0:T(8,128)S(1)}) custom-call(s32[5]{0:T(128)S(1)} %stack.47.place_ref, bf16[4,256,16,128]{3,2,1,0:T(8,128)(2,1)} %copy-done, bf16[128,48,128]{2,1,0:T(8,128)(2,1)} %get-tuple-element.124.refs_0_.refs_1_.refs_6_, ...), custom_call_target="tpu_custom_call", output_to_operand_aliasing={{0}: (9, {})} | custom-call | flops 8049999872 | tf_op jit(solution)/shard_map/correlate/pallas_call | solution.py:49
  331.3 8.6 %correlate.14 = (f32[2,256,64,512]{3,2,1,0:T(8,128)}, f32[8,128]{1,0:T(8,128)S(1)}) custom-call(s32[5]{0:T(128)S(1)} %stack.37.place_ref, bf16[4,256,16,128]{3,2,1,0:T(8,128)(2,1)} %copy-done, bf16[128,48,128]{2,1,0:T(8,128)(2,1)S(1)} %get-tuple-element.123.refs_0_.refs_1_.refs_6_, ...), custom_call_target="tpu_custom_call", output_to_operand_aliasing={{0}: (11, {})} | custom-call | flops 8049999872 | tf_op jit(solution)/shard_map/correlate/pallas_call | solution.py:49
  341.0 3.0 collective-permute-done.38.refs_7_
  345.2 8.6 %correlate.15 = (f32[2,256,64,512]{3,2,1,0:T(8,128)}, f32[8,128]{1,0:T(8,128)}) custom-call(s32[5]{0:T(128)S(1)} %stack.37.place_ref, bf16[4,256,16,128]{3,2,1,0:T(8,128)(2,1)} %copy-done, bf16[128,48,128]{2,1,0:T(8,128)(2,1)} %get-tuple-element.124.refs_0_.refs_1_.refs_6_, ...), custom_call_target="tpu_custom_call", output_to_operand_aliasing={{0}: (11, {})} | custom-call | flops 8049999872 | tf_op jit(solution)/shard_map/correlate/pallas_call | solution.py:49
  (87 shorter events, 12.4 us)
Async XLA Ops:
  6.5 119.8 %all-gather.3.cloned.1.call-start = ((), (), s32[]{:S(2)}) async-start(), calls=%async_computation.1 | async-start | bytes 5242880 | tf_op jit(solution)/shard_map/all_gather | solution.py:513
  9.9 17.1 %collective-permute-start = (bf16[1,4,16,2048]{3,2,1,0:T(8,128)(2,1)S(1)}, bf16[1,4,16,2048]{3,2,1,0:T(8,128)(2,1)S(1)}, u32[]{:S(2)}, u32[]{:S(2)}) collective-permute-start(bf16[1,4,16,2048]{3,2,1,0:T(8,128)(2,1)S(1)} %get-tuple-element.85), channel_id=1, source_target_pairs={{0,1},{1,0},{2,3},{3,2},{4,5},{5,4},{6,7},{7,6},{8,9},{9,8},{10,11... | collective-permute-start | bytes 786440 | tf_op jit(solution)/shard_map/ppermute | solution.py:457
  13.0 14.1 %collective-permute-start.1 = (bf16[1,4,16,2048]{3,2,1,0:T(8,128)(2,1)S(1)}, bf16[1,4,16,2048]{3,2,1,0:T(8,128)(2,1)S(1)}, u32[]{:S(2)}, u32[]{:S(2)}) collective-permute-start(bf16[1,4,16,2048]{3,2,1,0:T(8,128)(2,1)S(1)} %get-tuple-element.86), channel_id=1, source_target_pairs={{0,2},{1,3},{2,0},{3,1},{4,6},{5,7},{6,4},{7,5},{8,10},{9,11},{10,... | collective-permute-start | bytes 786440 | tf_op jit(solution)/shard_map/ppermute | solution.py:457
  14.5 12.6 %collective-permute-start.2 = (bf16[1,4,16,2048]{3,2,1,0:T(8,128)(2,1)S(1)}, bf16[1,4,16,2048]{3,2,1,0:T(8,128)(2,1)S(1)}, u32[]{:S(2)}, u32[]{:S(2)}) collective-permute-start(bf16[1,4,16,2048]{3,2,1,0:T(8,128)(2,1)S(1)} %get-tuple-element.87), channel_id=1, source_target_pairs={{0,3},{1,2},{2,1},{3,0},{4,7},{5,6},{6,5},{7,4},{8,11},{9,10},{10,... | collective-permute-start | bytes 786440 | tf_op jit(solution)/shard_map/ppermute | solution.py:457
  22.5 4.6 %copy-start.10 = (bf16[4,4,16,2048]{3,2,1,0:T(8,128)(2,1)}, bf16[4,4,16,2048]{3,2,1,0:T(8,128)(2,1)S(1)}, u32[]{:S(2)}) copy-start(bf16[4,4,16,2048]{3,2,1,0:T(8,128)(2,1)S(1)} %get-tuple-element.83.refs_1_) | copy-start | bytes 3145732
  22.5 4.6 %copy-start.9 = (s32[16,2048]{1,0:T(8,128)S(1)}, s32[16,2048]{1,0:T(8,128)}, u32[]{:S(2)}) copy-start(s32[16,2048]{1,0:T(8,128)} %refs_0_.15) | copy-start | bytes 393220
  34.8 9.3 %collective-permute-start.6 = (bf16[1,4,16,2048]{3,2,1,0:T(8,128)(2,1)S(1)}, bf16[1,4,16,2048]{3,2,1,0:T(8,128)(2,1)S(1)}, u32[]{:S(2)}, u32[]{:S(2)}) collective-permute-start(bf16[1,4,16,2048]{3,2,1,0:T(8,128)(2,1)S(1)} %get-tuple-element.96), channel_id=1, source_target_pairs={{0,1},{1,0},{2,3},{3,2},{4,5},{5,4},{6,7},{7,6},{8,9},{9,8},{10,11... | collective-permute-start | bytes 786440 | tf_op jit(solution)/shard_map/ppermute | solution.py:457
  36.9 14.9 %collective-permute-start.7 = (bf16[1,4,16,2048]{3,2,1,0:T(8,128)(2,1)S(1)}, bf16[1,4,16,2048]{3,2,1,0:T(8,128)(2,1)S(1)}, u32[]{:S(2)}, u32[]{:S(2)}) collective-permute-start(bf16[1,4,16,2048]{3,2,1,0:T(8,128)(2,1)S(1)} %get-tuple-element.97), channel_id=1, source_target_pairs={{0,2},{1,3},{2,0},{3,1},{4,6},{5,7},{6,4},{7,5},{8,10},{9,11},{10,... | collective-permute-start | bytes 786440 | tf_op jit(solution)/shard_map/ppermute | solution.py:457
  38.6 13.2 %collective-permute-start.8 = (bf16[1,4,16,2048]{3,2,1,0:T(8,128)(2,1)S(1)}, bf16[1,4,16,2048]{3,2,1,0:T(8,128)(2,1)S(1)}, u32[]{:S(2)}, u32[]{:S(2)}) collective-permute-start(bf16[1,4,16,2048]{3,2,1,0:T(8,128)(2,1)S(1)} %get-tuple-element.98), channel_id=1, source_target_pairs={{0,3},{1,2},{2,1},{3,0},{4,7},{5,6},{6,5},{7,4},{8,11},{9,10},{10,... | collective-permute-start | bytes 786440 | tf_op jit(solution)/shard_map/ppermute | solution.py:457
  38.6 23.8 %collective-permute-start.3 = (bf16[2,4,16,2048]{3,2,1,0:T(8,128)(2,1)S(1)}, bf16[2,4,16,2048]{3,2,1,0:T(8,128)(2,1)S(1)}, u32[]{:S(2)}, u32[]{:S(2)}) collective-permute-start(bf16[2,4,16,2048]{3,2,1,0:T(8,128)(2,1)S(1)} %get-tuple-element.92), channel_id=1, source_target_pairs={{0,1},{1,0},{2,3},{3,2},{4,5},{5,4},{6,7},{7,6},{8,9},{9,8},{10,11... | collective-permute-start | bytes 1572872 | tf_op jit(solution)/shard_map/ppermute | solution.py:457
  40.4 39.5 %collective-permute-start.4 = (bf16[2,4,16,2048]{3,2,1,0:T(8,128)(2,1)S(1)}, bf16[2,4,16,2048]{3,2,1,0:T(8,128)(2,1)S(1)}, u32[]{:S(2)}, u32[]{:S(2)}) collective-permute-start(bf16[2,4,16,2048]{3,2,1,0:T(8,128)(2,1)S(1)} %get-tuple-element.93), channel_id=1, source_target_pairs={{0,2},{1,3},{2,0},{3,1},{4,6},{5,7},{6,4},{7,5},{8,10},{9,11},{10,... | collective-permute-start | bytes 1572872 | tf_op jit(solution)/shard_map/ppermute | solution.py:457
  44.1 35.7 %collective-permute-start.5 = (bf16[2,4,16,2048]{3,2,1,0:T(8,128)(2,1)S(1)}, bf16[2,4,16,2048]{3,2,1,0:T(8,128)(2,1)S(1)}, u32[]{:S(2)}, u32[]{:S(2)}) collective-permute-start(bf16[2,4,16,2048]{3,2,1,0:T(8,128)(2,1)S(1)} %get-tuple-element.94), channel_id=1, source_target_pairs={{0,3},{1,2},{2,1},{3,0},{4,7},{5,6},{6,5},{7,4},{8,11},{9,10},{10,... | collective-permute-start | bytes 1572872 | tf_op jit(solution)/shard_map/ppermute | solution.py:457
  51.8 1.2 copy-start.11
  53.0 26.9 %copy-start.12 = (bf16[4,4,16,2048]{3,2,1,0:T(8,128)(2,1)S(1)}, bf16[4,4,16,2048]{3,2,1,0:T(8,128)(2,1)}, u32[]{:S(2)}) copy-start(bf16[4,4,16,2048]{3,2,1,0:T(8,128)(2,1)} %copy-done.10) | copy-start | bytes 3145732
  59.7 29.1 %collective-permute-start.10 = (bf16[4,256,128]{2,1,0:T(8,128)(2,1)S(1)}, bf16[4,256,128]{2,1,0:T(8,128)(2,1)S(1)}, u32[]{:S(2)}, u32[]{:S(2)}) collective-permute-start(bf16[4,256,128]{2,1,0:T(8,128)(2,1)S(1)} %get-tuple-element.102), channel_id=1, source_target_pairs={{0,2},{1,3},{2,0},{3,1},{4,6},{5,7},{6,4},{7,5},{8,10},{9,11},{10,... | collective-permute-start | bytes 786440 | tf_op jit(solution)/shard_map/ppermute | solution.py:457
  61.5 28.8 %collective-permute-start.11 = (bf16[4,256,128]{2,1,0:T(8,128)(2,1)S(1)}, bf16[4,256,128]{2,1,0:T(8,128)(2,1)S(1)}, u32[]{:S(2)}, u32[]{:S(2)}) collective-permute-start(bf16[4,256,128]{2,1,0:T(8,128)(2,1)S(1)} %get-tuple-element.103), channel_id=1, source_target_pairs={{0,3},{1,2},{2,1},{3,0},{4,7},{5,6},{6,5},{7,4},{8,11},{9,10},{10,... | collective-permute-start | bytes 786440 | tf_op jit(solution)/shard_map/ppermute | solution.py:457
  62.4 27.8 %collective-permute-start.9 = (bf16[4,256,128]{2,1,0:T(8,128)(2,1)S(1)}, bf16[4,256,128]{2,1,0:T(8,128)(2,1)S(1)}, u32[]{:S(2)}, u32[]{:S(2)}) collective-permute-start(bf16[4,256,128]{2,1,0:T(8,128)(2,1)S(1)} %get-tuple-element.101), channel_id=1, source_target_pairs={{0,1},{1,0},{2,3},{3,2},{4,5},{5,4},{6,7},{7,6},{8,9},{9,8},{10,11... | collective-permute-start | bytes 786440 | tf_op jit(solution)/shard_map/ppermute | solution.py:457
  86.7 15.4 %collective-permute-start.15 = (bf16[4,256,128]{2,1,0:T(8,128)(2,1)S(1)}, bf16[4,256,128]{2,1,0:T(8,128)(2,1)S(1)}, u32[]{:S(2)}, u32[]{:S(2)}) collective-permute-start(bf16[4,256,128]{2,1,0:T(8,128)(2,1)S(1)} %get-tuple-element.112), channel_id=1, source_target_pairs={{0,1},{1,0},{2,3},{3,2},{4,5},{5,4},{6,7},{7,6},{8,9},{9,8},{10,11... | collective-permute-start | bytes 786440 | tf_op jit(solution)/shard_map/ppermute | solution.py:457
  86.7 16.8 %collective-permute-start.16 = (bf16[4,256,128]{2,1,0:T(8,128)(2,1)S(1)}, bf16[4,256,128]{2,1,0:T(8,128)(2,1)S(1)}, u32[]{:S(2)}, u32[]{:S(2)}) collective-permute-start(bf16[4,256,128]{2,1,0:T(8,128)(2,1)S(1)} %get-tuple-element.113), channel_id=1, source_target_pairs={{0,2},{1,3},{2,0},{3,1},{4,6},{5,7},{6,4},{7,5},{8,10},{9,11},{10,... | collective-permute-start | bytes 786440 | tf_op jit(solution)/shard_map/ppermute | solution.py:457
  88.8 14.7 %collective-permute-start.17 = (bf16[4,256,128]{2,1,0:T(8,128)(2,1)S(1)}, bf16[4,256,128]{2,1,0:T(8,128)(2,1)S(1)}, u32[]{:S(2)}, u32[]{:S(2)}) collective-permute-start(bf16[4,256,128]{2,1,0:T(8,128)(2,1)S(1)} %get-tuple-element.114), channel_id=1, source_target_pairs={{0,3},{1,2},{2,1},{3,0},{4,7},{5,6},{6,5},{7,4},{8,11},{9,10},{10,... | collective-permute-start | bytes 786440 | tf_op jit(solution)/shard_map/ppermute | solution.py:457
  100.0 6.8 %collective-permute-start.12 = (bf16[4,256,128]{2,1,0:T(8,128)(2,1)S(1)}, bf16[4,256,128]{2,1,0:T(8,128)(2,1)S(1)}, u32[]{:S(2)}, u32[]{:S(2)}) collective-permute-start(bf16[4,256,128]{2,1,0:T(8,128)(2,1)S(1)} %get-tuple-element.108), channel_id=1, source_target_pairs={{0,1},{1,0},{2,3},{3,2},{4,5},{5,4},{6,7},{7,6},{8,9},{9,8},{10,11... | collective-permute-start | bytes 786440 | tf_op jit(solution)/shard_map/ppermute | solution.py:457
  101.2 9.2 %collective-permute-start.13 = (bf16[4,256,128]{2,1,0:T(8,128)(2,1)S(1)}, bf16[4,256,128]{2,1,0:T(8,128)(2,1)S(1)}, u32[]{:S(2)}, u32[]{:S(2)}) collective-permute-start(bf16[4,256,128]{2,1,0:T(8,128)(2,1)S(1)} %get-tuple-element.109), channel_id=1, source_target_pairs={{0,2},{1,3},{2,0},{3,1},{4,6},{5,7},{6,4},{7,5},{8,10},{9,11},{10,... | collective-permute-start | bytes 786440 | tf_op jit(solution)/shard_map/ppermute | solution.py:457
  102.0 8.3 %collective-permute-start.14 = (bf16[4,256,128]{2,1,0:T(8,128)(2,1)S(1)}, bf16[4,256,128]{2,1,0:T(8,128)(2,1)S(1)}, u32[]{:S(2)}, u32[]{:S(2)}) collective-permute-start(bf16[4,256,128]{2,1,0:T(8,128)(2,1)S(1)} %get-tuple-element.110), channel_id=1, source_target_pairs={{0,3},{1,2},{2,1},{3,0},{4,7},{5,6},{6,5},{7,4},{8,11},{9,10},{10,... | collective-permute-start | bytes 786440 | tf_op jit(solution)/shard_map/ppermute | solution.py:457
  113.3 38.2 %collective-permute-start.18 = (bf16[128,48,128]{2,1,0:T(8,128)(2,1)S(1)}, bf16[128,48,128]{2,1,0:T(8,128)(2,1)}, u32[]{:S(2)}, u32[]{:S(2)}) collective-permute-start(bf16[128,48,128]{2,1,0:T(8,128)(2,1)S(1)} %get-tuple-element.123.refs_0_.refs_1_.refs_6_), channel_id=1, source_target_pairs={{0,8},{4,12},{8,16},{12,20},{16,24},{20,28},{1,9},{5,13},{9,17},{1... | collective-permute-start | bytes 4718600 | tf_op jit(solution)/shard_map/ppermute | solution.py:480
  117.8 39.3 %collective-permute-start.19 = (bf16[128,48,128]{2,1,0:T(8,128)(2,1)S(1)}, bf16[128,48,128]{2,1,0:T(8,128)(2,1)}, u32[]{:S(2)}, u32[]{:S(2)}) collective-permute-start(bf16[128,48,128]{2,1,0:T(8,128)(2,1)S(1)} %get-tuple-element.123.refs_0_.refs_1_.refs_6_), channel_id=1, source_target_pairs={{8,0},{12,4},{16,8},{20,12},{24,16},{28,20},{9,1},{13,5},{17,9},{2... | collective-permute-start | bytes 4718600 | tf_op jit(solution)/shard_map/ppermute | solution.py:480
  119.1 62.0 %collective-permute-start.20 = (bf16[128,48,128]{2,1,0:T(8,128)(2,1)}, bf16[128,48,128]{2,1,0:T(8,128)(2,1)}, u32[]{:S(2)}, u32[]{:S(2)}) collective-permute-start(bf16[128,48,128]{2,1,0:T(8,128)(2,1)} %get-tuple-element.124.refs_0_.refs_1_.refs_6_), channel_id=1, source_target_pairs={{0,8},{4,12},{8,16},{12,20},{16,24},{20,28},{1,9},{5,13},{9,17},{1... | collective-permute-start | bytes 4718600 | tf_op jit(solution)/shard_map/ppermute | solution.py:480
  124.9 61.9 %collective-permute-start.21 = (bf16[128,48,128]{2,1,0:T(8,128)(2,1)}, bf16[128,48,128]{2,1,0:T(8,128)(2,1)}, u32[]{:S(2)}, u32[]{:S(2)}) collective-permute-start(bf16[128,48,128]{2,1,0:T(8,128)(2,1)} %get-tuple-element.124.refs_0_.refs_1_.refs_6_), channel_id=1, source_target_pairs={{8,0},{12,4},{16,8},{20,12},{24,16},{28,20},{9,1},{13,5},{17,9},{2... | collective-permute-start | bytes 4718600 | tf_op jit(solution)/shard_map/ppermute | solution.py:480
  126.3 69.0 %collective-permute-start.28 = (bf16[128,48,128]{2,1,0:T(8,128)(2,1)S(1)}, bf16[128,48,128]{2,1,0:T(8,128)(2,1)}, u32[]{:S(2)}, u32[]{:S(2)}) collective-permute-start(bf16[128,48,128]{2,1,0:T(8,128)(2,1)S(1)} %get-tuple-element.123.refs_0_.refs_1_.refs_6_), channel_id=1, source_target_pairs={{0,4},{4,0},{8,12},{12,8},{16,20},{20,16},{24,28},{28,24},{1,5},{5... | collective-permute-start | bytes 4718600 | tf_op jit(solution)/shard_map/ppermute | solution.py:483
  126.4 2.2 copy-start.8
  131.6 55.7 %all-to-all-start = ((bf16[4,4,4,256,128]{4,3,2,1,0:T(8,128)(2,1)}), bf16[4,4,4,256,128]{4,3,2,1,0:T(8,128)(2,1)}, u32[]{:S(2)}, u32[]{:S(2)}) async-start(bf16[4,4,4,256,128]{4,3,2,1,0:T(8,128)(2,1)} %bitcast.15), calls=%async_computation | async-start | bytes 8388608 | tf_op jit(solution)/shard_map/all_to_all | solution.py:542
  151.5 44.4 %collective-permute-start.27 = (bf16[128,48,128]{2,1,0:T(8,128)(2,1)}, bf16[128,48,128]{2,1,0:T(8,128)(2,1)}, u32[]{:S(2)}, u32[]{:S(2)}) collective-permute-start(bf16[128,48,128]{2,1,0:T(8,128)(2,1)} %get-tuple-element.124.refs_0_.refs_1_.refs_6_), channel_id=1, source_target_pairs={{0,4},{4,0},{8,12},{12,8},{16,20},{20,16},{24,28},{28,24},{1,5},{5... | collective-permute-start | bytes 4718600 | tf_op jit(solution)/shard_map/ppermute | solution.py:483
  157.2 68.1 %collective-permute-start.29 = (bf16[128,48,128]{2,1,0:T(8,128)(2,1)}, bf16[128,48,128]{2,1,0:T(8,128)(2,1)}, u32[]{:S(2)}, u32[]{:S(2)}) collective-permute-start(bf16[128,48,128]{2,1,0:T(8,128)(2,1)} %collective-permute-done.18.refs_0_.refs_6_), channel_id=1, source_target_pairs={{8,16},{12,20},{16,24},{20,28},{9,17},{13,21},{17,25},{21,29},{10,... | collective-permute-start | bytes 4718600 | tf_op jit(solution)/shard_map/ppermute | solution.py:480
  181.2 54.5 %collective-permute-start.30 = (bf16[128,48,128]{2,1,0:T(8,128)(2,1)}, bf16[128,48,128]{2,1,0:T(8,128)(2,1)}, u32[]{:S(2)}, u32[]{:S(2)}) collective-permute-start(bf16[128,48,128]{2,1,0:T(8,128)(2,1)} %collective-permute-done.19.refs_1_.refs_8_), channel_id=1, source_target_pairs={{8,0},{12,4},{16,8},{20,12},{9,1},{13,5},{17,9},{21,13},{10,2},{14... | collective-permute-start | bytes 4718600 | tf_op jit(solution)/shard_map/ppermute | solution.py:480
  187.3 8.7 %collective-permute-start.22 = (bf16[4,4,4,256,128]{4,3,2,1,0:T(8,128)(2,1)}, bf16[4,4,4,256,128]{4,3,2,1,0:T(8,128)(2,1)S(1)}, u32[]{:S(2)}, u32[]{:S(2)}) collective-permute-start(bf16[4,4,4,256,128]{4,3,2,1,0:T(8,128)(2,1)} %all-to-all-done.refs_0_), channel_id=1, source_target_pairs={{0,4},{4,0},{8,12},{12,8},{16,20},{20,16},{24,28},{28,24},{1,5},{5... | collective-permute-start | bytes 12582920 | tf_op jit(solution)/shard_map/ppermute | solution.py:483
  195.3 19.7 %copy-start = (bf16[4,256,16,128]{3,2,1,0:T(8,128)(2,1)}, bf16[4,256,16,128]{3,2,1,0:T(8,128)(2,1)S(1)}, u32[]{:S(2)}) copy-start(bf16[4,256,16,128]{3,2,1,0:T(8,128)(2,1)S(1)} %get-tuple-element.126.refs_0_.refs_4_) | copy-start | bytes 12582916
  195.3 45.1 %collective-permute-start.25 = (bf16[128,48,128]{2,1,0:T(8,128)(2,1)}, bf16[128,48,128]{2,1,0:T(8,128)(2,1)}, u32[]{:S(2)}, u32[]{:S(2)}) collective-permute-start(bf16[128,48,128]{2,1,0:T(8,128)(2,1)} %collective-permute-done.18.refs_0_.refs_6_), channel_id=1, source_target_pairs={{0,4},{4,0},{8,12},{12,8},{16,20},{20,16},{24,28},{28,24},{1,5},{5... | collective-permute-start | bytes 4718600 | tf_op jit(solution)/shard_map/ppermute | solution.py:483
  195.9 45.9 %collective-permute-start.26 = (bf16[128,48,128]{2,1,0:T(8,128)(2,1)}, bf16[128,48,128]{2,1,0:T(8,128)(2,1)}, u32[]{:S(2)}, u32[]{:S(2)}) collective-permute-start(bf16[128,48,128]{2,1,0:T(8,128)(2,1)} %collective-permute-done.19.refs_1_.refs_8_), channel_id=1, source_target_pairs={{0,4},{4,0},{8,12},{12,8},{16,20},{20,16},{24,28},{28,24},{1,5},{5... | collective-permute-start | bytes 4718600 | tf_op jit(solution)/shard_map/ppermute | solution.py:483
  196.0 2.5 copy-start.15
  196.0 46.0 %collective-permute-start.23 = (bf16[128,48,128]{2,1,0:T(8,128)(2,1)}, bf16[128,48,128]{2,1,0:T(8,128)(2,1)}, u32[]{:S(2)}, u32[]{:S(2)}) collective-permute-start(bf16[128,48,128]{2,1,0:T(8,128)(2,1)} %collective-permute-done.20.refs_2_.refs_6_), channel_id=1, source_target_pairs={{8,16},{12,20},{16,24},{20,28},{9,17},{13,21},{17,25},{21,29},{10,... | collective-permute-start | bytes 4718600 | tf_op jit(solution)/shard_map/ppermute | solution.py:480
  206.4 2.0 copy-start.1
  210.0 7.2 %copy-start.2 = (bf16[128,48,128]{2,1,0:T(8,128)(2,1)}, bf16[128,48,128]{2,1,0:T(8,128)(2,1)S(1)}, u32[]{:S(2)}) copy-start(bf16[128,48,128]{2,1,0:T(8,128)(2,1)S(1)} %get-tuple-element.134.refs_3_) | copy-start | bytes 4718596
  215.1 11.5 %copy-start.5 = (bf16[128,48,128]{2,1,0:T(8,128)(2,1)}, bf16[128,48,128]{2,1,0:T(8,128)(2,1)S(1)}, u32[]{:S(2)}) copy-start(bf16[128,48,128]{2,1,0:T(8,128)(2,1)S(1)} %get-tuple-element.132.refs_3_) | copy-start | bytes 4718596
  225.3 43.2 %collective-permute-start.24 = (bf16[128,48,128]{2,1,0:T(8,128)(2,1)}, bf16[128,48,128]{2,1,0:T(8,128)(2,1)}, u32[]{:S(2)}, u32[]{:S(2)}) collective-permute-start(bf16[128,48,128]{2,1,0:T(8,128)(2,1)} %collective-permute-done.21.refs_3_.refs_8_), channel_id=1, source_target_pairs={{8,0},{12,4},{16,8},{20,12},{9,1},{13,5},{17,9},{21,13},{10,2},{14... | collective-permute-start | bytes 4718600 | tf_op jit(solution)/shard_map/ppermute | solution.py:480
  235.7 37.3 %collective-permute-start.36 = (bf16[128,48,128]{2,1,0:T(8,128)(2,1)}, bf16[128,48,128]{2,1,0:T(8,128)(2,1)}, u32[]{:S(2)}, u32[]{:S(2)}) collective-permute-start(bf16[128,48,128]{2,1,0:T(8,128)(2,1)} %collective-permute-done.20.refs_2_.refs_6_), channel_id=1, source_target_pairs={{0,4},{4,0},{8,12},{12,8},{16,20},{20,16},{24,28},{28,24},{1,5},{5... | collective-permute-start | bytes 4718600 | tf_op jit(solution)/shard_map/ppermute | solution.py:483
  240.5 61.8 %collective-permute-start.32 = (bf16[128,48,128]{2,1,0:T(8,128)(2,1)}, bf16[128,48,128]{2,1,0:T(8,128)(2,1)}, u32[]{:S(2)}, u32[]{:S(2)}) collective-permute-start(bf16[128,48,128]{2,1,0:T(8,128)(2,1)} %get-tuple-element.143.refs_6_), channel_id=1, source_target_pairs={{16,24},{20,28},{8,0},{12,4},{17,25},{21,29},{9,1},{13,5},{18,26},... | collective-permute-start | bytes 4718600 | tf_op jit(solution)/shard_map/ppermute | solution.py:531
  241.8 60.5 %collective-permute-start.37 = (bf16[128,48,128]{2,1,0:T(8,128)(2,1)}, bf16[128,48,128]{2,1,0:T(8,128)(2,1)}, u32[]{:S(2)}, u32[]{:S(2)}) collective-permute-start(bf16[128,48,128]{2,1,0:T(8,128)(2,1)} %collective-permute-done.21.refs_3_.refs_8_), channel_id=1, source_target_pairs={{0,4},{4,0},{8,12},{12,8},{16,20},{20,16},{24,28},{28,24},{1,5},{5... | collective-permute-start | bytes 4718600 | tf_op jit(solution)/shard_map/ppermute | solution.py:483
  242.0 70.8 %collective-permute-start.35 = (bf16[128,48,128]{2,1,0:T(8,128)(2,1)}, bf16[128,48,128]{2,1,0:T(8,128)(2,1)}, u32[]{:S(2)}, u32[]{:S(2)}) collective-permute-start(bf16[128,48,128]{2,1,0:T(8,128)(2,1)} %get-tuple-element.143.refs_6_), channel_id=1, source_target_pairs={{0,4},{4,0},{8,12},{12,8},{16,20},{20,16},{24,28},{28,24},{1,5},{5... | collective-permute-start | bytes 4718600 | tf_op jit(solution)/shard_map/ppermute | solution.py:483
  242.4 1.4 copy-start.3
  272.8 48.4 %collective-permute-start.34 = (bf16[128,48,128]{2,1,0:T(8,128)(2,1)}, bf16[128,48,128]{2,1,0:T(8,128)(2,1)}, u32[]{:S(2)}, u32[]{:S(2)}) collective-permute-start(bf16[128,48,128]{2,1,0:T(8,128)(2,1)} %get-tuple-element.142.refs_6_), channel_id=1, source_target_pairs={{0,4},{4,0},{8,12},{12,8},{16,20},{20,16},{24,28},{28,24},{1,5},{5... | collective-permute-start | bytes 4718600 | tf_op jit(solution)/shard_map/ppermute | solution.py:483
  273.0 66.9 %collective-permute-start.31 = (bf16[128,48,128]{2,1,0:T(8,128)(2,1)}, bf16[128,48,128]{2,1,0:T(8,128)(2,1)S(1)}, u32[]{:S(2)}, u32[]{:S(2)}) collective-permute-start(bf16[128,48,128]{2,1,0:T(8,128)(2,1)} %get-tuple-element.142.refs_6_), channel_id=1, source_target_pairs={{16,24},{20,28},{8,0},{12,4},{17,25},{21,29},{9,1},{13,5},{18,26},... | collective-permute-start | bytes 4718600 | tf_op jit(solution)/shard_map/ppermute | solution.py:531
  302.3 27.8 %collective-permute-start.33 = (bf16[128,48,128]{2,1,0:T(8,128)(2,1)}, bf16[128,48,128]{2,1,0:T(8,128)(2,1)S(1)}, u32[]{:S(2)}, u32[]{:S(2)}) collective-permute-start(bf16[128,48,128]{2,1,0:T(8,128)(2,1)} %collective-permute-done.32.refs_9_.refs_6_), channel_id=1, source_target_pairs={{0,4},{4,0},{8,12},{12,8},{16,20},{20,16},{24,28},{28,24},{1,5},{5... | collective-permute-start | bytes 4718600 | tf_op jit(solution)/shard_map/ppermute | solution.py:483
  302.3 1.4 copy-start.6
  303.7 9.1 %copy-start.4 = (bf16[128,48,128]{2,1,0:T(8,128)(2,1)S(1)}, bf16[128,48,128]{2,1,0:T(8,128)(2,1)}, u32[]{:S(2)}) copy-start(bf16[128,48,128]{2,1,0:T(8,128)(2,1)} %copy-done.2) | copy-start | bytes 4718596
  312.8 8.4 %copy-start.7 = (bf16[128,48,128]{2,1,0:T(8,128)(2,1)S(1)}, bf16[128,48,128]{2,1,0:T(8,128)(2,1)}, u32[]{:S(2)}) copy-start(bf16[128,48,128]{2,1,0:T(8,128)(2,1)} %copy-done.5) | copy-start | bytes 4718596
  330.1 1.2 copy-start.13
  340.4 3.6 collective-permute-start.38
  344.0 1.2 copy-start.14
Sparse Core Ops, SparseCore 0:
  35.0 84.0 all-gather.2

commit v4 on v3

--- a/solution.py
+++ b/solution.py
@@ -507,12 +507,12 @@
     if chunks > 1:
         read(1, 1)
     hist = own_history(order, here, history, parts, taps, fft)
-    if chunks > 2:
-        read(2, chunks - 2)
     (early,) = filter_chunk(0, False)
     early = lax.all_gather(
         early, "tile", axis_index_groups=[[2 * group + which for group in range(groups)] for which in range(2)]
     )
+    if chunks > 2:
+        read(2, chunks - 2)
     sent, plain = {}, []
     for chunk in range(1, chunks):
         sent[chunk] = exchange(filter_chunk(chunk, True))

time: 362 us -> 358 us (0.989)
    unnamed x32 -> x30, local copies, waits for them, and re-layouts: 10.8 us -> 9.55 us
  transfers between devices with their start and end apart: 41 -> 41, of which waited for: 11 -> 13; matrix products, arithmetic and copies ran while one was open for 1% -> 1% of each run, Pallas kernels for 38% -> 38%
where the time goes in v4:
time: 358 us; the launch traced here: 356 us
  Pallas kernels  157 us (44%)
  waiting for transfers between devices  122 us (34%)
  starting transfers between devices  51.4 us (14%)
  between operations  13.8 us (4%)
  local copies, waits for them, and re-layouts  12.5 us (3%)
    pallas_call x29, Pallas kernels, call(): pl.pallas_call(wrapped, out_shape=[*out_shape, jax.ShapeDtypeStruct((8, L...  157 us
    ppermute x8, waiting for transfers between devices, along(): return lax.ppermute(value, 'tile', pairs)  63.3 us
    ppermute x2, waiting for transfers between devices, step(): lax.ppermute(up[hop - 1], 'tile', [(2 * g + c, 2 * h + c) for g, h in pai...  28 us
    ppermute x18, waiting for transfers between devices, exchange(): lax.ppermute(pieces[slot], 'chan', [(i, i ^ slot) for i in range(count)])  27.4 us
    ppermute x18, starting transfers between devices, exchange(): lax.ppermute(pieces[slot], 'chan', [(i, i ^ slot) for i in range(count)])  22 us
    ppermute x8, starting transfers between devices, along(): return lax.ppermute(value, 'tile', pairs)  19.5 us
    unnamed x30, local copies, waits for them, and re-layouts  9.55 us
  transfers between devices with their start and end apart: 41, of which 13 were waited for; matrix products, arithmetic and copies ran while one was open for 1% of the time, Pallas kernels for 38%

profile of v4, /device:TPU:0, one launch (start us, length us, event | category | flops | bytes accessed | tf_op | source)
XLA Modules:
  0.0 356.4 jit_solution(2332857841026655542)
XLA Ops:
  6.6 3.3 convert.3
  9.9 3.0 collective-permute-start
  13.0 1.6 collective-permute-start.1
  14.5 3.3 convert.4
  17.9 4.6 %history.1 = (bf16[4,4,16,2048]{3,2,1,0:T(8,128)(2,1)S(1)}, f32[8,128]{1,0:T(8,128)S(1)}) custom-call(s32[3]{0:T(128)S(1)} %pad_add_fusion.place_ref, s32[64,30720]{1,0:T(8,128)} %refs_0_.10, f32[8,128]{1,0:T(8,128)S(1)} %get-tuple-element.82.refs_1_), custom_call_target="tpu_custom_call" | custom-call | flops 5175000064 | tf_op jit(solution)/shard_map/history/pallas_call | solution.py:49
  22.5 3.8 %collective-permute-done.1.refs_4_ = bf16[1,4,16,2048]{3,2,1,0:T(8,128)(2,1)S(1)} collective-permute-done((bf16[1,4,16,2048]{3,2,1,0:T(8,128)(2,1)S(1)}, bf16[1,4,16,2048]{3,2,1,0:T(8,128)(2,1)S(1)}, u32[]{:S(2)}, u32[]{:S(2)}) %collective-permute-start.1) | collective-permute-done | bytes 262176 | tf_op jit(solution)/shard_map/ppermute | solution.py:457
  26.4 7.7 %channelize.4 = (bf16[4,4,256,128]{3,2,1,0:T(8,128)(2,1)}, f32[8,128]{1,0:T(8,128)S(1)}) custom-call(s32[3]{0:T(128)S(1)} %pad_add_fusion.place_ref, s32[16,2048]{1,0:T(8,128)S(1)} %copy-done.9, bf16[4,4,16,2048]{3,2,1,0:T(8,128)(2,1)S(1)} %get-tuple-element.83.refs_1_, bf16[1,4,16,2048]{3,2,1,0:T(8,128)(2,1)S(1)} %get-tuple-element.84.refs_2_, ...), custom_call_target="tpu_custom_call" | custom-call | flops 10350000128 | tf_op jit(solution)/shard_map/channelize/pallas_call | solution.py:49
  36.2 1.5 collective-permute-start.8
  37.7 4.6 %convert.5 = (bf16[2,4,16,2048]{3,2,1,0:T(8,128)(2,1)S(1)}, bf16[2,4,16,2048]{3,2,1,0:T(8,128)(2,1)S(1)}, bf16[2,4,16,2048]{3,2,1,0:T(8,128)(2,1)S(1)}, bf16[2,4,16,2048]{3,2,1,0:T(8,128)(2,1)S(1)}, f32[8,128]{1,0:T(8,128)S(1)}) custom-call(s32[3]{0:T(128)S(1)} %pad_add_fusion.place_ref, s32[64,32768]{1,0:T(8,128)} %refs_0_.12, ...), custom_call_target="tpu_custom_call" | custom-call | flops 5750000128 | tf_op jit(solution)/shard_map/convert/pallas_call | solution.py:49
  42.3 1.3 collective-permute-start.3
  44.4 1.4 collective-permute-start.5
  45.8 2.1 collective-permute-done.7.refs_4_
  47.9 2.1 collective-permute-done.8.refs_5_
  50.0 6.7 %channelize.5 = (bf16[4,256,128]{2,1,0:T(8,128)(2,1)S(1)}, bf16[4,256,128]{2,1,0:T(8,128)(2,1)S(1)}, bf16[4,256,128]{2,1,0:T(8,128)(2,1)S(1)}, bf16[4,256,128]{2,1,0:T(8,128)(2,1)S(1)}, f32[8,128]{1,0:T(8,128)S(1)}) custom-call(s32[3]{0:T(128)S(1)} %pad_add_fusion.place_ref, s32[16,2048]{1,0:T(8,128)S(1)} %copy-done.9, ...), custom_call_target="tpu_custom_call" | custom-call | flops 10350000128 | tf_op jit(solution)/shard_map/channelize/pallas_call | solution.py:49
  57.3 1.4 collective-permute-start.11
  58.7 1.6 collective-permute-done.3.refs_3_
  61.5 14.4 %collective-permute-done.4.refs_4_ = bf16[2,4,16,2048]{3,2,1,0:T(8,128)(2,1)S(1)} collective-permute-done((bf16[2,4,16,2048]{3,2,1,0:T(8,128)(2,1)S(1)}, bf16[2,4,16,2048]{3,2,1,0:T(8,128)(2,1)S(1)}, u32[]{:S(2)}, u32[]{:S(2)}) %collective-permute-start.4) | collective-permute-done | bytes 524320 | tf_op jit(solution)/shard_map/ppermute | solution.py:457
  75.9 6.8 %channelize.6 = (bf16[4,256,128]{2,1,0:T(8,128)(2,1)S(1)}, bf16[4,256,128]{2,1,0:T(8,128)(2,1)S(1)}, bf16[4,256,128]{2,1,0:T(8,128)(2,1)S(1)}, bf16[4,256,128]{2,1,0:T(8,128)(2,1)S(1)}, f32[8,128]{1,0:T(8,128)S(1)}) custom-call(s32[3]{0:T(128)S(1)} %pad_add_fusion.place_ref, s32[16,2048]{1,0:T(8,128)S(1)} %copy-done.9, ...), custom_call_target="tpu_custom_call" | custom-call | flops 10350000128 | tf_op jit(solution)/shard_map/channelize/pallas_call | solution.py:49
  82.9 1.6 collective-permute-start.16
  84.4 1.8 collective-permute-start.17
  86.3 3.0 merge.3
  89.2 6.7 %channelize.7 = (bf16[4,256,128]{2,1,0:T(8,128)(2,1)S(1)}, bf16[4,256,128]{2,1,0:T(8,128)(2,1)S(1)}, bf16[4,256,128]{2,1,0:T(8,128)(2,1)S(1)}, bf16[4,256,128]{2,1,0:T(8,128)(2,1)S(1)}, f32[8,128]{1,0:T(8,128)S(1)}) custom-call(s32[3]{0:T(128)S(1)} %pad_add_fusion.place_ref, s32[16,2048]{1,0:T(8,128)S(1)} %copy-done.9, ...), custom_call_target="tpu_custom_call" | custom-call | flops 10350000128 | tf_op jit(solution)/shard_map/channelize/pallas_call | solution.py:49
  96.1 1.6 collective-permute-start.13
  97.7 1.8 collective-permute-start.14
  99.5 3.1 merge.4
  102.6 3.4 collective-permute-done.13.refs_2_
  106.1 3.0 merge.5
  109.0 4.5 %collective-permute-start.18 = (bf16[128,48,128]{2,1,0:T(8,128)(2,1)S(1)}, bf16[128,48,128]{2,1,0:T(8,128)(2,1)}, u32[]{:S(2)}, u32[]{:S(2)}) collective-permute-start(bf16[128,48,128]{2,1,0:T(8,128)(2,1)S(1)} %get-tuple-element.123.refs_0_.refs_1_.refs_6_), channel_id=1, source_target_pairs={{0,8},{4,12},{8,16},{12,20},{16,24},{20,28},{1,9},{5,13},{9,17},{1... | collective-permute-start | bytes 4718600 | tf_op jit(solution)/shard_map/ppermute | solution.py:480
  113.5 1.3 collective-permute-start.19
  114.8 5.7 %collective-permute-start.20 = (bf16[128,48,128]{2,1,0:T(8,128)(2,1)}, bf16[128,48,128]{2,1,0:T(8,128)(2,1)}, u32[]{:S(2)}, u32[]{:S(2)}) collective-permute-start(bf16[128,48,128]{2,1,0:T(8,128)(2,1)} %get-tuple-element.124.refs_0_.refs_1_.refs_6_), channel_id=1, source_target_pairs={{0,8},{4,12},{8,16},{12,20},{16,24},{20,28},{1,9},{5,13},{9,17},{1... | collective-permute-start | bytes 4718600 | tf_op jit(solution)/shard_map/ppermute | solution.py:480
  120.6 1.3 collective-permute-start.21
  122.1 2.2 copy-done.8
  124.8 2.5 copy.21
  127.3 4.9 %all-to-all-start = ((bf16[4,4,4,256,128]{4,3,2,1,0:T(8,128)(2,1)}), bf16[4,4,4,256,128]{4,3,2,1,0:T(8,128)(2,1)}, u32[]{:S(2)}, u32[]{:S(2)}) async-start(bf16[4,4,4,256,128]{4,3,2,1,0:T(8,128)(2,1)} %bitcast.15), calls=%async_computation | async-start | bytes 8388608 | tf_op jit(solution)/shard_map/all_to_all | solution.py:542
  132.2 15.0 %collective-permute-done.18.refs_0_.refs_6_ = bf16[128,48,128]{2,1,0:T(8,128)(2,1)} collective-permute-done((bf16[128,48,128]{2,1,0:T(8,128)(2,1)S(1)}, bf16[128,48,128]{2,1,0:T(8,128)(2,1)}, u32[]{:S(2)}, u32[]{:S(2)}) %collective-permute-start.18) | collective-permute-done | bytes 1572896 | tf_op jit(solution)/shard_map/ppermute | solution.py:480
  147.2 5.6 %collective-permute-done.19.refs_1_.refs_8_ = bf16[128,48,128]{2,1,0:T(8,128)(2,1)} collective-permute-done((bf16[128,48,128]{2,1,0:T(8,128)(2,1)S(1)}, bf16[128,48,128]{2,1,0:T(8,128)(2,1)}, u32[]{:S(2)}, u32[]{:S(2)}) %collective-permute-start.19) | collective-permute-done | bytes 1572896 | tf_op jit(solution)/shard_map/ppermute | solution.py:480
  152.9 1.8 collective-permute-start.29
  154.7 24.1 %collective-permute-done.20.refs_2_.refs_6_ = bf16[128,48,128]{2,1,0:T(8,128)(2,1)} collective-permute-done((bf16[128,48,128]{2,1,0:T(8,128)(2,1)}, bf16[128,48,128]{2,1,0:T(8,128)(2,1)}, u32[]{:S(2)}, u32[]{:S(2)}) %collective-permute-start.20) | collective-permute-done | bytes 1572896 | tf_op jit(solution)/shard_map/ppermute | solution.py:480
  180.1 2.5 collective-permute-done.21.refs_3_.refs_8_
  183.2 7.9 %merge_early.2 = (bf16[4,256,16,128]{3,2,1,0:T(8,128)(2,1)S(1)}, f32[8,128]{1,0:T(8,128)S(1)}) custom-call(s32[3]{0:T(128)S(1)} %pad_add_fusion.place_ref, bf16[4,4,4,256,128]{4,3,2,1,0:T(8,128)(2,1)} %all-to-all-done.refs_0_, f32[8,128]{1,0:T(8,128)S(1)} %gate.4.refs_1_), custom_call_target="tpu_custom_call" | custom-call | flops 46000001024 | tf_op jit(solution)/shard_map/merge_early/pallas_call | solution.py:49
  191.9 2.3 collective-permute-start.23
  194.3 7.9 %merge_early.3 = (bf16[4,256,16,128]{3,2,1,0:T(8,128)(2,1)S(1)}, f32[8,128]{1,0:T(8,128)S(1)}) custom-call(s32[3]{0:T(128)S(1)} %pad_add_fusion.place_ref, bf16[4,4,4,256,128]{4,3,2,1,0:T(8,128)(2,1)} %copy-done.14, f32[8,128]{1,0:T(8,128)S(1)} %get-tuple-element.127.refs_1_), custom_call_target="tpu_custom_call" | custom-call | flops 46000001024 | tf_op jit(solution)/shard_map/merge_early/pallas_call | solution.py:49
  202.3 2.0 copy-done.1
  204.3 1.6 turn.3
  205.9 5.0 %turn.4 = (bf16[128,48,128]{2,1,0:T(8,128)(2,1)S(1)}, f32[8,128]{1,0:T(8,128)S(1)}) custom-call(s32[3]{0:T(128)S(1)} %pad_add_fusion.place_ref, bf16[128,48,128]{2,1,0:T(8,128)(2,1)} %get-tuple-element.124.refs_0_.refs_1_.refs_6_, f32[8,128]{1,0:T(8,128)S(1)} %get-tuple-element.129.refs_1_), custom_call_target="tpu_custom_call" | custom-call | flops 115000000 | tf_op jit(solution)/shard_map/turn/pallas_call | solution.py:49
  210.9 2.2 turn.5
  213.1 8.1 %correlate.8 = (f32[2,256,64,512]{3,2,1,0:T(8,128)}, f32[8,128]{1,0:T(8,128)S(1)}) custom-call(s32[5]{0:T(128)S(1)} %stack.44.place_ref, bf16[4,256,16,128]{3,2,1,0:T(8,128)(2,1)} %copy-done, bf16[128,48,128]{2,1,0:T(8,128)(2,1)S(1)} %get-tuple-element.123.refs_0_.refs_1_.refs_6_, bf16[256,16,128]{2,1,0:T(8,128)(2,1)S(1)} %get-tuple-element.131.refs_2_, ...), custom_call_target="tpu_custom_call" | custom-call | flops 1150000000 | tf_op jit(solution)/shard_map/correlate/pallas_call | solution.py:49
  221.2 1.3 collective-permute-start.24
  222.5 9.1 %correlate.9 = (f32[2,256,64,512]{3,2,1,0:T(8,128)}, f32[8,128]{1,0:T(8,128)S(1)}) custom-call(s32[5]{0:T(128)S(1)} %stack.44.place_ref, bf16[4,256,16,128]{3,2,1,0:T(8,128)(2,1)} %copy-done, bf16[128,48,128]{2,1,0:T(8,128)(2,1)} %get-tuple-element.124.refs_0_.refs_1_.refs_6_, ...), custom_call_target="tpu_custom_call", output_to_operand_aliasing={{0}: (9, {})} | custom-call | flops 1150000000 | tf_op jit(solution)/shard_map/correlate/pallas_call | solution.py:49
  232.1 4.3 %select.6 = (bf16[128,48,128]{2,1,0:T(8,128)(2,1)}, f32[8,128]{1,0:T(8,128)S(1)}) custom-call(s32[5]{0:T(128)S(1)} %stack.40.place_ref, bf16[128,48,128]{2,1,0:T(8,128)(2,1)} %collective-permute-done.29.refs_0_, bf16[128,48,128]{2,1,0:T(8,128)(2,1)} %collective-permute-done.30.refs_1_, f32[8,128]{1,0:T(8,128)S(1)} %get-tuple-element.139.refs_2_), custom_call_target="tpu_custom_call" | custom-call | flops 1150000000 | tf_op jit(solution)/shard_map/select/pallas_call | solution.py:49
  236.4 1.3 collective-permute-start.32
  238.4 1.4 copy-done.3
  239.8 8.6 %correlate.10 = (f32[2,256,64,512]{3,2,1,0:T(8,128)}, f32[8,128]{1,0:T(8,128)S(1)}) custom-call(s32[5]{0:T(128)S(1)} %stack.43.place_ref, bf16[4,256,16,128]{3,2,1,0:T(8,128)(2,1)} %copy-done, bf16[128,48,128]{2,1,0:T(8,128)(2,1)S(1)} %get-tuple-element.123.refs_0_.refs_1_.refs_6_, ...), custom_call_target="tpu_custom_call", output_to_operand_aliasing={{0}: (11, {})} | custom-call | flops 8049999872 | tf_op jit(solution)/shard_map/correlate/pallas_call | solution.py:49
  248.3 16.0 %collective-permute-done.24.refs_1_ = bf16[128,48,128]{2,1,0:T(8,128)(2,1)} collective-permute-done((bf16[128,48,128]{2,1,0:T(8,128)(2,1)}, bf16[128,48,128]{2,1,0:T(8,128)(2,1)}, u32[]{:S(2)}, u32[]{:S(2)}) %collective-permute-start.24) | collective-permute-done | bytes 1572896 | tf_op jit(solution)/shard_map/ppermute | solution.py:480
  264.3 4.2 %select.7 = (bf16[128,48,128]{2,1,0:T(8,128)(2,1)}, f32[8,128]{1,0:T(8,128)S(1)}) custom-call(s32[5]{0:T(128)S(1)} %stack.40.place_ref, bf16[128,48,128]{2,1,0:T(8,128)(2,1)} %collective-permute-done.23.refs_0_, bf16[128,48,128]{2,1,0:T(8,128)(2,1)} %collective-permute-done.24.refs_1_, f32[8,128]{1,0:T(8,128)S(1)} %get-tuple-element.141.refs_2_), custom_call_target="tpu_custom_call" | custom-call | flops 1150000000 | tf_op jit(solution)/shard_map/select/pallas_call | solution.py:49
  268.8 1.3 collective-permute-start.31
  270.0 28.0 %collective-permute-done.32.refs_9_.refs_6_ = bf16[128,48,128]{2,1,0:T(8,128)(2,1)} collective-permute-done((bf16[128,48,128]{2,1,0:T(8,128)(2,1)}, bf16[128,48,128]{2,1,0:T(8,128)(2,1)}, u32[]{:S(2)}, u32[]{:S(2)}) %collective-permute-start.32) | collective-permute-done | bytes 1572896 | tf_op jit(solution)/shard_map/ppermute | solution.py:531
  298.1 1.4 copy-done.6
  299.5 9.1 %correlate.11 = (f32[2,256,64,512]{3,2,1,0:T(8,128)}, f32[8,128]{1,0:T(8,128)S(1)}) custom-call(s32[5]{0:T(128)S(1)} %stack.43.place_ref, bf16[4,256,16,128]{3,2,1,0:T(8,128)(2,1)} %copy-done, bf16[128,48,128]{2,1,0:T(8,128)(2,1)} %get-tuple-element.124.refs_0_.refs_1_.refs_6_, ...), custom_call_target="tpu_custom_call", output_to_operand_aliasing={{0}: (11, {})} | custom-call | flops 8049999872 | tf_op jit(solution)/shard_map/correlate/pallas_call | solution.py:49
  308.6 8.4 %correlate.12 = (f32[2,256,64,512]{3,2,1,0:T(8,128)}, f32[8,128]{1,0:T(8,128)S(1)}) custom-call(s32[5]{0:T(128)S(1)} %stack.47.place_ref, bf16[4,256,16,128]{3,2,1,0:T(8,128)(2,1)} %copy-done, bf16[128,48,128]{2,1,0:T(8,128)(2,1)S(1)} %get-tuple-element.123.refs_0_.refs_1_.refs_6_, ...), custom_call_target="tpu_custom_call", output_to_operand_aliasing={{0}: (9, {})} | custom-call | flops 8049999872 | tf_op jit(solution)/shard_map/correlate/pallas_call | solution.py:49
  317.0 8.9 %correlate.13 = (f32[2,256,64,512]{3,2,1,0:T(8,128)}, f32[8,128]{1,0:T(8,128)S(1)}) custom-call(s32[5]{0:T(128)S(1)} %stack.47.place_ref, bf16[4,256,16,128]{3,2,1,0:T(8,128)(2,1)} %copy-done, bf16[128,48,128]{2,1,0:T(8,128)(2,1)} %get-tuple-element.124.refs_0_.refs_1_.refs_6_, ...), custom_call_target="tpu_custom_call", output_to_operand_aliasing={{0}: (9, {})} | custom-call | flops 8049999872 | tf_op jit(solution)/shard_map/correlate/pallas_call | solution.py:49
  327.0 8.6 %correlate.14 = (f32[2,256,64,512]{3,2,1,0:T(8,128)}, f32[8,128]{1,0:T(8,128)S(1)}) custom-call(s32[5]{0:T(128)S(1)} %stack.37.place_ref, bf16[4,256,16,128]{3,2,1,0:T(8,128)(2,1)} %copy-done, bf16[128,48,128]{2,1,0:T(8,128)(2,1)S(1)} %get-tuple-element.123.refs_0_.refs_1_.refs_6_, ...), custom_call_target="tpu_custom_call", output_to_operand_aliasing={{0}: (11, {})} | custom-call | flops 8049999872 | tf_op jit(solution)/shard_map/correlate/pallas_call | solution.py:49
  336.8 3.0 collective-permute-done.38.refs_7_
  341.0 8.6 %correlate.15 = (f32[2,256,64,512]{3,2,1,0:T(8,128)}, f32[8,128]{1,0:T(8,128)}) custom-call(s32[5]{0:T(128)S(1)} %stack.37.place_ref, bf16[4,256,16,128]{3,2,1,0:T(8,128)(2,1)} %copy-done, bf16[128,48,128]{2,1,0:T(8,128)(2,1)} %get-tuple-element.124.refs_0_.refs_1_.refs_6_, ...), custom_call_target="tpu_custom_call", output_to_operand_aliasing={{0}: (11, {})} | custom-call | flops 8049999872 | tf_op jit(solution)/shard_map/correlate/pallas_call | solution.py:49
  (85 shorter events, 13.5 us)
Async XLA Ops:
  6.5 115.5 %all-gather.3.cloned.1.call-start = ((), (), s32[]{:S(2)}) async-start(), calls=%async_computation.1 | async-start | bytes 5242880 | tf_op jit(solution)/shard_map/all_gather | solution.py:511
  9.9 12.6 %collective-permute-start = (bf16[1,4,16,2048]{3,2,1,0:T(8,128)(2,1)S(1)}, bf16[1,4,16,2048]{3,2,1,0:T(8,128)(2,1)S(1)}, u32[]{:S(2)}, u32[]{:S(2)}) collective-permute-start(bf16[1,4,16,2048]{3,2,1,0:T(8,128)(2,1)S(1)} %get-tuple-element.85), channel_id=1, source_target_pairs={{0,1},{1,0},{2,3},{3,2},{4,5},{5,4},{6,7},{7,6},{8,9},{9,8},{10,11... | collective-permute-start | bytes 786440 | tf_op jit(solution)/shard_map/ppermute | solution.py:457
  13.0 13.4 %collective-permute-start.1 = (bf16[1,4,16,2048]{3,2,1,0:T(8,128)(2,1)S(1)}, bf16[1,4,16,2048]{3,2,1,0:T(8,128)(2,1)S(1)}, u32[]{:S(2)}, u32[]{:S(2)}) collective-permute-start(bf16[1,4,16,2048]{3,2,1,0:T(8,128)(2,1)S(1)} %get-tuple-element.86), channel_id=1, source_target_pairs={{0,2},{1,3},{2,0},{3,1},{4,6},{5,7},{6,4},{7,5},{8,10},{9,11},{10,... | collective-permute-start | bytes 786440 | tf_op jit(solution)/shard_map/ppermute | solution.py:457
  14.5 11.8 %collective-permute-start.2 = (bf16[1,4,16,2048]{3,2,1,0:T(8,128)(2,1)S(1)}, bf16[1,4,16,2048]{3,2,1,0:T(8,128)(2,1)S(1)}, u32[]{:S(2)}, u32[]{:S(2)}) collective-permute-start(bf16[1,4,16,2048]{3,2,1,0:T(8,128)(2,1)S(1)} %get-tuple-element.87), channel_id=1, source_target_pairs={{0,3},{1,2},{2,1},{3,0},{4,7},{5,6},{6,5},{7,4},{8,11},{9,10},{10,... | collective-permute-start | bytes 786440 | tf_op jit(solution)/shard_map/ppermute | solution.py:457
  17.9 8.5 %copy-start.9 = (s32[16,2048]{1,0:T(8,128)S(1)}, s32[16,2048]{1,0:T(8,128)}, u32[]{:S(2)}) copy-start(s32[16,2048]{1,0:T(8,128)} %refs_0_.15) | copy-start | bytes 393220
  22.5 11.6 %copy-start.10 = (bf16[4,4,16,2048]{3,2,1,0:T(8,128)(2,1)}, bf16[4,4,16,2048]{3,2,1,0:T(8,128)(2,1)S(1)}, u32[]{:S(2)}) copy-start(bf16[4,4,16,2048]{3,2,1,0:T(8,128)(2,1)S(1)} %get-tuple-element.83.refs_1_) | copy-start | bytes 3145732
  34.1 10.3 %collective-permute-start.6 = (bf16[1,4,16,2048]{3,2,1,0:T(8,128)(2,1)S(1)}, bf16[1,4,16,2048]{3,2,1,0:T(8,128)(2,1)S(1)}, u32[]{:S(2)}, u32[]{:S(2)}) collective-permute-start(bf16[1,4,16,2048]{3,2,1,0:T(8,128)(2,1)S(1)} %get-tuple-element.96), channel_id=1, source_target_pairs={{0,1},{1,0},{2,3},{3,2},{4,5},{5,4},{6,7},{7,6},{8,9},{9,8},{10,11... | collective-permute-start | bytes 786440 | tf_op jit(solution)/shard_map/ppermute | solution.py:457
  35.4 12.5 %collective-permute-start.7 = (bf16[1,4,16,2048]{3,2,1,0:T(8,128)(2,1)S(1)}, bf16[1,4,16,2048]{3,2,1,0:T(8,128)(2,1)S(1)}, u32[]{:S(2)}, u32[]{:S(2)}) collective-permute-start(bf16[1,4,16,2048]{3,2,1,0:T(8,128)(2,1)S(1)} %get-tuple-element.97), channel_id=1, source_target_pairs={{0,2},{1,3},{2,0},{3,1},{4,6},{5,7},{6,4},{7,5},{8,10},{9,11},{10,... | collective-permute-start | bytes 786440 | tf_op jit(solution)/shard_map/ppermute | solution.py:457
  36.2 13.8 %collective-permute-start.8 = (bf16[1,4,16,2048]{3,2,1,0:T(8,128)(2,1)S(1)}, bf16[1,4,16,2048]{3,2,1,0:T(8,128)(2,1)S(1)}, u32[]{:S(2)}, u32[]{:S(2)}) collective-permute-start(bf16[1,4,16,2048]{3,2,1,0:T(8,128)(2,1)S(1)} %get-tuple-element.98), channel_id=1, source_target_pairs={{0,3},{1,2},{2,1},{3,0},{4,7},{5,6},{6,5},{7,4},{8,11},{9,10},{10,... | collective-permute-start | bytes 786440 | tf_op jit(solution)/shard_map/ppermute | solution.py:457
  37.7 12.3 %copy-start.11 = (bf16[4,4,16,2048]{3,2,1,0:T(8,128)(2,1)S(1)}, bf16[4,4,16,2048]{3,2,1,0:T(8,128)(2,1)}, u32[]{:S(2)}) copy-start(bf16[4,4,16,2048]{3,2,1,0:T(8,128)(2,1)} %copy-done.10) | copy-start | bytes 3145732
  42.3 18.1 %collective-permute-start.3 = (bf16[2,4,16,2048]{3,2,1,0:T(8,128)(2,1)S(1)}, bf16[2,4,16,2048]{3,2,1,0:T(8,128)(2,1)S(1)}, u32[]{:S(2)}, u32[]{:S(2)}) collective-permute-start(bf16[2,4,16,2048]{3,2,1,0:T(8,128)(2,1)S(1)} %get-tuple-element.92), channel_id=1, source_target_pairs={{0,1},{1,0},{2,3},{3,2},{4,5},{5,4},{6,7},{7,6},{8,9},{9,8},{10,11... | collective-permute-start | bytes 1572872 | tf_op jit(solution)/shard_map/ppermute | solution.py:457
  43.6 32.4 %collective-permute-start.4 = (bf16[2,4,16,2048]{3,2,1,0:T(8,128)(2,1)S(1)}, bf16[2,4,16,2048]{3,2,1,0:T(8,128)(2,1)S(1)}, u32[]{:S(2)}, u32[]{:S(2)}) collective-permute-start(bf16[2,4,16,2048]{3,2,1,0:T(8,128)(2,1)S(1)} %get-tuple-element.93), channel_id=1, source_target_pairs={{0,2},{1,3},{2,0},{3,1},{4,6},{5,7},{6,4},{7,5},{8,10},{9,11},{10,... | collective-permute-start | bytes 1572872 | tf_op jit(solution)/shard_map/ppermute | solution.py:457
  44.4 31.5 %collective-permute-start.5 = (bf16[2,4,16,2048]{3,2,1,0:T(8,128)(2,1)S(1)}, bf16[2,4,16,2048]{3,2,1,0:T(8,128)(2,1)S(1)}, u32[]{:S(2)}, u32[]{:S(2)}) collective-permute-start(bf16[2,4,16,2048]{3,2,1,0:T(8,128)(2,1)S(1)} %get-tuple-element.94), channel_id=1, source_target_pairs={{0,3},{1,2},{2,1},{3,0},{4,7},{5,6},{6,5},{7,4},{8,11},{9,10},{10,... | collective-permute-start | bytes 1572872 | tf_op jit(solution)/shard_map/ppermute | solution.py:457
  56.7 27.7 %collective-permute-start.10 = (bf16[4,256,128]{2,1,0:T(8,128)(2,1)S(1)}, bf16[4,256,128]{2,1,0:T(8,128)(2,1)S(1)}, u32[]{:S(2)}, u32[]{:S(2)}) collective-permute-start(bf16[4,256,128]{2,1,0:T(8,128)(2,1)S(1)} %get-tuple-element.102), channel_id=1, source_target_pairs={{0,2},{1,3},{2,0},{3,1},{4,6},{5,7},{6,4},{7,5},{8,10},{9,11},{10,... | collective-permute-start | bytes 786440 | tf_op jit(solution)/shard_map/ppermute | solution.py:457
  57.3 28.9 %collective-permute-start.11 = (bf16[4,256,128]{2,1,0:T(8,128)(2,1)S(1)}, bf16[4,256,128]{2,1,0:T(8,128)(2,1)S(1)}, u32[]{:S(2)}, u32[]{:S(2)}) collective-permute-start(bf16[4,256,128]{2,1,0:T(8,128)(2,1)S(1)} %get-tuple-element.103), channel_id=1, source_target_pairs={{0,3},{1,2},{2,1},{3,0},{4,7},{5,6},{6,5},{7,4},{8,11},{9,10},{10,... | collective-permute-start | bytes 786440 | tf_op jit(solution)/shard_map/ppermute | solution.py:457
  60.3 25.9 %collective-permute-start.9 = (bf16[4,256,128]{2,1,0:T(8,128)(2,1)S(1)}, bf16[4,256,128]{2,1,0:T(8,128)(2,1)S(1)}, u32[]{:S(2)}, u32[]{:S(2)}) collective-permute-start(bf16[4,256,128]{2,1,0:T(8,128)(2,1)S(1)} %get-tuple-element.101), channel_id=1, source_target_pairs={{0,1},{1,0},{2,3},{3,2},{4,5},{5,4},{6,7},{7,6},{8,9},{9,8},{10,11... | collective-permute-start | bytes 786440 | tf_op jit(solution)/shard_map/ppermute | solution.py:457
  82.7 15.0 %collective-permute-start.15 = (bf16[4,256,128]{2,1,0:T(8,128)(2,1)S(1)}, bf16[4,256,128]{2,1,0:T(8,128)(2,1)S(1)}, u32[]{:S(2)}, u32[]{:S(2)}) collective-permute-start(bf16[4,256,128]{2,1,0:T(8,128)(2,1)S(1)} %get-tuple-element.112), channel_id=1, source_target_pairs={{0,1},{1,0},{2,3},{3,2},{4,5},{5,4},{6,7},{7,6},{8,9},{9,8},{10,11... | collective-permute-start | bytes 786440 | tf_op jit(solution)/shard_map/ppermute | solution.py:457
  82.9 16.6 %collective-permute-start.16 = (bf16[4,256,128]{2,1,0:T(8,128)(2,1)S(1)}, bf16[4,256,128]{2,1,0:T(8,128)(2,1)S(1)}, u32[]{:S(2)}, u32[]{:S(2)}) collective-permute-start(bf16[4,256,128]{2,1,0:T(8,128)(2,1)S(1)} %get-tuple-element.113), channel_id=1, source_target_pairs={{0,2},{1,3},{2,0},{3,1},{4,6},{5,7},{6,4},{7,5},{8,10},{9,11},{10,... | collective-permute-start | bytes 786440 | tf_op jit(solution)/shard_map/ppermute | solution.py:457
  84.4 15.1 %collective-permute-start.17 = (bf16[4,256,128]{2,1,0:T(8,128)(2,1)S(1)}, bf16[4,256,128]{2,1,0:T(8,128)(2,1)S(1)}, u32[]{:S(2)}, u32[]{:S(2)}) collective-permute-start(bf16[4,256,128]{2,1,0:T(8,128)(2,1)S(1)} %get-tuple-element.114), channel_id=1, source_target_pairs={{0,3},{1,2},{2,1},{3,0},{4,7},{5,6},{6,5},{7,4},{8,11},{9,10},{10,... | collective-permute-start | bytes 786440 | tf_op jit(solution)/shard_map/ppermute | solution.py:457
  95.9 6.7 %collective-permute-start.12 = (bf16[4,256,128]{2,1,0:T(8,128)(2,1)S(1)}, bf16[4,256,128]{2,1,0:T(8,128)(2,1)S(1)}, u32[]{:S(2)}, u32[]{:S(2)}) collective-permute-start(bf16[4,256,128]{2,1,0:T(8,128)(2,1)S(1)} %get-tuple-element.108), channel_id=1, source_target_pairs={{0,1},{1,0},{2,3},{3,2},{4,5},{5,4},{6,7},{7,6},{8,9},{9,8},{10,11... | collective-permute-start | bytes 786440 | tf_op jit(solution)/shard_map/ppermute | solution.py:457
  96.1 10.0 %collective-permute-start.13 = (bf16[4,256,128]{2,1,0:T(8,128)(2,1)S(1)}, bf16[4,256,128]{2,1,0:T(8,128)(2,1)S(1)}, u32[]{:S(2)}, u32[]{:S(2)}) collective-permute-start(bf16[4,256,128]{2,1,0:T(8,128)(2,1)S(1)} %get-tuple-element.109), channel_id=1, source_target_pairs={{0,2},{1,3},{2,0},{3,1},{4,6},{5,7},{6,4},{7,5},{8,10},{9,11},{10,... | collective-permute-start | bytes 786440 | tf_op jit(solution)/shard_map/ppermute | solution.py:457
  97.7 8.4 %collective-permute-start.14 = (bf16[4,256,128]{2,1,0:T(8,128)(2,1)S(1)}, bf16[4,256,128]{2,1,0:T(8,128)(2,1)S(1)}, u32[]{:S(2)}, u32[]{:S(2)}) collective-permute-start(bf16[4,256,128]{2,1,0:T(8,128)(2,1)S(1)} %get-tuple-element.110), channel_id=1, source_target_pairs={{0,3},{1,2},{2,1},{3,0},{4,7},{5,6},{6,5},{7,4},{8,11},{9,10},{10,... | collective-permute-start | bytes 786440 | tf_op jit(solution)/shard_map/ppermute | solution.py:457
  109.0 38.2 %collective-permute-start.18 = (bf16[128,48,128]{2,1,0:T(8,128)(2,1)S(1)}, bf16[128,48,128]{2,1,0:T(8,128)(2,1)}, u32[]{:S(2)}, u32[]{:S(2)}) collective-permute-start(bf16[128,48,128]{2,1,0:T(8,128)(2,1)S(1)} %get-tuple-element.123.refs_0_.refs_1_.refs_6_), channel_id=1, source_target_pairs={{0,8},{4,12},{8,16},{12,20},{16,24},{20,28},{1,9},{5,13},{9,17},{1... | collective-permute-start | bytes 4718600 | tf_op jit(solution)/shard_map/ppermute | solution.py:480
  113.5 39.3 %collective-permute-start.19 = (bf16[128,48,128]{2,1,0:T(8,128)(2,1)S(1)}, bf16[128,48,128]{2,1,0:T(8,128)(2,1)}, u32[]{:S(2)}, u32[]{:S(2)}) collective-permute-start(bf16[128,48,128]{2,1,0:T(8,128)(2,1)S(1)} %get-tuple-element.123.refs_0_.refs_1_.refs_6_), channel_id=1, source_target_pairs={{8,0},{12,4},{16,8},{20,12},{24,16},{28,20},{9,1},{13,5},{17,9},{2... | collective-permute-start | bytes 4718600 | tf_op jit(solution)/shard_map/ppermute | solution.py:480
  114.8 64.0 %collective-permute-start.20 = (bf16[128,48,128]{2,1,0:T(8,128)(2,1)}, bf16[128,48,128]{2,1,0:T(8,128)(2,1)}, u32[]{:S(2)}, u32[]{:S(2)}) collective-permute-start(bf16[128,48,128]{2,1,0:T(8,128)(2,1)} %get-tuple-element.124.refs_0_.refs_1_.refs_6_), channel_id=1, source_target_pairs={{0,8},{4,12},{8,16},{12,20},{16,24},{20,28},{1,9},{5,13},{9,17},{1... | collective-permute-start | bytes 4718600 | tf_op jit(solution)/shard_map/ppermute | solution.py:480
  120.6 62.0 %collective-permute-start.21 = (bf16[128,48,128]{2,1,0:T(8,128)(2,1)}, bf16[128,48,128]{2,1,0:T(8,128)(2,1)}, u32[]{:S(2)}, u32[]{:S(2)}) collective-permute-start(bf16[128,48,128]{2,1,0:T(8,128)(2,1)} %get-tuple-element.124.refs_0_.refs_1_.refs_6_), channel_id=1, source_target_pairs={{8,0},{12,4},{16,8},{20,12},{24,16},{28,20},{9,1},{13,5},{17,9},{2... | collective-permute-start | bytes 4718600 | tf_op jit(solution)/shard_map/ppermute | solution.py:480
  122.0 69.2 %collective-permute-start.28 = (bf16[128,48,128]{2,1,0:T(8,128)(2,1)S(1)}, bf16[128,48,128]{2,1,0:T(8,128)(2,1)}, u32[]{:S(2)}, u32[]{:S(2)}) collective-permute-start(bf16[128,48,128]{2,1,0:T(8,128)(2,1)S(1)} %get-tuple-element.123.refs_0_.refs_1_.refs_6_), channel_id=1, source_target_pairs={{0,4},{4,0},{8,12},{12,8},{16,20},{20,16},{24,28},{28,24},{1,5},{5... | collective-permute-start | bytes 4718600 | tf_op jit(solution)/shard_map/ppermute | solution.py:483
  122.1 2.2 copy-start.8
  127.3 55.8 %all-to-all-start = ((bf16[4,4,4,256,128]{4,3,2,1,0:T(8,128)(2,1)}), bf16[4,4,4,256,128]{4,3,2,1,0:T(8,128)(2,1)}, u32[]{:S(2)}, u32[]{:S(2)}) async-start(bf16[4,4,4,256,128]{4,3,2,1,0:T(8,128)(2,1)} %bitcast.15), calls=%async_computation | async-start | bytes 8388608 | tf_op jit(solution)/shard_map/all_to_all | solution.py:542
  147.2 44.5 %collective-permute-start.27 = (bf16[128,48,128]{2,1,0:T(8,128)(2,1)}, bf16[128,48,128]{2,1,0:T(8,128)(2,1)}, u32[]{:S(2)}, u32[]{:S(2)}) collective-permute-start(bf16[128,48,128]{2,1,0:T(8,128)(2,1)} %get-tuple-element.124.refs_0_.refs_1_.refs_6_), channel_id=1, source_target_pairs={{0,4},{4,0},{8,12},{12,8},{16,20},{20,16},{24,28},{28,24},{1,5},{5... | collective-permute-start | bytes 4718600 | tf_op jit(solution)/shard_map/ppermute | solution.py:483
  152.9 68.3 %collective-permute-start.29 = (bf16[128,48,128]{2,1,0:T(8,128)(2,1)}, bf16[128,48,128]{2,1,0:T(8,128)(2,1)}, u32[]{:S(2)}, u32[]{:S(2)}) collective-permute-start(bf16[128,48,128]{2,1,0:T(8,128)(2,1)} %collective-permute-done.18.refs_0_.refs_6_), channel_id=1, source_target_pairs={{8,16},{12,20},{16,24},{20,28},{9,17},{13,21},{17,25},{21,29},{10,... | collective-permute-start | bytes 4718600 | tf_op jit(solution)/shard_map/ppermute | solution.py:480
  178.8 52.8 %collective-permute-start.30 = (bf16[128,48,128]{2,1,0:T(8,128)(2,1)}, bf16[128,48,128]{2,1,0:T(8,128)(2,1)}, u32[]{:S(2)}, u32[]{:S(2)}) collective-permute-start(bf16[128,48,128]{2,1,0:T(8,128)(2,1)} %collective-permute-done.19.refs_1_.refs_8_), channel_id=1, source_target_pairs={{8,0},{12,4},{16,8},{20,12},{9,1},{13,5},{17,9},{21,13},{10,2},{14... | collective-permute-start | bytes 4718600 | tf_op jit(solution)/shard_map/ppermute | solution.py:480
  183.2 8.7 %collective-permute-start.22 = (bf16[4,4,4,256,128]{4,3,2,1,0:T(8,128)(2,1)}, bf16[4,4,4,256,128]{4,3,2,1,0:T(8,128)(2,1)S(1)}, u32[]{:S(2)}, u32[]{:S(2)}) collective-permute-start(bf16[4,4,4,256,128]{4,3,2,1,0:T(8,128)(2,1)} %all-to-all-done.refs_0_), channel_id=1, source_target_pairs={{0,4},{4,0},{8,12},{12,8},{16,20},{20,16},{24,28},{28,24},{1,5},{5... | collective-permute-start | bytes 12582920 | tf_op jit(solution)/shard_map/ppermute | solution.py:483
  191.2 19.8 %copy-start = (bf16[4,256,16,128]{3,2,1,0:T(8,128)(2,1)}, bf16[4,256,16,128]{3,2,1,0:T(8,128)(2,1)S(1)}, u32[]{:S(2)}) copy-start(bf16[4,256,16,128]{3,2,1,0:T(8,128)(2,1)S(1)} %get-tuple-element.126.refs_0_.refs_4_) | copy-start | bytes 12582916
  191.2 45.2 %collective-permute-start.25 = (bf16[128,48,128]{2,1,0:T(8,128)(2,1)}, bf16[128,48,128]{2,1,0:T(8,128)(2,1)}, u32[]{:S(2)}, u32[]{:S(2)}) collective-permute-start(bf16[128,48,128]{2,1,0:T(8,128)(2,1)} %collective-permute-done.18.refs_0_.refs_6_), channel_id=1, source_target_pairs={{0,4},{4,0},{8,12},{12,8},{16,20},{20,16},{24,28},{28,24},{1,5},{5... | collective-permute-start | bytes 4718600 | tf_op jit(solution)/shard_map/ppermute | solution.py:483
  191.8 45.9 %collective-permute-start.26 = (bf16[128,48,128]{2,1,0:T(8,128)(2,1)}, bf16[128,48,128]{2,1,0:T(8,128)(2,1)}, u32[]{:S(2)}, u32[]{:S(2)}) collective-permute-start(bf16[128,48,128]{2,1,0:T(8,128)(2,1)} %collective-permute-done.19.refs_1_.refs_8_), channel_id=1, source_target_pairs={{0,4},{4,0},{8,12},{12,8},{16,20},{20,16},{24,28},{28,24},{1,5},{5... | collective-permute-start | bytes 4718600 | tf_op jit(solution)/shard_map/ppermute | solution.py:483
  191.9 2.5 copy-start.14
  191.9 46.1 %collective-permute-start.23 = (bf16[128,48,128]{2,1,0:T(8,128)(2,1)}, bf16[128,48,128]{2,1,0:T(8,128)(2,1)}, u32[]{:S(2)}, u32[]{:S(2)}) collective-permute-start(bf16[128,48,128]{2,1,0:T(8,128)(2,1)} %collective-permute-done.20.refs_2_.refs_6_), channel_id=1, source_target_pairs={{8,16},{12,20},{16,24},{20,28},{9,17},{13,21},{17,25},{21,29},{10,... | collective-permute-start | bytes 4718600 | tf_op jit(solution)/shard_map/ppermute | solution.py:480
  202.3 2.0 copy-start.1
  205.9 7.2 %copy-start.2 = (bf16[128,48,128]{2,1,0:T(8,128)(2,1)}, bf16[128,48,128]{2,1,0:T(8,128)(2,1)S(1)}, u32[]{:S(2)}) copy-start(bf16[128,48,128]{2,1,0:T(8,128)(2,1)S(1)} %get-tuple-element.134.refs_3_) | copy-start | bytes 4718596
  210.9 11.6 %copy-start.5 = (bf16[128,48,128]{2,1,0:T(8,128)(2,1)}, bf16[128,48,128]{2,1,0:T(8,128)(2,1)S(1)}, u32[]{:S(2)}) copy-start(bf16[128,48,128]{2,1,0:T(8,128)(2,1)S(1)} %get-tuple-element.132.refs_3_) | copy-start | bytes 4718596
  221.2 43.2 %collective-permute-start.24 = (bf16[128,48,128]{2,1,0:T(8,128)(2,1)}, bf16[128,48,128]{2,1,0:T(8,128)(2,1)}, u32[]{:S(2)}, u32[]{:S(2)}) collective-permute-start(bf16[128,48,128]{2,1,0:T(8,128)(2,1)} %collective-permute-done.21.refs_3_.refs_8_), channel_id=1, source_target_pairs={{8,0},{12,4},{16,8},{20,12},{9,1},{13,5},{17,9},{21,13},{10,2},{14... | collective-permute-start | bytes 4718600 | tf_op jit(solution)/shard_map/ppermute | solution.py:480
  231.6 37.1 %collective-permute-start.36 = (bf16[128,48,128]{2,1,0:T(8,128)(2,1)}, bf16[128,48,128]{2,1,0:T(8,128)(2,1)}, u32[]{:S(2)}, u32[]{:S(2)}) collective-permute-start(bf16[128,48,128]{2,1,0:T(8,128)(2,1)} %collective-permute-done.20.refs_2_.refs_6_), channel_id=1, source_target_pairs={{0,4},{4,0},{8,12},{12,8},{16,20},{20,16},{24,28},{28,24},{1,5},{5... | collective-permute-start | bytes 4718600 | tf_op jit(solution)/shard_map/ppermute | solution.py:483
  236.4 61.7 %collective-permute-start.32 = (bf16[128,48,128]{2,1,0:T(8,128)(2,1)}, bf16[128,48,128]{2,1,0:T(8,128)(2,1)}, u32[]{:S(2)}, u32[]{:S(2)}) collective-permute-start(bf16[128,48,128]{2,1,0:T(8,128)(2,1)} %get-tuple-element.143.refs_6_), channel_id=1, source_target_pairs={{16,24},{20,28},{8,0},{12,4},{17,25},{21,29},{9,1},{13,5},{18,26},... | collective-permute-start | bytes 4718600 | tf_op jit(solution)/shard_map/ppermute | solution.py:531
  237.7 60.4 %collective-permute-start.37 = (bf16[128,48,128]{2,1,0:T(8,128)(2,1)}, bf16[128,48,128]{2,1,0:T(8,128)(2,1)}, u32[]{:S(2)}, u32[]{:S(2)}) collective-permute-start(bf16[128,48,128]{2,1,0:T(8,128)(2,1)} %collective-permute-done.21.refs_3_.refs_8_), channel_id=1, source_target_pairs={{0,4},{4,0},{8,12},{12,8},{16,20},{20,16},{24,28},{28,24},{1,5},{5... | collective-permute-start | bytes 4718600 | tf_op jit(solution)/shard_map/ppermute | solution.py:483
  237.9 70.6 %collective-permute-start.35 = (bf16[128,48,128]{2,1,0:T(8,128)(2,1)}, bf16[128,48,128]{2,1,0:T(8,128)(2,1)}, u32[]{:S(2)}, u32[]{:S(2)}) collective-permute-start(bf16[128,48,128]{2,1,0:T(8,128)(2,1)} %get-tuple-element.143.refs_6_), channel_id=1, source_target_pairs={{0,4},{4,0},{8,12},{12,8},{16,20},{20,16},{24,28},{28,24},{1,5},{5... | collective-permute-start | bytes 4718600 | tf_op jit(solution)/shard_map/ppermute | solution.py:483
  238.4 1.4 copy-start.3
  268.6 48.4 %collective-permute-start.34 = (bf16[128,48,128]{2,1,0:T(8,128)(2,1)}, bf16[128,48,128]{2,1,0:T(8,128)(2,1)}, u32[]{:S(2)}, u32[]{:S(2)}) collective-permute-start(bf16[128,48,128]{2,1,0:T(8,128)(2,1)} %get-tuple-element.142.refs_6_), channel_id=1, source_target_pairs={{0,4},{4,0},{8,12},{12,8},{16,20},{20,16},{24,28},{28,24},{1,5},{5... | collective-permute-start | bytes 4718600 | tf_op jit(solution)/shard_map/ppermute | solution.py:483
  268.8 66.9 %collective-permute-start.31 = (bf16[128,48,128]{2,1,0:T(8,128)(2,1)}, bf16[128,48,128]{2,1,0:T(8,128)(2,1)S(1)}, u32[]{:S(2)}, u32[]{:S(2)}) collective-permute-start(bf16[128,48,128]{2,1,0:T(8,128)(2,1)} %get-tuple-element.142.refs_6_), channel_id=1, source_target_pairs={{16,24},{20,28},{8,0},{12,4},{17,25},{21,29},{9,1},{13,5},{18,26},... | collective-permute-start | bytes 4718600 | tf_op jit(solution)/shard_map/ppermute | solution.py:531
  298.1 27.8 %collective-permute-start.33 = (bf16[128,48,128]{2,1,0:T(8,128)(2,1)}, bf16[128,48,128]{2,1,0:T(8,128)(2,1)S(1)}, u32[]{:S(2)}, u32[]{:S(2)}) collective-permute-start(bf16[128,48,128]{2,1,0:T(8,128)(2,1)} %collective-permute-done.32.refs_9_.refs_6_), channel_id=1, source_target_pairs={{0,4},{4,0},{8,12},{12,8},{16,20},{20,16},{24,28},{28,24},{1,5},{5... | collective-permute-start | bytes 4718600 | tf_op jit(solution)/shard_map/ppermute | solution.py:483
  298.1 1.4 copy-start.6
  299.5 9.1 %copy-start.4 = (bf16[128,48,128]{2,1,0:T(8,128)(2,1)S(1)}, bf16[128,48,128]{2,1,0:T(8,128)(2,1)}, u32[]{:S(2)}) copy-start(bf16[128,48,128]{2,1,0:T(8,128)(2,1)} %copy-done.2) | copy-start | bytes 4718596
  308.6 8.4 %copy-start.7 = (bf16[128,48,128]{2,1,0:T(8,128)(2,1)S(1)}, bf16[128,48,128]{2,1,0:T(8,128)(2,1)}, u32[]{:S(2)}) copy-start(bf16[128,48,128]{2,1,0:T(8,128)(2,1)} %copy-done.5) | copy-start | bytes 4718596
  325.9 1.2 copy-start.12
  336.2 3.6 %collective-permute-start.38 = (bf16[128,48,128]{2,1,0:T(8,128)(2,1)S(1)}, bf16[128,48,128]{2,1,0:T(8,128)(2,1)S(1)}, u32[]{:S(2)}, u32[]{:S(2)}) collective-permute-start(bf16[128,48,128]{2,1,0:T(8,128)(2,1)S(1)} %get-tuple-element.153.refs_6_), channel_id=1, source_target_pairs={{0,4},{4,0},{8,12},{12,8},{16,20},{20,16},{24,28},{28,24},{1,5},{5... | collective-permute-start | bytes 4718600 | tf_op jit(solution)/shard_map/ppermute | solution.py:483
  339.9 1.2 copy-start.13
Sparse Core Ops, SparseCore 0:
  34.3 82.0 all-gather.2
